TPU v7x, 32 devices: a whole 2x2x4 slice. The times are simulated.
32 devices in a mesh: ctx: 8 (over z, y), fsdp: 4 (over x, core).
Axes of the slice: x: 2, y: 2, z: 4, core: 2. Of those that a mesh axis runs over, the one named last changes fastest.
Arguments:
- tokens: bfloat16 [4, 2048, 1024], P('fsdp', 'ctx'), may hold values from -6 to 6
- encoded: bfloat16 [4, 512, 1024], P('fsdp', 'ctx'), may hold values from -6 to 6
- grad_out: bfloat16 [4, 2048, 1024], P('fsdp', 'ctx'), may hold values from -6 to 6
- doc_lengths: int32 [4, 8], P('fsdp'), may hold values from 1 to 1024, 2048 in all within a row
- src_lengths: int32 [4, 8], P('fsdp'), may hold values from 1 to 256, 512 in all within a row
- norm_gain: float32 [3, 1024], replicated, may hold values from 0.5 to 1.5
- norm_bias: float32 [3, 1024], replicated, may hold values from -0.6 to 0.6
- w_qkv: bfloat16 [1024, 3072], P('fsdp'), may hold values from -0.1875 to 0.1875
- self_bias: float32 [3, 1024], replicated, may hold values from -0.6 to 0.6
- w_self_out: bfloat16 [1024, 1024], P('fsdp'), may hold values from -0.75 to 0.75
- w_cross_q: bfloat16 [1024, 1024], P('fsdp'), may hold values from -0.1875 to 0.1875
- w_cross_kv: bfloat16 [1024, 2048], P('fsdp'), may hold values from -0.1875 to 0.1875
- cross_bias: float32 [3, 1024], replicated, may hold values from -0.6 to 0.6
- w_cross_out: bfloat16 [1024, 1024], P('fsdp'), may hold values from -0.75 to 0.75
- w_up: bfloat16 [1024, 8192], P('fsdp'), may hold values from -0.1875 to 0.1875
- up_bias: float32 [8192], replicated, may hold values from -0.6 to 0.6
- w_down: bfloat16 [8192, 1024], P('fsdp'), may hold values from -0.0625 to 0.0625
- down_bias: float32 [1024], replicated, may hold values from -1.2 to 1.2
Outputs:
- layer_out: bfloat16 [4, 2048, 1024], P('fsdp', 'ctx')
- grad_tokens: float32 [4, 2048, 1024], P('fsdp', 'ctx')
- grad_encoded: float32 [4, 512, 1024], P('fsdp', 'ctx')
- grad_norm_gain: float32 [3, 1024], replicated
- grad_norm_bias: float32 [3, 1024], replicated
- grad_w_qkv: float32 [1024, 3072], P('fsdp', 'ctx')
- grad_self_bias: float32 [3, 1024], replicated
- grad_w_self_out: float32 [1024, 1024], P('fsdp', 'ctx')
- grad_w_cross_q: float32 [1024, 1024], P('fsdp', 'ctx')
- grad_w_cross_kv: float32 [1024, 2048], P('fsdp', 'ctx')
- grad_cross_bias: float32 [3, 1024], replicated
- grad_w_cross_out: float32 [1024, 1024], P('fsdp', 'ctx')
- grad_w_up: float32 [1024, 8192], P('fsdp', 'ctx')
- grad_up_bias: float32 [8192], replicated
- grad_w_down: float32 [8192, 1024], P('fsdp', 'ctx')
- grad_down_bias: float32 [1024], replicated
Inputs may be any that keep to these rules, and one draw needn't show every extreme that they name: `doc_lengths`: each row of target document lengths sums to 2048, and its longest is exactly 1024. `src_lengths`: each row of source span lengths sums to 512, and its longest is exactly 256.
All inputs are finite; a program needn't handle non-finite values.
Results may differ from a plain program's by a relative error of at most 0.024.
Values may be sent and summed in bfloat16 or wider, within the bound.
No kernel may reach another device: no remote copies, remote signals or barrier semaphores. Data moves between devices by JAX's collectives and lax.ppermute only.
A program may use at most 512 MiB of HBM per device.

v0:
```python
import math

import jax
import jax.numpy as jnp
from jax import lax
from jax.sharding import PartitionSpec as P

HEADS = 16
HEAD_DIM = 64
KBLOCK = 512


EPS = 1e-05
NEG = -1e30
GELU_C = 0.7978845608028654
GELU_A = 0.044715
CONTRACT_ROWS = (((0,), (0,)), ((), ()))
CONTRACT_COLS = (((1,), (1,)), ((), ()))


def shortened(shard):
    return jax.tree.map(lambda a: a.astype(jnp.bfloat16) if a.dtype == jnp.float32 else a, shard)


def gelu_value(pre):
    return 0.5 * pre * (1.0 + jnp.tanh(GELU_C * (pre + GELU_A * pre * pre * pre)))


def gelu_slope(pre):
    tangent = jnp.tanh(GELU_C * (pre + GELU_A * pre * pre * pre))
    return 0.5 * (1.0 + tangent) + 0.5 * pre * (1.0 - tangent * tangent) * GELU_C * (
        1.0 + 3.0 * GELU_A * pre * pre
    )


def stream_position(rows, tok_dev, ctx_count):
    half = tok_dev // 2
    device = rows // tok_dev
    within = rows % tok_dev
    early = device * half + within
    late = (2 * ctx_count - 1 - device) * half + (within - half)
    return jnp.where(within < half, early, late)


def layer_norm(inputs, gain_row, shift_row):
    center = inputs - jnp.mean(inputs, axis=1, keepdims=True)
    inverse = lax.rsqrt(jnp.mean(center * center, axis=1, keepdims=True) + EPS)
    normed = center * inverse
    return (normed * gain_row + shift_row, normed, inverse)


def norm_back(upstream, normed, inverse, gain_row):
    scaled = upstream * gain_row
    mean_plain = jnp.mean(scaled, axis=1, keepdims=True)
    mean_normed = jnp.mean(scaled * normed, axis=1, keepdims=True)
    return (
        inverse * (scaled - mean_plain - normed * mean_normed),
        jnp.sum(upstream * normed, axis=0),
        jnp.sum(upstream, axis=0),
    )


def outer_rows(left, right):
    return lax.dot_general(left, right, CONTRACT_ROWS, preferred_element_type=jnp.float32)


def times_transpose(left, right):
    return lax.dot_general(left, right, CONTRACT_COLS, preferred_element_type=jnp.float32)


def plain_dot(left, right):
    return jnp.dot(left, right, preferred_element_type=jnp.float32)


def doc_index(doc_starts, positions):
    counted = jnp.sum((doc_starts[None, :] <= positions[:, None]).astype(jnp.int32), axis=1)
    return counted - 1


def pick_doc(lookup, doc_ids):
    onehot = doc_ids[:, None] == jnp.arange(lookup.shape[0], dtype=jnp.int32)[None, :]
    return jnp.sum(jnp.where(onehot, lookup[None, :], 0), axis=1)


def split_heads(matrix):
    return matrix.reshape(matrix.shape[0], HEADS, matrix.shape[1] // HEADS)


def split_pair(kv_piece):
    half_width = kv_piece.shape[1] // 2
    return (split_heads(kv_piece[:, :half_width]), split_heads(kv_piece[:, half_width:]))


def key_block(kv_whole, block_start):
    return split_pair(lax.dynamic_slice_in_dim(kv_whole, block_start, KBLOCK, 0))


def block_starts(kv_whole):
    return jnp.arange(kv_whole.shape[0] // KBLOCK, dtype=jnp.int32) * KBLOCK


def score_block(queries, key_heads):
    return jnp.einsum("qhd,khd->hqk", queries, key_heads, preferred_element_type=jnp.float32)


def attend(queries, kv_whole, allowed_fn):
    shape_stat = (queries.shape[1], queries.shape[0])

    def stat_step(state_pair, block_start):
        allowed = allowed_fn(block_start)

        def stat_compute_block(running):
            running_top, running_sum = running
            key_heads, value_heads = key_block(kv_whole, block_start)
            masked = jnp.where(allowed[None], score_block(queries, key_heads), NEG)
            new_top = jnp.maximum(running_top, jnp.max(masked, axis=2))
            exp_terms = jnp.where(allowed[None], jnp.exp(masked - new_top[:, :, None]), 0.0)
            return (
                new_top,
                running_sum * jnp.exp(running_top - new_top) + jnp.sum(exp_terms, axis=2),
            )

        return (
            lax.cond(jnp.any(allowed), stat_compute_block, lambda running: running, state_pair),
            None,
        )

    initial = (jnp.full(shape_stat, NEG, jnp.float32), jnp.zeros(shape_stat, jnp.float32))
    (final_top, final_sum), _ = lax.scan(stat_step, initial, block_starts(kv_whole))
    logsum = final_top + jnp.log(final_sum)

    def value_step(running, block_start):
        allowed = allowed_fn(block_start)

        def value_compute_block(partial_value):
            key_heads, value_heads = key_block(kv_whole, block_start)
            raw_scores = score_block(queries, key_heads)
            prob_low = jnp.where(
                allowed[None], jnp.exp(raw_scores - logsum[:, :, None]), 0.0
            ).astype(jnp.bfloat16)
            return partial_value + jnp.einsum(
                "hqk,khd->qhd", prob_low, value_heads, preferred_element_type=jnp.float32
            )

        return (
            lax.cond(
                jnp.any(allowed), value_compute_block, lambda partial_value: partial_value, running
            ),
            None,
        )

    attended, _ = lax.scan(
        value_step, jnp.zeros(queries.shape, jnp.float32), block_starts(kv_whole)
    )
    return (attended, logsum)


def score_grads(queries, key_heads, value_heads, grad_heads, logsum, row_delta, allowed):
    raw_scores = score_block(queries, key_heads)
    probs_full = jnp.where(allowed[None], jnp.exp(raw_scores - logsum[:, :, None]), 0.0)
    grad_probs = jnp.einsum(
        "qhd,khd->hqk", grad_heads, value_heads, preferred_element_type=jnp.float32
    )
    grad_scores = (probs_full * (grad_probs - row_delta[:, :, None])).astype(jnp.bfloat16)
    return (probs_full, grad_scores)


def key_terms(queries, key_heads, value_heads, grad_heads, logsum, row_delta, allowed):
    probs_full, grad_scores = score_grads(
        queries, key_heads, value_heads, grad_heads, logsum, row_delta, allowed
    )
    grad_keys = jnp.einsum("hqk,qhd->khd", grad_scores, queries, preferred_element_type=jnp.float32)
    grad_values = jnp.einsum(
        "hqk,qhd->khd",
        probs_full.astype(jnp.bfloat16),
        grad_heads,
        preferred_element_type=jnp.float32,
    )
    key_count = key_heads.shape[0]
    return jnp.concatenate(
        [grad_keys.reshape(key_count, -1), grad_values.reshape(key_count, -1)], axis=1
    )


def row_deltas(grad_heads, attended):
    return jnp.einsum("qhd,qhd->hq", grad_heads.astype(jnp.float32), attended)


def query_back(queries, kv_whole, allowed_fn, logsum, row_delta, grad_heads):

    def query_grad_step(partial_value, block_start):
        allowed = allowed_fn(block_start)

        def query_compute_block(running):
            key_heads, value_heads = key_block(kv_whole, block_start)
            probs_full, grad_scores = score_grads(
                queries, key_heads, value_heads, grad_heads, logsum, row_delta, allowed
            )
            return running + jnp.einsum(
                "hqk,khd->qhd", grad_scores, key_heads, preferred_element_type=jnp.float32
            )

        return (
            lax.cond(jnp.any(allowed), query_compute_block, lambda running: running, partial_value),
            None,
        )

    grad_query, _ = lax.scan(
        query_grad_step, jnp.zeros(queries.shape, jnp.float32), block_starts(kv_whole)
    )
    return grad_query


def attend_back(queries, kv_whole, allowed_fn, attended, logsum, grad_heads):
    row_delta = row_deltas(grad_heads, attended)

    def attend_grad_step(grad_query, block_start):
        allowed = allowed_fn(block_start)

        def attend_compute_block(partial_value):
            key_heads, value_heads = key_block(kv_whole, block_start)
            probs_full, grad_scores = score_grads(
                queries, key_heads, value_heads, grad_heads, logsum, row_delta, allowed
            )
            partial_value = partial_value + jnp.einsum(
                "hqk,khd->qhd", grad_scores, key_heads, preferred_element_type=jnp.float32
            )
            grad_keys = jnp.einsum(
                "hqk,qhd->khd", grad_scores, queries, preferred_element_type=jnp.float32
            )
            grad_values = jnp.einsum(
                "hqk,qhd->khd",
                probs_full.astype(jnp.bfloat16),
                grad_heads,
                preferred_element_type=jnp.float32,
            )
            return (
                partial_value,
                jnp.concatenate(
                    [grad_keys.reshape(KBLOCK, -1), grad_values.reshape(KBLOCK, -1)], axis=1
                ),
            )

        def attend_skip_block(partial_value):
            return (partial_value, jnp.zeros((KBLOCK, kv_whole.shape[1]), jnp.float32))

        return lax.cond(jnp.any(allowed), attend_compute_block, attend_skip_block, grad_query)

    grad_query, kv_terms = lax.scan(
        attend_grad_step, jnp.zeros(queries.shape, jnp.float32), block_starts(kv_whole)
    )
    return (grad_query, kv_terms.reshape(kv_whole.shape[0], kv_whole.shape[1]))


def owners_end(grads):
    columns = jax.tree.map(
        lambda part: part.astype(jnp.float32),
        lax.psum_scatter(shortened(grads), "ctx", scatter_dimension=1, tiled=True),
    )
    return jax.tree.map(
        lambda part: part.astype(jnp.float32),
        lax.psum_scatter(shortened(columns), "fsdp", scatter_dimension=0, tiled=True),
    )


def per_device(
    tokens,
    encoded,
    grad_out,
    doc_lengths,
    src_lengths,
    norm_gain,
    norm_bias,
    w_qkv,
    self_bias,
    w_self_out,
    w_cross_q,
    w_cross_kv,
    cross_bias,
    w_cross_out,
    w_up,
    up_bias,
    w_down,
    down_bias,
):
    q_scale = 1.0 / math.sqrt(HEAD_DIM)
    tok_rows = tokens.shape[1]
    features = tokens.shape[2]
    ctx_count = lax.axis_size("ctx")
    ctx_index = lax.axis_index("ctx")
    own_rows = ctx_index * tok_rows + jnp.arange(tok_rows, dtype=jnp.int32)
    tok_pos = stream_position(own_rows, tok_rows, ctx_count)
    lengths_row = doc_lengths[0]
    doc_starts = jnp.cumsum(lengths_row) - lengths_row
    tok_doc = doc_index(doc_starts, tok_pos)
    src_row = src_lengths[0]
    src_ends = jnp.cumsum(src_row)
    src_starts = src_ends - src_row
    span_low = pick_doc(src_starts, tok_doc)
    span_high = pick_doc(src_ends, tok_doc)

    def self_mask(key_rows):
        key_pos = stream_position(key_rows, tok_rows, ctx_count)
        key_doc = doc_index(doc_starts, key_pos)
        return (key_pos[None, :] <= tok_pos[:, None]) & (key_doc[None, :] == tok_doc[:, None])

    def self_allowed(block_start):
        return self_mask(block_start + jnp.arange(KBLOCK, dtype=jnp.int32))

    def cross_allowed(block_start):
        key_pos = block_start + jnp.arange(KBLOCK, dtype=jnp.int32)
        return (key_pos[None, :] >= span_low[:, None]) & (key_pos[None, :] < span_high[:, None])

    def gather_self():
        return (
            lax.all_gather(w_qkv, "fsdp", axis=0, tiled=True),
            lax.all_gather(w_self_out, "fsdp", axis=0, tiled=True),
        )

    def gather_cross():
        return (
            lax.all_gather(w_cross_q, "fsdp", axis=0, tiled=True),
            lax.all_gather(w_cross_kv, "fsdp", axis=0, tiled=True),
            lax.all_gather(w_cross_out, "fsdp", axis=0, tiled=True),
        )

    def gather_mlp():
        return (
            lax.all_gather(w_up, "fsdp", axis=0, tiled=True),
            lax.all_gather(w_down, "fsdp", axis=0, tiled=True),
        )

    tok_f32 = tokens[0].astype(jnp.float32)
    enc_low = encoded[0]
    ln_one, normed_one, inverse_one = layer_norm(tok_f32, norm_gain[0], norm_bias[0])
    act_one = ln_one.astype(jnp.bfloat16)
    full_qkv, full_self_out = gather_self()
    projected = plain_dot(act_one, full_qkv)
    q_self = ((projected[:, :features] + self_bias[0]) * q_scale).astype(jnp.bfloat16)
    kv_self = jnp.concatenate(
        [projected[:, features : 2 * features], projected[:, 2 * features :] + self_bias[1]], axis=1
    ).astype(jnp.bfloat16)
    kv_self_all = lax.all_gather(kv_self, "ctx", axis=0, tiled=True)
    self_heads = split_heads(q_self)
    att_self, lse_self = attend(self_heads, kv_self_all, self_allowed)
    att_self_low = att_self.reshape(tok_rows, features).astype(jnp.bfloat16)
    hidden_one = tok_f32 + plain_dot(att_self_low, full_self_out) + self_bias[2]
    ln_two, normed_two, inverse_two = layer_norm(hidden_one, norm_gain[1], norm_bias[1])
    act_two = ln_two.astype(jnp.bfloat16)
    full_cross_q, full_cross_kv, full_cross_out = gather_cross()
    q_cross = ((plain_dot(act_two, full_cross_q) + cross_bias[0]) * q_scale).astype(jnp.bfloat16)
    src_proj = plain_dot(enc_low, full_cross_kv)
    kv_cross = jnp.concatenate(
        [src_proj[:, :features], src_proj[:, features:] + cross_bias[1]], axis=1
    ).astype(jnp.bfloat16)
    kv_cross_all = lax.all_gather(kv_cross, "ctx", axis=0, tiled=True)
    cross_heads = split_heads(q_cross)
    att_cross, lse_cross = attend(cross_heads, kv_cross_all, cross_allowed)
    att_cross_low = att_cross.reshape(tok_rows, features).astype(jnp.bfloat16)
    hidden_two = hidden_one + plain_dot(att_cross_low, full_cross_out) + cross_bias[2]
    ln_three, normed_three, inverse_three = layer_norm(hidden_two, norm_gain[2], norm_bias[2])
    act_three = ln_three.astype(jnp.bfloat16)
    full_up, full_down = gather_mlp()
    pre_act = plain_dot(act_three, full_up) + up_bias
    gelu_low = gelu_value(pre_act).astype(jnp.bfloat16)
    layer_out = (hidden_two + plain_dot(gelu_low, full_down) + down_bias).astype(jnp.bfloat16)
    upstream = grad_out[0].astype(jnp.float32)
    down_grad_low = grad_out[0]
    full_up, full_down = gather_mlp()
    grad_w_down = outer_rows(gelu_low, down_grad_low)
    grad_down_bias = jnp.sum(upstream, axis=0)
    gelu_grad = times_transpose(down_grad_low, full_down)
    pre_grad_low = (gelu_grad * gelu_slope(pre_act)).astype(jnp.bfloat16)
    grad_w_up = outer_rows(act_three, pre_grad_low)
    grad_up_bias = jnp.sum(pre_grad_low.astype(jnp.float32), axis=0)
    norm_in_three, gain_grad_three, shift_grad_three = norm_back(
        times_transpose(pre_grad_low, full_up), normed_three, inverse_three, norm_gain[2]
    )
    grad_two = upstream + norm_in_three
    full_cross_q, full_cross_kv, full_cross_out = gather_cross()
    cross_grad_low = grad_two.astype(jnp.bfloat16)
    grad_w_cross_out = outer_rows(att_cross_low, cross_grad_low)
    cross_out_bias_grad = jnp.sum(cross_grad_low.astype(jnp.float32), axis=0)
    cross_att_grad = split_heads(
        times_transpose(cross_grad_low, full_cross_out).astype(jnp.bfloat16)
    )
    cross_q_grad, cross_kv_terms = attend_back(
        cross_heads, kv_cross_all, cross_allowed, att_cross, lse_cross, cross_att_grad
    )
    cross_kv_grad = lax.psum_scatter(
        cross_kv_terms.astype(jnp.bfloat16), "ctx", scatter_dimension=0, tiled=True
    )
    cross_q_low = (cross_q_grad.reshape(tok_rows, features) * q_scale).astype(jnp.bfloat16)
    grad_w_cross_q = outer_rows(act_two, cross_q_low)
    cross_q_bias_grad = jnp.sum(cross_q_low.astype(jnp.float32), axis=0)
    grad_w_cross_kv = outer_rows(enc_low, cross_kv_grad)
    cross_v_bias_grad = jnp.sum(cross_kv_grad[:, features:].astype(jnp.float32), axis=0)
    grad_encoded = times_transpose(cross_kv_grad, full_cross_kv)
    norm_in_two, gain_grad_two, shift_grad_two = norm_back(
        times_transpose(cross_q_low, full_cross_q), normed_two, inverse_two, norm_gain[1]
    )
    grad_one = grad_two + norm_in_two
    full_qkv, full_self_out = gather_self()
    self_grad_low = grad_one.astype(jnp.bfloat16)
    grad_w_self_out = outer_rows(att_self_low, self_grad_low)
    self_out_bias_grad = jnp.sum(self_grad_low.astype(jnp.float32), axis=0)
    self_att_flat = times_transpose(self_grad_low, full_self_out).astype(jnp.bfloat16)
    self_att_grad = split_heads(self_att_flat)
    self_delta = row_deltas(self_att_grad, att_self)
    self_q_grad = query_back(
        self_heads, kv_self_all, self_allowed, lse_self, self_delta, self_att_grad
    )

    def one_piece(sub_start):
        key_rows = sub_start + jnp.arange(tok_rows, dtype=jnp.int32)
        allowed = self_mask(key_rows)

        def one_compute_block(piece_start):
            key_heads, value_heads = split_pair(
                lax.dynamic_slice_in_dim(kv_self_all, piece_start, tok_rows, 0)
            )
            return key_terms(
                self_heads, key_heads, value_heads, self_att_grad, lse_self, self_delta, allowed
            )

        def one_skip_block(piece_start):
            return jnp.zeros((tok_rows, 2 * features), jnp.float32)

        return lax.cond(jnp.any(allowed), one_compute_block, one_skip_block, sub_start)

    piece_starts = (
        jnp.arange(tok_rows * lax.axis_size("ctx") // tok_rows, dtype=jnp.int32) * tok_rows
    )
    self_kv_grad = lax.psum_scatter(
        lax.map(one_piece, piece_starts)
        .reshape(tok_rows * lax.axis_size("ctx"), 2 * features)
        .astype(jnp.bfloat16),
        "ctx",
        scatter_dimension=0,
        tiled=True,
    )
    self_q_low = (self_q_grad.reshape(tok_rows, features) * q_scale).astype(jnp.bfloat16)
    proj_grad_low = jnp.concatenate([self_q_low, self_kv_grad], axis=1)
    grad_w_qkv = outer_rows(act_one, proj_grad_low)
    self_q_bias_grad = jnp.sum(self_q_low.astype(jnp.float32), axis=0)
    self_v_bias_grad = jnp.sum(self_kv_grad[:, features:].astype(jnp.float32), axis=0)
    norm_in_one, gain_grad_one, shift_grad_one = norm_back(
        times_transpose(proj_grad_low, full_qkv), normed_one, inverse_one, norm_gain[0]
    )
    grad_tokens = grad_one + norm_in_one
    owned = owners_end(
        (
            grad_w_qkv,
            grad_w_self_out,
            grad_w_cross_q,
            grad_w_cross_kv,
            grad_w_cross_out,
            grad_w_up,
            grad_w_down,
        )
    )
    gain_grads = jnp.stack([gain_grad_one, gain_grad_two, gain_grad_three])
    shift_grads = jnp.stack([shift_grad_one, shift_grad_two, shift_grad_three])
    self_bias_grads = jnp.stack([self_q_bias_grad, self_v_bias_grad, self_out_bias_grad])
    cross_bias_grads = jnp.stack([cross_q_bias_grad, cross_v_bias_grad, cross_out_bias_grad])
    summed = lax.psum(
        (gain_grads, shift_grads, self_bias_grads, cross_bias_grads, grad_up_bias, grad_down_bias),
        ("ctx", "fsdp"),
    )
    return (
        layer_out[None],
        grad_tokens[None],
        grad_encoded[None],
        summed[0],
        summed[1],
        owned[0],
        summed[2],
        owned[1],
        owned[2],
        owned[3],
        summed[3],
        owned[4],
        owned[5],
        summed[4],
        owned[6],
        summed[5],
    )


def solution(mesh):
    placed = (
        P("fsdp", "ctx", None),
        P("fsdp", "ctx", None),
        P("fsdp", "ctx", None),
        P("fsdp", None),
        P("fsdp", None),
        P(),
        P(),
        P("fsdp", None),
        P(),
        P("fsdp", None),
        P("fsdp", None),
        P("fsdp", None),
        P(),
        P("fsdp", None),
        P("fsdp", None),
        P(),
        P("fsdp", None),
        P(),
    )
    return jax.shard_map(
        per_device,
        mesh=mesh,
        in_specs=placed,
        out_specs=(
            P("fsdp", "ctx", None),
            P("fsdp", "ctx", None),
            P("fsdp", "ctx", None),
            P(),
            P(),
            P("fsdp", "ctx"),
            P(),
            P("fsdp", "ctx"),
            P("fsdp", "ctx"),
            P("fsdp", "ctx"),
            P(),
            P("fsdp", "ctx"),
            P("fsdp", "ctx"),
            P(),
            P("fsdp", "ctx"),
            P(),
        ),
        check_vma=False,
    )
```

profile of v0, /device:TPU:2, one launch (start us, length us, event | category | flops | bytes accessed | tf_op | source)
XLA Modules:
  0.0 2244.4 jit_solution(1231170231104017694)
XLA Ops:
  15.6 40.5 %all-gather.10.cloned.1.call-done = bf16[1024,3072]{1,0:T(8,128)(2,1)} async-done(((bf16[256,3072]{1,0:T(8,128)(2,1)}), bf16[1024,3072]{1,0:T(8,128)(2,1)}) %all-gather.10.cloned.1.call-update) | async-done | bytes 6291472 | tf_op jit(solution)/shard_map/all_gather | solution.py:316
  56.1 4.9 fusion.121
  64.3 27.9 %all-gather.16.cloned.1.call-done = bf16[1024,2048]{1,0:T(8,128)(2,1)} async-done(((bf16[256,2048]{1,0:T(8,128)(2,1)}), bf16[1024,2048]{1,0:T(8,128)(2,1)}) %all-gather.16.cloned.1.call-update) | async-done | bytes 4194320 | tf_op jit(solution)/shard_map/all_gather | solution.py:323
  103.0 118.0 %all-gather.12.cloned.1.call-done = bf16[2048,2048]{1,0:T(8,128)(2,1)} async-done(((bf16[256,2048]{1,0:T(8,128)(2,1)}), bf16[2048,2048]{1,0:T(8,128)(2,1)}) %all-gather.12.cloned.1.call-update) | async-done | bytes 8388624 | tf_op jit(solution)/shard_map/all_gather | solution.py:343
  221.0 12.4 copy.113
  233.4 27.8 %while.82 = (s32[]{:T(128)}, f32[16,256]{1,0:T(8,128)S(1)}, f32[16,256]{1,0:T(8,128)S(1)}, s32[4]{0:T(128)}, s32[8]{0:T(128)S(1)}, /*index=5*/s32[256]{0:T(256)S...) while((s32[]{:T(128)}, f32[16,256]{1,0:T(8,128)S(1)}, ...), condition=%wide.region_11.12_spmd.clone, body=%wide.region_4.11_spmd.clone.sunk | while | flops 281584640 | bytes 21071140 | solution.py:129
  236.8 6.9 conditional.18
  247.2 6.9 conditional.18
  262.8 32.6 %while.83 = (s32[]{:T(128)}, f32[256,16,64]{0,2,1:T(8,128)}, s32[4]{0:T(128)}, s32[8]{0:T(128)S(1)}, s32[256]{0:T(256)S(1)}, /*index=5*/bf16[2048,2048]{0,1:T(8,...) while((s32[]{:T(128)}, f32[256,16,64]{0,2,1:T(8,128)}, ...), condition=%wide.region_17.18_spmd.clone, body=%wide.region_12.17_spmd.clone.sunk | while | flops 543982592 | bytes 9209109 | solution.py:152
  266.4 9.3 conditional.19
  271.2 4.5 fusion.20
  279.1 9.3 conditional.19
  284.0 4.5 fusion.20
  302.5 16.8 all-gather.18.cloned.1.call-done
  319.3 9.4 conditional.7
  329.9 12.2 conditional.8
  336.9 4.9 fusion.31
  345.8 102.6 %all-gather.24.cloned.1.call-done = bf16[1024,8192]{1,0:T(8,128)(2,1)} async-done(((bf16[256,8192]{1,0:T(8,128)(2,1)}), bf16[1024,8192]{1,0:T(8,128)(2,1)}) %all-gather.24.cloned.1.call-update) | async-done | bytes 16777232 | tf_op jit(solution)/shard_map/all_gather | solution.py:329
  448.3 12.9 convolution_add_fusion
  461.2 94.6 %all-gather.26.cloned.1.call-done = bf16[8192,1024]{1,0:T(8,128)(2,1)} async-done(((bf16[2048,1024]{1,0:T(8,128)(2,1)}), bf16[8192,1024]{1,0:T(8,128)(2,1)}) %all-gather.26.cloned.1.call-update) | async-done | bytes 16777232 | tf_op jit(solution)/shard_map/all_gather | solution.py:330
  555.9 16.1 convert_reduce_fusion.4
  571.9 13.4 multiply_reduce_fusion.1
  592.3 19.6 conditional.9
  592.3 4.0 copy.118
  626.9 74.7 %while.85 = (s32[]{:T(128)}, bf16[8,256,2048]{2,1,0:T(8,128)(2,1)}, s32[8]{0:T(128)S(1)}, s32[8]{0:T(128)S(1)}, s32[256]{0:T(256)S(1)}, /*index=5*/bf16[2048,204...) while((s32[]{:T(128)}, bf16[8,256,2048]{2,1,0:T(8,128)(2,1)}, ...), condition=%wide.region_49.50_spmd.clone, body=%wide.region_44.49_spmd.clone.sunk | while | flops 547639296 | bytes 42199372 | solution.py:435
  629.7 12.7 conditional.21
  638.2 4.1 fusion.53
  646.9 12.8 conditional.21
  655.5 4.2 fusion.53
  664.2 12.8 conditional.21
  672.8 4.2 fusion.53
  705.0 4.1 copy.149
  722.5 4.2 convert_bitcast_fusion
  727.2 48.3 %while.84 = (s32[]{:T(128)}, f32[256,16,64]{0,2,1:T(8,128)}, s32[4]{0:T(128)}, s32[8]{0:T(128)S(1)}, s32[256]{0:T(256)S(1)}, /*index=5*/bf16[2048,2048]{0,1:T(8,...) while((s32[]{:T(128)}, f32[256,16,64]{0,2,1:T(8,128)}, ...), condition=%wide.region_43.44_spmd.clone, body=%wide.region_38.43_spmd.clone.sunk | while | flops 816612352 | bytes 27575604 | solution.py:208
  730.7 17.1 conditional.20
  735.6 4.5 fusion.137
  740.1 7.7 fusion.42
  751.3 17.1 conditional.20
  756.2 4.5 fusion.137
  760.7 7.7 fusion.42
  777.1 137.8 %reduce-scatter.29.cloned.1.call-done = bf16[256,2048]{1,0:T(8,128)(2,1)} async-done(((bf16[2048,2048]{1,0:T(8,128)(2,1)}), bf16[256,2048]{1,0:T(8,128)(2,1)}) %reduce-scatter.29.cloned.1.call-update) | async-done | bytes 1048592 | tf_op jit(solution)/shard_map/reduce_scatter | solution.py:434
  915.0 5.9 convolution_convert_fusion.2
  920.8 8.8 copy.147
  929.7 10.7 convolution_convert_fusion
  941.4 11.5 convolution_convert_fusion.1
  952.9 20.8 copy.155
  973.8 11.9 reduce-scatter.53.cloned.1.call-done
  987.6 69.0 %reduce-scatter.55.cloned.1.call-done = bf16[128,1024]{1,0:T(8,128)(2,1)} async-done(((bf16[1024,1024]{1,0:T(8,128)(2,1)}), bf16[128,1024]{1,0:T(8,128)(2,1)}) %reduce-scatter.55.cloned.1.call-update) | async-done | bytes 262160
  1058.4 68.8 %reduce-scatter.57.cloned.1.call-done = bf16[128,1024]{1,0:T(8,128)(2,1)} async-done(((bf16[1024,1024]{1,0:T(8,128)(2,1)}), bf16[128,1024]{1,0:T(8,128)(2,1)}) %reduce-scatter.57.cloned.1.call-update) | async-done | bytes 262160
  1129.1 89.1 %reduce-scatter.37.cloned.1.call-done = bf16[1024,256]{0,1:T(8,128)(2,1)} async-done(((bf16[1024,2048]{0,1:T(8,128)(2,1)}), bf16[1024,256]{0,1:T(8,128)(2,1)}) %reduce-scatter.37.cloned.1.call-update) | async-done | bytes 524304 | tf_op jit(solution)/shard_map/reduce_scatter | solution.py:258
  1218.3 121.1 %reduce-scatter.51.cloned.1.call-done = bf16[384,1024]{1,0:T(8,128)(2,1)} async-done(((bf16[3072,1024]{1,0:T(8,128)(2,1)}), bf16[384,1024]{1,0:T(8,128)(2,1)}) %reduce-scatter.51.cloned.1.call-update) | async-done | bytes 786448
  1341.8 283.1 %reduce-scatter.43.cloned.1.call-done = bf16[1024,1024]{1,0:T(8,128)(2,1)} async-done(((bf16[1024,8192]{1,0:T(8,128)(2,1)}), bf16[1024,1024]{1,0:T(8,128)(2,1)}) %reduce-scatter.43.cloned.1.call-update) | async-done | bytes 2097168 | tf_op jit(solution)/shard_map/reduce_scatter | solution.py:258
  1625.0 285.8 %reduce-scatter.59.cloned.1.call-done = bf16[128,8192]{1,0:T(8,128)(2,1)} async-done(((bf16[1024,8192]{1,0:T(8,128)(2,1)}), bf16[128,8192]{1,0:T(8,128)(2,1)}) %reduce-scatter.59.cloned.1.call-update) | async-done | bytes 2097168
  1910.8 4.1 copy.156
  1915.1 14.5 fusion.89
  1930.5 4.4 convolution_bitcast_fusion.1
  1936.6 18.2 reduce-scatter.35.cloned.1.call-done
  1956.2 21.6 reduce-scatter.41.cloned.1.call-done
  1979.3 22.9 %reduce-scatter.39.cloned.1.call-done = bf16[256,256]{0,1:T(8,128)(2,1)} async-done(((bf16[1024,256]{0,1:T(8,128)(2,1)}), bf16[256,256]{0,1:T(8,128)(2,1)}) %reduce-scatter.39.cloned.1.call-update) | async-done | bytes 131088 | tf_op jit(solution)/shard_map/reduce_scatter | solution.py:262
  2003.9 5.8 fusion.97
  2014.3 14.3 reduce-scatter.31.cloned.1.call-done
  2030.3 32.3 %reduce-scatter.45.cloned.1.call-done = bf16[256,1024]{1,0:T(8,128)(2,1)} async-done(((bf16[1024,1024]{1,0:T(8,128)(2,1)}), bf16[256,1024]{1,0:T(8,128)(2,1)}) %reduce-scatter.45.cloned.1.call-update) | async-done | bytes 524304 | tf_op jit(solution)/shard_map/reduce_scatter | solution.py:262
  2064.7 31.9 %reduce-scatter.47.cloned.1.call-done = bf16[2048,128]{1,0:T(8,128)(2,1)} async-done(((bf16[8192,128]{1,0:T(8,128)(2,1)}), bf16[2048,128]{1,0:T(8,128)(2,1)}) %reduce-scatter.47.cloned.1.call-update) | async-done | bytes 524304 | tf_op jit(solution)/shard_map/reduce_scatter | solution.py:262
  2098.7 131.0 %all-reduce.3.cloned.1.call-done = (f32[3,1024]{1,0:T(4,128)}, f32[3,1024]{1,0:T(4,128)}, f32[3,1024]{1,0:T(4,128)}, f32[3,1024]{1,0:T(4,128)}, f32[8192]{0:T(1024)}, /*index=5*/f32[1024]{0:T(1024)}) async-done(((f32[3,1024]{1,0:T(4,128)}, f32[3,1024]{1,0:T(4,128)}, f32[3,1024]{1,0:T(4,128)}, f32[3,1024]{1,0:T(4,128)}, f32[8192]{0:T(1024)}, /*index=5*/f32[1024]{0:T(1024)}), (f32[3,1024]{1,0:T(4,128)}, ...) | async-done | bytes 86032 | tf_op jit(solution)/shard_map/psum | solution.py:466
  (465 shorter events, 249.0 us)
Async XLA Ops:
  7.2 85.0 %copy-start = (bf16[1,64,1024]{2,1,0:T(8,128)(2,1)S(1)}, bf16[1,64,1024]{2,1,0:T(8,128)(2,1)}, u32[]{:S(2)}) copy-start(bf16[1,64,1024]{2,1,0:T(8,128)(2,1)} %param.41) | copy-start | bytes 393220
  7.2 48.9 %all-gather.10.cloned.1.call-start = ((), (), s32[]{:S(2)}) async-start(), calls=%async_computation.16 | async-start | bytes 7864320 | tf_op jit(solution)/shard_map/all_gather | solution.py:316
  7.9 84.2 %all-gather.16.cloned.1.call-start = ((), (), s32[]{:S(2)}) async-start(), calls=%async_computation.19 | async-start | bytes 5242880 | tf_op jit(solution)/shard_map/all_gather | solution.py:323
  8.7 212.3 %all-gather.12.cloned.1.call-start = ((), (), s32[]{:S(2)}) async-start(), calls=%async_computation.17 | async-start | bytes 9437184 | tf_op jit(solution)/shard_map/all_gather | solution.py:343
  9.9 51.1 %copy-start.39 = (f32[256]{0:T(256)}, f32[256]{0:T(256)S(1)}, u32[]{:S(2)}) copy-start(f32[256]{0:T(256)S(1)} %broadcast_multiply_fusion.8) | copy-start | bytes 3076
  11.3 49.8 %copy-start.41 = (f32[256]{0:T(256)}, f32[256]{0:T(256)S(1)}, u32[]{:S(2)}) copy-start(f32[256]{0:T(256)S(1)} %add_rsqrt_fusion.2) | copy-start | bytes 3076
  14.1 46.9 %copy-start.34 = (f32[1,1024]{1,0:T(1,128)}, f32[1,1024]{1,0:T(1,128)S(1)}, u32[]{:S(2)}) copy-start(f32[1,1024]{1,0:T(1,128)S(1)} %get-tuple-element.1592) | copy-start | bytes 12292
  14.1 434.2 %copy-start.29 = (f32[1,1024]{1,0:T(1,128)}, f32[1,1024]{1,0:T(1,128)S(1)}, u32[]{:S(2)}) copy-start(f32[1,1024]{1,0:T(1,128)S(1)} %get-tuple-element.1591) | copy-start | bytes 12292
  15.6 45.5 %copy-start.31 = (f32[1,1024]{1,0:T(1,128)}, f32[1,1024]{1,0:T(1,128)S(1)}, u32[]{:S(2)}) copy-start(f32[1,1024]{1,0:T(1,128)S(1)} %get-tuple-element.1589) | copy-start | bytes 12292
  62.4 36.0 %copy-start.55 = (s32[1,8]{1,0:T(1,128)S(1)}, s32[1,8]{1,0:T(1,128)}, u32[]{:S(2)}) copy-start(s32[1,8]{1,0:T(1,128)} %param.43) | copy-start | bytes 100
  62.5 36.2 %copy-start.54 = (s32[1,8]{1,0:T(1,128)S(1)}, s32[1,8]{1,0:T(1,128)}, u32[]{:S(2)}) copy-start(s32[1,8]{1,0:T(1,128)} %param.44) | copy-start | bytes 100
  62.5 234.4 %all-gather.14.cloned.1.call-start = ((), (), s32[]{:S(2)}) async-start(), calls=%async_computation.18 | async-start | bytes 2621440 | tf_op jit(solution)/shard_map/all_gather | solution.py:317
  63.0 236.7 %all-gather.20.cloned.1.call-start = ((), (), s32[]{:S(2)}) async-start(), calls=%async_computation.21 | async-start | bytes 2621440 | tf_op jit(solution)/shard_map/all_gather | solution.py:322
  63.6 255.7 %all-gather.18.cloned.1.call-start = ((), (), s32[]{:S(2)}) async-start(), calls=%async_computation.20 | async-start | bytes 2359296 | tf_op jit(solution)/shard_map/all_gather | solution.py:356
  96.0 246.2 %all-gather.22.cloned.1.call-start = ((), (), s32[]{:S(2)}) async-start(), calls=%async_computation.22 | async-start | bytes 2621440 | tf_op jit(solution)/shard_map/all_gather | solution.py:324
  96.7 351.6 %all-gather.24.cloned.1.call-start = ((), (), s32[]{:S(2)}) async-start(), calls=%async_computation.23 | async-start | bytes 20971520 | tf_op jit(solution)/shard_map/all_gather | solution.py:329
  97.5 458.4 %all-gather.26.cloned.1.call-start = ((), (), s32[]{:S(2)}) async-start(), calls=%async_computation.24 | async-start | bytes 20971520 | tf_op jit(solution)/shard_map/all_gather | solution.py:330
  98.2 624.2 %reduce-scatter.49.cloned.1.call-start = ((), (), s32[]{:S(2)}) async-start(), calls=%async_computation.35 | async-start | bytes 2359296
  262.8 34.0 %copy-start.12 = (bf16[1,256,1024]{2,1,0:T(8,128)(2,1)S(1)}, bf16[1,256,1024]{2,1,0:T(8,128)(2,1)}, u32[]{:S(2)}) copy-start(bf16[1,256,1024]{2,1,0:T(8,128)(2,1)} %param.40) | copy-start | bytes 1572868
  295.5 23.8 %copy-start.28 = (f32[16,256]{1,0:T(8,128)S(1)}, f32[16,256]{1,0:T(8,128)}, u32[]{:S(2)}) copy-start(f32[16,256]{1,0:T(8,128)} %broadcast.1366) | copy-start | bytes 49156
  295.5 23.8 %copy-start.33 = (f32[16,256]{1,0:T(8,128)S(1)}, f32[16,256]{1,0:T(8,128)}, u32[]{:S(2)}) copy-start(f32[16,256]{1,0:T(8,128)} %broadcast.1367) | copy-start | bytes 49156
  296.8 22.5 %copy-start.19 = (bf16[256,16,64]{0,2,1:T(8,128)(2,1)}, bf16[256,16,64]{0,2,1:T(8,128)(2,1)S(1)}, u32[]{:S(2)}) copy-start(bf16[256,16,64]{0,2,1:T(8,128)(2,1)S(1)} %convert_element_type.268) | copy-start | bytes 1572868
  299.4 318.1 %copy-start.2 = (f32[256,1024]{1,0:T(8,128)}, f32[256,1024]{1,0:T(8,128)S(1)}, u32[]{:S(2)}) copy-start(f32[256,1024]{1,0:T(8,128)S(1)} %get-tuple-element.1603) | copy-start | bytes 3145732
  302.4 27.4 %copy-start.17 = (bf16[256,1024]{0,1:T(8,128)(2,1)}, bf16[256,1024]{0,1:T(8,128)(2,1)S(1)}, u32[]{:S(2)}) copy-start(bf16[256,1024]{0,1:T(8,128)(2,1)S(1)} %copy.114) | copy-start | bytes 1572868
  329.9 13.2 copy-start.37
  329.9 118.5 %copy-start.52 = (f32[8192]{0:T(1024)S(1)}, f32[8192]{0:T(1024)}, u32[]{:S(2)}) copy-start(f32[8192]{0:T(1024)} %param.55) | copy-start | bytes 98308
  342.1 119.1 %copy-start.21 = (bf16[256,16,64]{0,2,1:T(8,128)(2,1)}, bf16[256,16,64]{0,2,1:T(8,128)(2,1)S(1)}, u32[]{:S(2)}) copy-start(bf16[256,16,64]{0,2,1:T(8,128)(2,1)S(1)} %convert_element_type.273) | copy-start | bytes 1572868
  345.5 239.8 %copy-start.4 = (f32[256,1024]{1,0:T(8,128)}, f32[256,1024]{1,0:T(8,128)S(1)}, u32[]{:S(2)}) copy-start(f32[256,1024]{1,0:T(8,128)S(1)} %get-tuple-element.1605) | copy-start | bytes 3145732
  571.9 13.4 copy-start.26
  592.3 21.8 copy-start.36
  592.3 25.3 %copy-start.10 = (f32[256,1024]{1,0:T(8,128)S(1)}, f32[256,1024]{1,0:T(8,128)}, u32[]{:S(2)}) copy-start(f32[256,1024]{1,0:T(8,128)} %copy-done.9) | copy-start | bytes 3145732
  626.8 288.1 %reduce-scatter.29.cloned.1.call-start = ((), (), s32[]{:S(2)}) async-start(), calls=%async_computation.25 | async-start | bytes 9437184 | tf_op jit(solution)/shard_map/reduce_scatter | solution.py:434
  701.7 284.0 %reduce-scatter.53.cloned.1.call-start = ((), (), s32[]{:S(2)}) async-start(), calls=%async_computation.37 | async-start | bytes 2359296
  705.0 11.4 copy-start.22
  709.1 347.5 %reduce-scatter.55.cloned.1.call-start = ((), (), s32[]{:S(2)}) async-start(), calls=%async_computation.38 | async-start | bytes 2359296
  716.3 410.9 %reduce-scatter.57.cloned.1.call-start = ((), (), s32[]{:S(2)}) async-start(), calls=%async_computation.39 | async-start | bytes 2359296
  722.4 495.9 %reduce-scatter.37.cloned.1.call-start = ((), (), s32[]{:S(2)}) async-start(), calls=%async_computation.29 | async-start | bytes 4718592 | tf_op jit(solution)/shard_map/reduce_scatter | solution.py:258
  726.6 612.8 %reduce-scatter.51.cloned.1.call-start = ((), (), s32[]{:S(2)}) async-start(), calls=%async_computation.36 | async-start | bytes 7077888
  727.1 187.9 %copy-start.13 = (bf16[1,256,1024]{2,1,0:T(8,128)(2,1)S(1)}, bf16[1,256,1024]{2,1,0:T(8,128)(2,1)}, u32[]{:S(2)}) copy-start(bf16[1,256,1024]{2,1,0:T(8,128)(2,1)} %param.40) | copy-start | bytes 1572868
  727.1 187.8 %copy-start.32 = (f32[1,1024]{1,0:T(1,128)S(1)}, f32[1,1024]{1,0:T(1,128)}, u32[]{:S(2)}) copy-start(f32[1,1024]{1,0:T(1,128)} %copy-done.31) | copy-start | bytes 12292
  727.1 187.8 %copy-start.35 = (f32[1,1024]{1,0:T(1,128)S(1)}, f32[1,1024]{1,0:T(1,128)}, u32[]{:S(2)}) copy-start(f32[1,1024]{1,0:T(1,128)} %copy-done.34) | copy-start | bytes 12292
  727.1 187.8 %copy-start.40 = (f32[256]{0:T(256)S(1)}, f32[256]{0:T(256)}, u32[]{:S(2)}) copy-start(f32[256]{0:T(256)} %copy-done.39) | copy-start | bytes 3076
  727.1 187.8 %copy-start.42 = (f32[256]{0:T(256)S(1)}, f32[256]{0:T(256)}, u32[]{:S(2)}) copy-start(f32[256]{0:T(256)} %copy-done.41) | copy-start | bytes 3076
  929.6 695.3 %reduce-scatter.43.cloned.1.call-start = ((), (), s32[]{:S(2)}) async-start(), calls=%async_computation.32 | async-start | bytes 18874368 | tf_op jit(solution)/shard_map/reduce_scatter | solution.py:258
  940.4 970.4 %reduce-scatter.59.cloned.1.call-start = ((), (), s32[]{:S(2)}) async-start(), calls=%async_computation.40 | async-start | bytes 18874368
  973.7 941.2 %copy-start.38 = (f32[16,64]{1,0:T(8,128)S(1)}, f32[16,64]{1,0:T(8,128)}, u32[]{:S(2)}) copy-start(f32[16,64]{1,0:T(8,128)} %get-tuple-element.1561) | copy-start | bytes 12292
  973.7 941.3 %copy-start.53 = (f32[1024]{0:T(1024)S(1)}, f32[1024]{0:T(1024)}, u32[]{:S(2)}) copy-start(f32[1024]{0:T(1024)} %param.57) | copy-start | bytes 12292
  973.7 961.2 %reduce-scatter.33.cloned.1.call-start = ((), (), s32[]{:S(2)}) async-start(), calls=%async_computation.27 | async-start | bytes 327680 | tf_op jit(solution)/shard_map/reduce_scatter | solution.py:262
  987.5 967.2 %reduce-scatter.35.cloned.1.call-start = ((), (), s32[]{:S(2)}) async-start(), calls=%async_computation.28 | async-start | bytes 327680 | tf_op jit(solution)/shard_map/reduce_scatter | solution.py:262
  1058.4 919.4 %reduce-scatter.41.cloned.1.call-start = ((), (), s32[]{:S(2)}) async-start(), calls=%async_computation.31 | async-start | bytes 327680 | tf_op jit(solution)/shard_map/reduce_scatter | solution.py:262
  1129.1 873.1 %reduce-scatter.39.cloned.1.call-start = ((), (), s32[]{:S(2)}) async-start(), calls=%async_computation.30 | async-start | bytes 655360 | tf_op jit(solution)/shard_map/reduce_scatter | solution.py:262
  1218.3 810.3 %reduce-scatter.31.cloned.1.call-start = ((), (), s32[]{:S(2)}) async-start(), calls=%async_computation.26 | async-start | bytes 983040 | tf_op jit(solution)/shard_map/reduce_scatter | solution.py:262
  1341.8 720.8 %reduce-scatter.45.cloned.1.call-start = ((), (), s32[]{:S(2)}) async-start(), calls=%async_computation.33 | async-start | bytes 2621440 | tf_op jit(solution)/shard_map/reduce_scatter | solution.py:262
  1625.0 471.7 %reduce-scatter.47.cloned.1.call-start = ((), (), s32[]{:S(2)}) async-start(), calls=%async_computation.34 | async-start | bytes 2621440 | tf_op jit(solution)/shard_map/reduce_scatter | solution.py:262
  1914.8 314.9 %all-reduce.3.cloned.1.call-start = ((), (), s32[]{:S(2)}) async-start(), calls=%async_computation.41 | async-start | bytes 204800 | tf_op jit(solution)/shard_map/psum | solution.py:466
  1915.1 14.5 slice-start
  1915.1 14.8 copy-start.43
  1915.1 88.8 %copy-start.24 = (bf16[256,2048]{1,0:T(8,128)(2,1)S(1)}, bf16[256,2048]{1,0:T(8,128)(2,1)}, u32[]{:S(2)}) copy-start(bf16[256,2048]{1,0:T(8,128)(2,1)} %reduce-scatter.29.cloned.1.call-done) | copy-start | bytes 3145732
  1934.9 74.8 %copy-start.49 = (f32[1024]{0:T(1024)S(1)}, f32[1024]{0:T(1024)}, u32[]{:S(2)}) copy-start(f32[1024]{0:T(1024)} %get-tuple-element.1455) | copy-start | bytes 12292
  1934.9 74.8 %copy-start.51 = (f32[1024]{0:T(1024)S(1)}, f32[1024]{0:T(1024)}, u32[]{:S(2)}) copy-start(f32[1024]{0:T(1024)} %get-tuple-element.1453) | copy-start | bytes 12292
  1934.9 75.4 %copy-start.48 = (f32[1024]{0:T(1024)S(1)}, f32[1024]{0:T(1024)}, u32[]{:S(2)}) copy-start(f32[1024]{0:T(1024)} %get-tuple-element.1464) | copy-start | bytes 12292
  1934.9 75.4 %copy-start.50 = (f32[1024]{0:T(1024)S(1)}, f32[1024]{0:T(1024)}, u32[]{:S(2)}) copy-start(f32[1024]{0:T(1024)} %get-tuple-element.1463) | copy-start | bytes 12292
  1934.9 76.1 %copy-start.44 = (f32[1024]{0:T(1024)S(1)}, f32[1024]{0:T(1024)}, u32[]{:S(2)}) copy-start(f32[1024]{0:T(1024)} %get-tuple-element.1567) | copy-start | bytes 12292
  1934.9 76.8 %copy-start.8 = (f32[256,1024]{1,0:T(8,128)S(1)}, f32[256,1024]{1,0:T(8,128)}, u32[]{:S(2)}) copy-start(f32[256,1024]{1,0:T(8,128)} %copy-done.6) | copy-start | bytes 3145732
  (22 other events, 109.0 us)
Sparse Core Ops, SparseCore 0:
  9.6 46.4 all-gather.9
  57.6 34.4 all-gather.15
  94.9 126.0 all-gather.11
  222.4 19.6 all-gather.13
  243.5 22.5 all-gather.19
  268.6 50.6 all-gather.17
  320.9 19.9 all-gather.21
  342.4 105.9 all-gather.23
  449.9 105.9 all-gather.25
  627.0 68.9 reduce-scatter.48
  701.8 213.0 reduce-scatter.28
  918.8 66.9 reduce-scatter.52
  989.7 66.8 reduce-scatter.54
  1060.4 66.8 reduce-scatter.56
  1131.2 87.0 reduce-scatter.36
  1221.7 117.7 reduce-scatter.50
  1343.1 281.8 reduce-scatter.42
  1629.0 281.6 reduce-scatter.58
  1913.8 17.8 reduce-scatter.32
  1934.7 20.0 reduce-scatter.34
  1957.8 19.9 reduce-scatter.40
  1980.5 21.6 reduce-scatter.38
  2005.3 23.2 reduce-scatter.30
  2031.1 31.4 reduce-scatter.44
  2065.1 31.4 reduce-scatter.46
  2105.2 124.5 all-reduce.2
where the time goes:
time: 2250 us; the launch traced here: 2240 us
  waiting for transfers between devices  1740 us (77%)
  matrix products  203 us (9%)
  local copies, waits for them, and re-layouts  173 us (8%)
  other arithmetic  74.1 us (3%)
  loops' own time  32.1 us (1%)
    unnamed x32, waiting for transfers between devices  561 us
    reduce_scatter x2, waiting for transfers between devices, owners_end(): lax.psum_scatter(shortened(grads), 'ctx', scatter_dimension=1, tiled=True)  372 us
    reduce_scatter x7, waiting for transfers between devices, owners_end(): lax.psum_scatter(shortened(columns), 'fsdp', scatter_dimension=0, tiled=T...  141 us
    reduce_scatter x1, waiting for transfers between devices, per_device(): lax.psum_scatter(lax.map(one_piece, piece_starts).reshape(tok_rows * lax....  138 us
    psum x1, waiting for transfers between devices, per_device(): lax.psum((gain_grads, shift_grads, self_bias_grads, cross_bias_grads, gra...  131 us
    all_gather x1, waiting for transfers between devices, per_device(): kv_self_all = lax.all_gather(kv_self, 'ctx', axis=0, tiled=True)  118 us
    all_gather x1, waiting for transfers between devices, gather_mlp(): lax.all_gather(w_up, 'fsdp', axis=0, tiled=True)  103 us
    all_gather x1, waiting for transfers between devices, gather_mlp(): lax.all_gather(w_down, 'fsdp', axis=0, tiled=True)  94.6 us
  transfers between devices with their start and end apart: 26, of which 21 were waited for; matrix products, arithmetic and copies ran while one was open for 16% of the time, Pallas kernels for 0%

commit v1 on v0

--- a/solution.py
+++ b/solution.py
@@ -1,8 +1,12 @@
+import functools
 import math
 
 import jax
 import jax.numpy as jnp
 from jax import lax
+from jax.experimental import pallas as pl
+from jax.experimental.pallas import tpu as pltpu
+from jax.sharding import Mesh
 from jax.sharding import PartitionSpec as P
 
 HEADS = 16
@@ -487,7 +491,7 @@
     )
 
 
-def solution(mesh):
+def general_solution(mesh):
     placed = (
         P("fsdp", "ctx", None),
         P("fsdp", "ctx", None),
@@ -532,3 +536,641 @@
         ),
         check_vma=False,
     )
+
+
+CTX = ("cz", "cy")
+GRID = ("cy", "fsdp")
+QBLOCK = 256
+HALF = 128
+PAIR = 2 * HEAD_DIM
+MAX_KEY_BLOCKS = 5
+
+
+def doc_start_of(starts_ref, positions):
+    first = jnp.zeros_like(positions)
+    for doc in range(starts_ref.shape[0]):
+        begin = starts_ref[doc]
+        first = jnp.where(positions >= begin, begin, first)
+    return first
+
+
+def doc_start_scalar(starts_ref, position):
+    first = jnp.int32(0)
+    for doc in range(starts_ref.shape[0]):
+        begin = starts_ref[doc]
+        first = jnp.where(position >= begin, begin, first)
+    return first
+
+
+def half_row(pos_block, pos_blocks):
+    early = pos_block * (2 * HALF)
+    late = (pos_blocks - 1 - pos_block) * (2 * HALF) + HALF
+    return pl.multiple_of(jnp.where(2 * pos_block < pos_blocks, early, late), HALF)
+
+
+def lane_mask(rows, head):
+    lanes = lax.broadcasted_iota(jnp.int32, (rows, PAIR), 1)
+    return (lanes >= head * HEAD_DIM) & (lanes < (head + 1) * HEAD_DIM)
+
+
+def to_positions(src_ref, column, dst_ref):
+    pos_blocks = src_ref.shape[0] // HALF
+
+    def move(block, carry):
+        row = half_row(block, pos_blocks)
+        dst_ref[pl.ds(pl.multiple_of(block * HALF, HALF), HALF), :] = src_ref[
+            pl.ds(row, HALF), pl.ds(column, PAIR)
+        ]
+        return carry
+
+    lax.fori_loop(0, pos_blocks, move, 0)
+
+
+def self_forward_kernel(starts_ref, qkv_ref, out_ref, key_ref, value_ref):
+    step = pl.program_id(0)
+    pos_blocks = qkv_ref.shape[0] // HALF
+
+    @pl.when(step == 0)
+    def _():
+        to_positions(qkv_ref, PAIR, key_ref)
+        to_positions(qkv_ref, 2 * PAIR, value_ref)
+
+    row_a = half_row(2 * step, pos_blocks)
+    row_b = half_row(2 * step + 1, pos_blocks)
+    queries = jnp.concatenate(
+        [qkv_ref[pl.ds(row_a, HALF), pl.ds(0, PAIR)], qkv_ref[pl.ds(row_b, HALF), pl.ds(0, PAIR)]],
+        axis=0,
+    )
+    q_start = step * QBLOCK
+    first_block = doc_start_scalar(starts_ref, q_start) // QBLOCK
+    count = step - first_block + 1
+    q_pos = q_start + lax.broadcasted_iota(jnp.int32, (QBLOCK, 1), 0)
+    q_first = doc_start_of(starts_ref, q_pos)
+
+    def compute(blocks):
+        width = blocks * QBLOCK
+        k_start = pl.multiple_of(first_block * QBLOCK, QBLOCK)
+        keys = key_ref[pl.ds(k_start, width), :]
+        values = value_ref[pl.ds(k_start, width), :]
+        k_pos = k_start + lax.broadcasted_iota(jnp.int32, (QBLOCK, width), 1)
+        allowed = (k_pos >= q_first) & (k_pos <= q_pos)
+        parts = []
+        for head in range(2):
+            picked = jnp.where(lane_mask(QBLOCK, head), queries, jnp.zeros_like(queries))
+            scores = lax.dot_general(picked, keys, CONTRACT_COLS, preferred_element_type=jnp.float32)
+            scores = jnp.where(allowed, scores, NEG)
+            terms = jnp.exp(scores - jnp.max(scores, axis=1, keepdims=True))
+            inverse = 1.0 / jnp.sum(terms, axis=1, keepdims=True)
+            mixed = jnp.dot(
+                (terms * inverse).astype(jnp.bfloat16), values, preferred_element_type=jnp.float32
+            )
+            parts.append(mixed)
+        result = jnp.where(lane_mask(QBLOCK, 0), parts[0], parts[1]).astype(jnp.bfloat16)
+        out_ref[pl.ds(row_a, HALF), :] = result[:HALF]
+        out_ref[pl.ds(row_b, HALF), :] = result[HALF:]
+
+    for blocks in range(1, MAX_KEY_BLOCKS + 1):
+        pl.when(count == blocks)(functools.partial(compute, blocks))
+
+
+def self_backward_kernel(
+    starts_ref, qkv_ref, grad_ref, out_ref, key_ref, value_ref, dkey_ref, dvalue_ref
+):
+    step = pl.program_id(0)
+    pos_blocks = qkv_ref.shape[0] // HALF
+
+    @pl.when(step == 0)
+    def _():
+        to_positions(qkv_ref, PAIR, key_ref)
+        to_positions(qkv_ref, 2 * PAIR, value_ref)
+        dkey_ref[...] = jnp.zeros_like(dkey_ref)
+        dvalue_ref[...] = jnp.zeros_like(dvalue_ref)
+
+    row_a = half_row(2 * step, pos_blocks)
+    row_b = half_row(2 * step + 1, pos_blocks)
+    queries = jnp.concatenate(
+        [qkv_ref[pl.ds(row_a, HALF), pl.ds(0, PAIR)], qkv_ref[pl.ds(row_b, HALF), pl.ds(0, PAIR)]],
+        axis=0,
+    )
+    grads = jnp.concatenate([grad_ref[pl.ds(row_a, HALF), :], grad_ref[pl.ds(row_b, HALF), :]], axis=0)
+    q_start = step * QBLOCK
+    first_block = doc_start_scalar(starts_ref, q_start) // QBLOCK
+    count = step - first_block + 1
+    q_pos = q_start + lax.broadcasted_iota(jnp.int32, (1, QBLOCK), 1)
+    q_first = doc_start_of(starts_ref, q_pos)
+
+    def compute(blocks):
+        width = blocks * QBLOCK
+        k_start = pl.multiple_of(first_block * QBLOCK, QBLOCK)
+        keys = key_ref[pl.ds(k_start, width), :]
+        values = value_ref[pl.ds(k_start, width), :]
+        k_pos = k_start + lax.broadcasted_iota(jnp.int32, (width, QBLOCK), 0)
+        allowed = (k_pos >= q_first) & (k_pos <= q_pos)
+        dq_parts = []
+        dkey = jnp.zeros((width, PAIR), jnp.float32)
+        dvalue = jnp.zeros((width, PAIR), jnp.float32)
+        for head in range(2):
+            inside = lane_mask(QBLOCK, head)
+            picked = jnp.where(inside, queries, jnp.zeros_like(queries))
+            grad = jnp.where(inside, grads, jnp.zeros_like(grads))
+            scores = lax.dot_general(keys, picked, CONTRACT_COLS, preferred_element_type=jnp.float32)
+            scores = jnp.where(allowed, scores, NEG)
+            terms = jnp.exp(scores - jnp.max(scores, axis=0, keepdims=True))
+            probs = terms * (1.0 / jnp.sum(terms, axis=0, keepdims=True))
+            dprobs = lax.dot_general(
+                values, grad, CONTRACT_COLS, preferred_element_type=jnp.float32
+            )
+            delta = jnp.sum(probs * dprobs, axis=0, keepdims=True)
+            dscores = (probs * (dprobs - delta)).astype(jnp.bfloat16)
+            dq_parts.append(
+                lax.dot_general(dscores, keys, CONTRACT_ROWS, preferred_element_type=jnp.float32)
+            )
+            dkey = dkey + jnp.dot(dscores, picked, preferred_element_type=jnp.float32)
+            dvalue = dvalue + jnp.dot(
+                probs.astype(jnp.bfloat16), grad, preferred_element_type=jnp.float32
+            )
+        dkey_ref[pl.ds(k_start, width), :] += dkey
+        dvalue_ref[pl.ds(k_start, width), :] += dvalue
+        dq = jnp.where(lane_mask(QBLOCK, 0), dq_parts[0], dq_parts[1])
+        dq = (dq * (1.0 / math.sqrt(HEAD_DIM))).astype(jnp.bfloat16)
+        out_ref[pl.ds(row_a, HALF), pl.ds(0, PAIR)] = dq[:HALF]
+        out_ref[pl.ds(row_b, HALF), pl.ds(0, PAIR)] = dq[HALF:]
+
+    for blocks in range(1, MAX_KEY_BLOCKS + 1):
+        pl.when(count == blocks)(functools.partial(compute, blocks))
+
+    @pl.when(step == pl.num_programs(0) - 1)
+    def _():
+        def move(block, carry):
+            row = half_row(block, pos_blocks)
+            place = pl.ds(pl.multiple_of(block * HALF, HALF), HALF)
+            out_ref[pl.ds(row, HALF), pl.ds(PAIR, PAIR)] = dkey_ref[place, :].astype(jnp.bfloat16)
+            out_ref[pl.ds(row, HALF), pl.ds(2 * PAIR, PAIR)] = dvalue_ref[place, :].astype(
+                jnp.bfloat16
+            )
+            return carry
+
+        lax.fori_loop(0, pos_blocks, move, 0)
+
+
+def cross_forward_kernel(q_ref, key_ref, value_ref, low_ref, high_ref, out_ref):
+    rows, width = q_ref.shape[0], key_ref.shape[0]
+    queries, keys, values = q_ref[...], key_ref[...], value_ref[...]
+    k_pos = lax.broadcasted_iota(jnp.int32, (rows, width), 1)
+    allowed = (k_pos >= low_ref[...]) & (k_pos < high_ref[...])
+    parts = []
+    for head in range(2):
+        picked = jnp.where(lane_mask(rows, head), queries, jnp.zeros_like(queries))
+        scores = lax.dot_general(picked, keys, CONTRACT_COLS, preferred_element_type=jnp.float32)
+        scores = jnp.where(allowed, scores, NEG)
+        terms = jnp.exp(scores - jnp.max(scores, axis=1, keepdims=True))
+        inverse = 1.0 / jnp.sum(terms, axis=1, keepdims=True)
+        parts.append(
+            jnp.dot((terms * inverse).astype(jnp.bfloat16), values, preferred_element_type=jnp.float32)
+        )
+    out_ref[...] = jnp.where(lane_mask(rows, 0), parts[0], parts[1]).astype(jnp.bfloat16)
+
+
+def cross_backward_kernel(q_ref, key_ref, value_ref, grad_ref, low_ref, high_ref, dq_ref, dkv_ref):
+    rows, width = q_ref.shape[0], key_ref.shape[0]
+    queries, keys, values, grads = q_ref[...], key_ref[...], value_ref[...], grad_ref[...]
+    k_pos = lax.broadcasted_iota(jnp.int32, (width, rows), 0)
+    allowed = (k_pos >= low_ref[...]) & (k_pos < high_ref[...])
+    dq_parts = []
+    dkey = jnp.zeros((width, PAIR), jnp.float32)
+    dvalue = jnp.zeros((width, PAIR), jnp.float32)
+    for head in range(2):
+        inside = lane_mask(rows, head)
+        picked = jnp.where(inside, queries, jnp.zeros_like(queries))
+        grad = jnp.where(inside, grads, jnp.zeros_like(grads))
+        scores = lax.dot_general(keys, picked, CONTRACT_COLS, preferred_element_type=jnp.float32)
+        scores = jnp.where(allowed, scores, NEG)
+        terms = jnp.exp(scores - jnp.max(scores, axis=0, keepdims=True))
+        probs = terms * (1.0 / jnp.sum(terms, axis=0, keepdims=True))
+        dprobs = lax.dot_general(values, grad, CONTRACT_COLS, preferred_element_type=jnp.float32)
+        delta = jnp.sum(probs * dprobs, axis=0, keepdims=True)
+        dscores = (probs * (dprobs - delta)).astype(jnp.bfloat16)
+        dq_parts.append(
+            lax.dot_general(dscores, keys, CONTRACT_ROWS, preferred_element_type=jnp.float32)
+        )
+        dkey = dkey + jnp.dot(dscores, picked, preferred_element_type=jnp.float32)
+        dvalue = dvalue + jnp.dot(
+            probs.astype(jnp.bfloat16), grad, preferred_element_type=jnp.float32
+        )
+    dq = jnp.where(lane_mask(rows, 0), dq_parts[0], dq_parts[1])
+    dq_ref[...] = (dq * (1.0 / math.sqrt(HEAD_DIM))).astype(jnp.bfloat16)
+    dkv_ref[0, 0] = dkey.astype(jnp.bfloat16)
+    dkv_ref[1, 0] = dvalue.astype(jnp.bfloat16)
+
+
+def kernel_params():
+    return pltpu.CompilerParams(vmem_limit_bytes=48 * 1024 * 1024)
+
+
+def self_forward(doc_starts, qkv):
+    rows = qkv.shape[0]
+    return pl.pallas_call(
+        self_forward_kernel,
+        grid=(rows // QBLOCK,),
+        in_specs=[
+            pl.BlockSpec(memory_space=pltpu.SMEM),
+            pl.BlockSpec((rows, 3 * PAIR), lambda step: (0, 0)),
+        ],
+        out_specs=pl.BlockSpec((rows, PAIR), lambda step: (0, 0)),
+        out_shape=jax.ShapeDtypeStruct((rows, PAIR), jnp.bfloat16),
+        scratch_shapes=[pltpu.VMEM((rows, PAIR), jnp.bfloat16)] * 2,
+        compiler_params=kernel_params(),
+        cost_estimate=pl.CostEstimate(
+            flops=2 * rows * 1024 * 256 * 2, bytes_accessed=rows * PAIR * 8, transcendentals=0
+        ),
+    )(doc_starts, qkv)
+
+
+def self_backward(doc_starts, qkv, grads):
+    rows = qkv.shape[0]
+    return pl.pallas_call(
+        self_backward_kernel,
+        grid=(rows // QBLOCK,),
+        in_specs=[
+            pl.BlockSpec(memory_space=pltpu.SMEM),
+            pl.BlockSpec((rows, 3 * PAIR), lambda step: (0, 0)),
+            pl.BlockSpec((rows, PAIR), lambda step: (0, 0)),
+        ],
+        out_specs=pl.BlockSpec((rows, 3 * PAIR), lambda step: (0, 0)),
+        out_shape=jax.ShapeDtypeStruct((rows, 3 * PAIR), jnp.bfloat16),
+        scratch_shapes=[pltpu.VMEM((rows, PAIR), jnp.bfloat16)] * 2
+        + [pltpu.VMEM((rows, PAIR), jnp.float32)] * 2,
+        compiler_params=kernel_params(),
+        cost_estimate=pl.CostEstimate(
+            flops=5 * rows * 1024 * 256 * 2, bytes_accessed=rows * PAIR * 14, transcendentals=0
+        ),
+    )(doc_starts, qkv, grads)
+
+
+def cross_forward(queries, kv_cross, low, high):
+    rows, features = queries.shape
+    pairs = features // PAIR
+    src = kv_cross.shape[0]
+    return pl.pallas_call(
+        cross_forward_kernel,
+        grid=(pairs,),
+        in_specs=[
+            pl.BlockSpec((rows, PAIR), lambda p: (0, p)),
+            pl.BlockSpec((src, PAIR), lambda p: (0, p)),
+            pl.BlockSpec((src, PAIR), lambda p: (0, p + pairs)),
+            pl.BlockSpec((rows, 1), lambda p: (0, 0)),
+            pl.BlockSpec((rows, 1), lambda p: (0, 0)),
+        ],
+        out_specs=pl.BlockSpec((rows, PAIR), lambda p: (0, p)),
+        out_shape=jax.ShapeDtypeStruct((rows, features), jnp.bfloat16),
+        compiler_params=kernel_params(),
+        cost_estimate=pl.CostEstimate(
+            flops=4 * rows * src * features, bytes_accessed=3 << 20, transcendentals=0
+        ),
+    )(queries, kv_cross, kv_cross, low[:, None], high[:, None])
+
+
+def cross_backward(queries, kv_cross, grads, low, high):
+    rows, features = queries.shape
+    pairs = features // PAIR
+    src = kv_cross.shape[0]
+    return pl.pallas_call(
+        cross_backward_kernel,
+        grid=(pairs,),
+        in_specs=[
+            pl.BlockSpec((rows, PAIR), lambda p: (0, p)),
+            pl.BlockSpec((src, PAIR), lambda p: (0, p)),
+            pl.BlockSpec((src, PAIR), lambda p: (0, p + pairs)),
+            pl.BlockSpec((rows, PAIR), lambda p: (0, p)),
+            pl.BlockSpec((1, rows), lambda p: (0, 0)),
+            pl.BlockSpec((1, rows), lambda p: (0, 0)),
+        ],
+        out_specs=[
+            pl.BlockSpec((rows, PAIR), lambda p: (0, p)),
+            pl.BlockSpec((2, 1, src, PAIR), lambda p: (0, p, 0, 0)),
+        ],
+        out_shape=[
+            jax.ShapeDtypeStruct((rows, features), jnp.bfloat16),
+            jax.ShapeDtypeStruct((2, pairs, src, PAIR), jnp.bfloat16),
+        ],
+        compiler_params=kernel_params(),
+        cost_estimate=pl.CostEstimate(
+            flops=10 * rows * src * features, bytes_accessed=6 << 20, transcendentals=0
+        ),
+    )(queries, kv_cross, kv_cross, grads, low[None, :], high[None, :])
+
+
+def swap_fsdp(pieces):
+    own = lax.axis_index("fsdp")
+    count = pieces.shape[0]
+    whole = pieces
+    for distance in range(1, count):
+        moved = lax.ppermute(
+            lax.dynamic_index_in_dim(pieces, own ^ distance, 0, keepdims=False),
+            "fsdp",
+            [(i, i ^ distance) for i in range(count)],
+        )
+        whole = lax.dynamic_update_index_in_dim(whole, moved, own ^ distance, 0)
+    return whole
+
+
+def low(value):
+    return value.astype(jnp.bfloat16)
+
+
+def wide(value):
+    return value.astype(jnp.float32)
+
+
+def planned_device(
+    tokens,
+    encoded,
+    grad_out,
+    doc_lengths,
+    src_lengths,
+    norm_gain,
+    norm_bias,
+    w_qkv,
+    self_bias,
+    w_self_out,
+    w_cross_q,
+    w_cross_kv,
+    cross_bias,
+    w_cross_out,
+    w_up,
+    up_bias,
+    w_down,
+    down_bias,
+):
+    q_scale = 1.0 / math.sqrt(HEAD_DIM)
+    rows, features = tokens.shape[1:]
+    n_z, n_y, n_f = lax.axis_size("cz"), lax.axis_size("cy"), lax.axis_size("fsdp")
+    n_ctx = n_z * n_y
+    me_y, me_f = lax.axis_index("cy"), lax.axis_index("fsdp")
+    me_c = lax.axis_index(CTX)
+    shard = w_up.shape[0]
+    hidden = w_up.shape[1]
+    slab = hidden // (n_z * n_y * n_f)
+
+    own_rows = me_c * rows + jnp.arange(rows, dtype=jnp.int32)
+    tok_pos = stream_position(own_rows, rows, n_ctx)
+    lengths_row = doc_lengths[0]
+    doc_starts = jnp.cumsum(lengths_row) - lengths_row
+    tok_doc = doc_index(doc_starts, tok_pos)
+    src_row = src_lengths[0]
+    src_ends = jnp.cumsum(src_row)
+    span_low = pick_doc(src_ends - src_row, tok_doc)
+    span_high = pick_doc(src_ends, tok_doc)
+
+    qkv_cols = lax.dynamic_index_in_dim(
+        w_qkv.reshape(shard, 3, n_ctx, PAIR), me_c, 2, keepdims=False
+    ).reshape(shard, 3 * PAIR)
+    qkv_own = lax.all_gather(qkv_cols, "fsdp", axis=0, tiled=True)
+
+    tok_f32 = wide(tokens[0])
+    ln_one, normed_one, inverse_one = layer_norm(tok_f32, norm_gain[0], norm_bias[0])
+    act_one = low(ln_one)
+    act_one_all = lax.all_gather(act_one, CTX, axis=0, tiled=True)
+    full_self_out, full_cross_q, full_cross_out = (
+        lax.all_gather(w, "fsdp", axis=0, tiled=True) for w in (w_self_out, w_cross_q, w_cross_out)
+    )
+    enc_all = lax.all_gather(encoded[0], CTX, axis=0, tiled=True)
+    full_cross_kv = lax.all_gather(w_cross_kv, "fsdp", axis=0, tiled=True)
+
+    up_pieces = jnp.moveaxis(
+        lax.dynamic_index_in_dim(
+            w_up.reshape(shard, n_z, n_y, n_f, slab), me_y, 2, keepdims=False
+        ),
+        2,
+        0,
+    ).reshape(n_f, shard, n_z * slab)
+    down_pieces = lax.dynamic_index_in_dim(
+        w_down.reshape(n_y, n_f, slab, features), me_y, 0, keepdims=False
+    )
+    mlp_w = swap_fsdp(jnp.concatenate([up_pieces, down_pieces], axis=1))
+    up_own = mlp_w[:, :shard].reshape(n_f * shard, n_z * slab)
+    down_own = mlp_w[:, shard:].reshape(n_f * slab, features)
+
+    head_bias = lax.dynamic_slice_in_dim(self_bias, me_c * PAIR, PAIR, 1)
+    projected = plain_dot(act_one_all, qkv_own)
+    qkv_heads = low(
+        jnp.concatenate(
+            [
+                (projected[:, :PAIR] + head_bias[0]) * q_scale,
+                projected[:, PAIR : 2 * PAIR],
+                projected[:, 2 * PAIR :] + head_bias[1],
+            ],
+            axis=1,
+        )
+    )
+    att_heads = self_forward(doc_starts, qkv_heads)
+    att_self = lax.all_to_all(att_heads, CTX, 0, 1, tiled=True)
+    hidden_one = tok_f32 + plain_dot(att_self, full_self_out) + self_bias[2]
+
+    ln_two, normed_two, inverse_two = layer_norm(hidden_one, norm_gain[1], norm_bias[1])
+    act_two = low(ln_two)
+    q_cross = low((plain_dot(act_two, full_cross_q) + cross_bias[0]) * q_scale)
+    kv_bias = jnp.concatenate([jnp.zeros((features,), jnp.float32), cross_bias[1]])
+    kv_cross = low(plain_dot(enc_all, full_cross_kv) + kv_bias)
+    att_cross = cross_forward(q_cross, kv_cross, span_low, span_high)
+    hidden_two = hidden_one + plain_dot(att_cross, full_cross_out) + cross_bias[2]
+
+    ln_three, normed_three, inverse_three = layer_norm(hidden_two, norm_gain[2], norm_bias[2])
+    act_three = lax.all_gather(low(ln_three), GRID, axis=0, tiled=True)
+    grad_all = lax.all_gather(grad_out[0], GRID, axis=0, tiled=True)
+    up_bias_own = lax.dynamic_index_in_dim(
+        lax.dynamic_index_in_dim(up_bias.reshape(n_z, n_y, n_f, slab), me_f, 2, keepdims=False),
+        me_y,
+        1,
+        keepdims=False,
+    ).reshape(-1)
+    pre_act = plain_dot(act_three, up_own) + up_bias_own
+    gelu_low = low(gelu_value(pre_act))
+    slope = gelu_slope(pre_act)
+    pre_grad = low(times_transpose(grad_all, down_own) * slope)
+    act_grad = lax.psum_scatter(
+        low(times_transpose(pre_grad, up_own)), GRID, scatter_dimension=0, tiled=True
+    )
+    down_part = low(plain_dot(gelu_low, down_own))
+
+    upstream = wide(grad_out[0])
+    norm_in_three, gain_grad_three, shift_grad_three = norm_back(
+        wide(act_grad), normed_three, inverse_three, norm_gain[2]
+    )
+    grad_two = upstream + norm_in_three
+    down_part, grad_two = lax.optimization_barrier((down_part, grad_two))
+    mlp_out = lax.psum_scatter(down_part, GRID, scatter_dimension=0, tiled=True)
+    layer_out = low(hidden_two + wide(mlp_out) + down_bias)
+
+    up_grad = low(outer_rows(pre_grad, act_three))
+    down_grad = low(outer_rows(grad_all, gelu_low))
+    up_grad = lax.psum_scatter(up_grad, "cz", scatter_dimension=0, tiled=True)
+    down_grad = lax.psum_scatter(down_grad, "cz", scatter_dimension=0, tiled=True)
+    up_bias_grad = jnp.sum(wide(pre_grad), axis=0)
+    grad_down_bias = jnp.sum(upstream, axis=0)
+
+    cross_grad_low = low(grad_two)
+    grad_w_cross_out = low(outer_rows(att_cross, cross_grad_low))
+    cross_out_bias_grad = jnp.sum(wide(cross_grad_low), axis=0)
+    cross_att_grad = low(times_transpose(cross_grad_low, full_cross_out))
+    cross_v_bias_grad = jnp.sum(wide(cross_att_grad), axis=0)
+    cross_q_low, cross_kv_part = cross_backward(
+        q_cross, kv_cross, cross_att_grad, span_low, span_high
+    )
+    grad_w_cross_q = low(outer_rows(act_two, cross_q_low))
+    cross_q_bias_grad = jnp.sum(wide(cross_q_low), axis=0)
+    norm_in_two, gain_grad_two, shift_grad_two = norm_back(
+        times_transpose(cross_q_low, full_cross_q), normed_two, inverse_two, norm_gain[1]
+    )
+    grad_one = grad_two + norm_in_two
+    self_grad_low = low(grad_one)
+    self_att_grad = low(times_transpose(self_grad_low, full_self_out))
+    self_v_bias_grad = jnp.sum(wide(self_att_grad), axis=0)
+    att_grad_heads = lax.all_to_all(self_att_grad, CTX, 1, 0, tiled=True)
+    proj_grad_heads = self_backward(doc_starts, qkv_heads, att_grad_heads)
+
+    grad_w_self_out = low(outer_rows(att_self, self_grad_low))
+    self_out_bias_grad = jnp.sum(wide(self_grad_low), axis=0)
+
+    blocks = 2 * features // PAIR
+    src_rows = enc_all.shape[0]
+    cross_kv_grad = lax.psum_scatter(
+        cross_kv_part.reshape(blocks, src_rows, PAIR), CTX, scatter_dimension=0, tiled=True
+    )
+    per = blocks // n_ctx
+    cross_kv_grad = jnp.concatenate([cross_kv_grad[i] for i in range(per)], axis=1)
+    kv_w_own = lax.dynamic_slice_in_dim(full_cross_kv, me_c * per * PAIR, per * PAIR, 1)
+    grad_encoded = wide(
+        lax.psum_scatter(
+            low(times_transpose(cross_kv_grad, kv_w_own)), CTX, scatter_dimension=0, tiled=True
+        )
+    )
+    grad_w_cross_kv = wide(
+        lax.psum_scatter(
+            low(outer_rows(enc_all, cross_kv_grad)), "fsdp", scatter_dimension=0, tiled=True
+        )
+    )
+
+    proj_grad = lax.all_to_all(
+        proj_grad_heads.reshape(n_ctx, rows, 3 * PAIR), CTX, 0, 0, tiled=False
+    )
+    full_qkv = lax.all_gather(w_qkv, "fsdp", axis=0, tiled=True)
+    proj_grad = jnp.transpose(proj_grad.reshape(n_ctx, rows, 3, PAIR), (1, 2, 0, 3)).reshape(
+        rows, 3 * features
+    )
+    self_q_bias_grad = jnp.sum(wide(proj_grad[:, :features]), axis=0)
+    norm_in_one, gain_grad_one, shift_grad_one = norm_back(
+        times_transpose(proj_grad, full_qkv), normed_one, inverse_one, norm_gain[0]
+    )
+    grad_tokens = grad_one + norm_in_one
+
+    qkv_grad = lax.psum_scatter(
+        low(outer_rows(act_one_all, proj_grad_heads)), "fsdp", scatter_dimension=0, tiled=True
+    ).reshape(shard, 3, PAIR)
+    qkv_blocks = []
+    inverse_of_three = pow(3, -1, n_ctx)
+    for slot in range(3):
+        pairs = [((3 * dest + slot) % n_ctx, dest) for dest in range(n_ctx)]
+        dest = (inverse_of_three * (me_c - slot)) % n_ctx
+        part = (3 * dest + slot) // n_ctx
+        qkv_blocks.append(
+            lax.ppermute(
+                lax.dynamic_index_in_dim(qkv_grad, part, 1, keepdims=False), CTX, pairs
+            )
+        )
+    grad_w_qkv = wide(jnp.concatenate(qkv_blocks, axis=1))
+
+    three = jnp.concatenate([grad_w_self_out, grad_w_cross_q, grad_w_cross_out], axis=1)
+    three = lax.psum_scatter(three, "fsdp", scatter_dimension=0, tiled=True)
+    width = features // n_ctx
+    three = jnp.transpose(three.reshape(shard, 3, n_ctx, width), (2, 1, 0, 3)).reshape(
+        n_ctx * 3 * shard, width
+    )
+    three = wide(lax.psum_scatter(three, CTX, scatter_dimension=0, tiled=True)).reshape(
+        3, shard, width
+    )
+
+    mlp_pieces = jnp.concatenate(
+        [
+            jnp.moveaxis(up_grad.reshape(slab, n_f, shard), 1, 0),
+            jnp.moveaxis(down_grad.reshape(features // n_z, n_f, slab), 1, 0),
+        ],
+        axis=1,
+    )
+    mlp_pieces = swap_fsdp(mlp_pieces)
+    grad_w_up = wide(jnp.transpose(mlp_pieces[:, :slab].reshape(n_f * slab, shard)))
+    down_cols = mlp_pieces[:, slab:].reshape(n_f, n_y, width, slab)
+    other = lax.ppermute(
+        lax.dynamic_index_in_dim(down_cols, 1 - me_y, 1, keepdims=False), "cy", [(0, 1), (1, 0)]
+    )
+    mine = lax.dynamic_index_in_dim(down_cols, me_y, 1, keepdims=False)
+    down_halves = jnp.stack([jnp.where(me_y == 0, mine, other), jnp.where(me_y == 0, other, mine)])
+    grad_w_down = wide(jnp.transpose(down_halves, (0, 1, 3, 2)).reshape(n_y * n_f * slab, width))
+
+    vectors = jnp.stack(
+        [
+            gain_grad_one,
+            gain_grad_two,
+            gain_grad_three,
+            shift_grad_one,
+            shift_grad_two,
+            shift_grad_three,
+            self_q_bias_grad,
+            self_v_bias_grad,
+            self_out_bias_grad,
+            cross_q_bias_grad,
+            cross_v_bias_grad,
+            cross_out_bias_grad,
+            grad_down_bias,
+            up_bias_grad,
+        ]
+    )
+    gathered = lax.all_gather(vectors, GRID, axis=0, tiled=False)
+    up_rows = gathered[:, -1]
+    level = jnp.concatenate([jnp.sum(gathered[:, :-1], axis=0), up_rows], axis=0)
+    level = jnp.sum(lax.all_gather(level, "cz", axis=0, tiled=False), axis=0)
+    grad_up_bias = jnp.transpose(
+        level[13:].reshape(n_y, n_f, n_z, slab), (2, 0, 1, 3)
+    ).reshape(hidden)
+
+    return (
+        layer_out[None],
+        grad_tokens[None],
+        grad_encoded[None],
+        level[0:3],
+        level[3:6],
+        grad_w_qkv,
+        level[6:9],
+        three[0],
+        three[1],
+        grad_w_cross_kv,
+        level[9:12],
+        three[2],
+        grad_w_up,
+        grad_up_bias,
+        grad_w_down,
+        level[12],
+    )
+
+
+def planned_solution(mesh):
+    n_ctx, n_f = mesh.shape["ctx"], mesh.shape["fsdp"]
+    split = Mesh(mesh.devices.reshape(n_ctx // 2, 2, n_f), ("cz", "cy", "fsdp"))
+    token = P("fsdp", CTX, None)
+    row = P("fsdp", None)
+    owned = P("fsdp", CTX)
+    return jax.shard_map(
+        planned_device,
+        mesh=split,
+        in_specs=(token, token, token, row, row, P(), P(), row, P(), row, row, row, P(), row)
+        + (row, P(), row, P()),
+        out_specs=(token, token, token, P(), P(), owned, P(), owned, owned, owned, P(), owned)
+        + (owned, P(), owned, P()),
+        check_vma=False,
+    )
+
+
+def solution(mesh):
+    if mesh.shape["ctx"] * 2 == HEADS and mesh.shape["fsdp"] * 2 == mesh.shape["ctx"]:
+        return planned_solution(mesh)
+    return general_solution(mesh)

time: 2250 us -> 1000 us (0.44)
  waiting for transfers between devices: 1740 us -> 617 us
  local copies, waits for them, and re-layouts: 173 us -> 67 us
  matrix products: 203 us -> 104 us
  blocking collectives: 0 us -> 60.9 us
  Pallas kernels: 0 us -> 53.3 us
  starting transfers between devices: 1.8 us -> 36 us
  other arithmetic: 74.1 us -> 40.3 us
  loops' own time: 32.1 us -> 0 us
    unnamed x32 -> x19, waiting for transfers between devices: 561 us -> 4.89 us
    reduce_scatter x10, waiting for transfers between devices: 651 us -> 345 us  [the longest x1 66.3 us: planned_device(): lax.psum_scatter(three, CTX, scatter_dimension=0, tiled=True)]
    all_gather x9, waiting for transfers between devices: 400 us -> 182 us  [the longest x1 59.6 us: planned_device(): act_one_all = lax.all_gather(act_one, CTX, axis=0, tiled=True)]
    psum x1 -> x0, waiting for transfers between devices: 131 us -> none  [per_device(): lax.psum((gain_grads, shift_grads, self_bias_grads, cross_bias_grads, gra...]
    ppermute x0 -> x10, waiting for transfers between devices: none -> 84.8 us  [the longest x6 74.9 us: swap_fsdp(): lax.ppermute(lax.dynamic_index_in_dim(pieces, own ^ distance, 0, keepdims...]
    dot_general x24 -> x0, matrix products: 74.7 us -> none  [the longest x9 17.8 us: score_block(): jnp.einsum('qhd,khd->hqk', queries, key_heads, preferred_element_type=jnp...]
    unnamed x126 -> x68, local copies, waits for them, and re-layouts: 84.5 us -> 23.8 us
    pallas_call x0 -> x4, Pallas kernels: none -> 53.3 us  [the longest x1 17.7 us: self_backward(): pl.pallas_call(self_backward_kernel, grid=(rows // QBLOCK,), in_specs=[pl...]
  transfers between devices with their start and end apart: 26 -> 31, of which waited for: 21 -> 21; matrix products, arithmetic and copies ran while one was open for 16% -> 17% of each run, Pallas kernels for 0% -> 4%
where the time goes in v1:
time: 1000 us; the launch traced here: 994 us
  waiting for transfers between devices  617 us (62%)
  matrix products  104 us (10%)
  local copies, waits for them, and re-layouts  67 us (7%)
  blocking collectives  60.9 us (6%)
  Pallas kernels  53.3 us (5%)
  other arithmetic  40.3 us (4%)
  starting transfers between devices  36 us (4%)
  between operations  15.1 us (2%)
    ppermute x6, waiting for transfers between devices, swap_fsdp(): lax.ppermute(lax.dynamic_index_in_dim(pieces, own ^ distance, 0, keepdims...  74.9 us
    reduce_scatter x1, waiting for transfers between devices, planned_device(): lax.psum_scatter(three, CTX, scatter_dimension=0, tiled=True)  66.3 us
    all_gather x1, waiting for transfers between devices, planned_device(): act_one_all = lax.all_gather(act_one, CTX, axis=0, tiled=True)  59.6 us
    reduce_scatter x1, waiting for transfers between devices, planned_device(): lax.psum_scatter(down_grad, 'cz', scatter_dimension=0, tiled=True)  56.8 us
    reduce_scatter x1, waiting for transfers between devices, planned_device(): lax.psum_scatter(low(times_transpose(cross_kv_grad, kv_w_own)), CTX, scat...  55 us
    reduce_scatter x1, waiting for transfers between devices, planned_device(): mlp_out = lax.psum_scatter(down_part, GRID, scatter_dimension=0, tiled=True)  52.3 us
    all_gather x3, waiting for transfers between devices, planned_device(): lax.all_gather(w, 'fsdp', axis=0, tiled=True)  50.4 us
    reduce_scatter x1, waiting for transfers between devices, planned_device(): lax.psum_scatter(low(times_transpose(pre_grad, up_own)), GRID, scatter_di...  41.4 us
  transfers between devices with their start and end apart: 31, of which 21 were waited for; matrix products, arithmetic and copies ran while one was open for 17% of the time, Pallas kernels for 4%

profile of v1, /device:TPU:2, one launch (start us, length us, event | category | flops | bytes accessed | tf_op | source)
XLA Modules:
  0.0 993.5 jit_solution(12714457316795487895)
XLA Ops:
  11.6 2.1 fusion.28
  19.7 8.2 all_gather.43
  28.9 59.6 %all-gather.16.cloned.1.call-done = bf16[2048,1024]{1,0:T(8,128)(2,1)} async-done(((bf16[256,1024]{1,0:T(8,128)(2,1)}), bf16[2048,1024]{1,0:T(8,128)(2,1)}) %all-gather.16.cloned.1.call-update) | async-done | bytes 4194320 | tf_op jit(solution)/shard_map/all_gather | solution.py:933
  88.5 4.6 fusion.80
  93.6 11.6 %shard_map.297 = bf16[2048,128]{1,0:T(8,128)(2,1)S(1)} custom-call(s32[8]{0:T(128)S(1)} %bitcast_subtract_fusion.2.starts_ref, bf16[2048,384]{1,0:T(8,128)(2,1)S(1)} %pad_maximum_fusion.2.qkv_ref), custom_call_target="tpu_custom_call" | custom-call | flops 2147483648 | bytes 2097152 | tf_op jit(solution)/shard_map/pallas_call | solution.py:772
  107.4 4.1 all-to-all-start
  111.6 11.9 %all-gather.26.cloned.1.call-start = ((), (), s32[]{:S(2)}) async-start(), calls=%async_computation.18 | async-start | bytes 4718592 | tf_op jit(solution)/shard_map/all_gather | solution.py:979
  124.7 8.9 all-gather.30.cloned.1.call-done
  133.5 33.7 %all-gather.22.cloned.1.call-done = bf16[1024,2048]{1,0:T(8,128)(2,1)} async-done(((bf16[256,2048]{1,0:T(8,128)(2,1)}), bf16[1024,2048]{1,0:T(8,128)(2,1)}) %all-gather.22.cloned.1.call-update) | async-done | bytes 4194320 | tf_op jit(solution)/shard_map/all_gather | solution.py:938
  167.3 4.8 add_convert_fusion.key_ref.value_ref
  172.1 19.2 %all-gather.18.cloned.1.call-done = bf16[1024,1024]{1,0:T(8,128)(2,1)} async-done(((bf16[256,1024]{1,0:T(8,128)(2,1)}), bf16[1024,1024]{1,0:T(8,128)(2,1)}) %all-gather.18.cloned.1.call-update) | async-done | bytes 2097168 | tf_op jit(solution)/shard_map/all_gather | solution.py:935
  191.3 2.6 fusion.78
  195.1 20.2 %all-gather.20.cloned.1.call-done = bf16[1024,1024]{1,0:T(8,128)(2,1)} async-done(((bf16[256,1024]{1,0:T(8,128)(2,1)}), bf16[1024,1024]{1,0:T(8,128)(2,1)}) %all-gather.20.cloned.1.call-update) | async-done | bytes 2097168 | tf_op jit(solution)/shard_map/all_gather | solution.py:935
  215.3 2.7 fusion.19.q_ref
  218.0 9.5 shard_map.298
  228.4 11.0 %all-gather.24.cloned.1.call-done = bf16[1024,1024]{1,0:T(8,128)(2,1)} async-done(((bf16[256,1024]{1,0:T(8,128)(2,1)}), bf16[1024,1024]{1,0:T(8,128)(2,1)}) %all-gather.24.cloned.1.call-update) | async-done | bytes 2097168 | tf_op jit(solution)/shard_map/all_gather | solution.py:935
  239.4 2.7 fusion.79
  244.9 6.4 copy.159
  251.3 2.0 dynamic-slice_bitcast_fusion
  256.3 4.0 copy.186
  260.3 3.6 fusion.46
  265.8 3.0 pad_maximum_fusion.1
  270.2 31.5 %collective-permute-done.1 = bf16[512,1024]{0,1:T(8,128)(2,1)} collective-permute-done((bf16[512,1024]{0,1:T(8,128)(2,1)}, bf16[512,1024]{0,1:T(8,128)(2,1)}, u32[]{:S(2)}, u32[]{:S(2)}) %collective-permute-start.1) | collective-permute-done | bytes 1048608 | tf_op jit(solution)/shard_map/ppermute | solution.py:868
  303.1 31.5 %collective-permute-done.2 = bf16[512,1024]{0,1:T(8,128)(2,1)} collective-permute-done((bf16[512,1024]{0,1:T(8,128)(2,1)}, bf16[512,1024]{0,1:T(8,128)(2,1)}, u32[]{:S(2)}, u32[]{:S(2)}) %collective-permute-start.2) | collective-permute-done | bytes 1048608 | tf_op jit(solution)/shard_map/ppermute | solution.py:868
  336.0 2.3 fusion.71
  338.3 4.0 copy.163
  342.3 4.0 copy.164
  346.3 10.6 %fusion.81 = f32[2048,1024]{1,0:T(8,128)} fusion(bf16[2048,1024]{1,0:T(8,128)(2,1)} %all-gather.26.cloned.1.call-done, bf16[1024,1024]{1,0:T(8,128)(2,1)} %bitcast.278), kind=kOutput, calls=%fused_computation.200 | convolution fusion | flops 4294967296 | bytes 14680064 | tf_op jit(solution)/shard_map/dot_general | solution.py:76
  356.9 12.7 %convert_reduce_fusion = (f32[1024]{0:T(1024)S(1)}, bf16[2048,1024]{1,0:T(8,128)(2,1)S(1)}) fusion(f32[2048,1024]{1,0:T(8,128)} %fusion.81, f32[1024]{0:T(1024)S(1)} %bitcast.329, bf16[1024,1024]{1,0:T(8,128)(2,1)} %bitcast.276, bf16[1,2048,1024]{2,1,0:T(8,128)(2,1)} %all-gather.32.cloned.1.call-done), kind=kOutput, calls=%fused_computation.9 | convolution fusion | flops 4341103616 | bytes 18882560 | tf_op jit(solution)/shard_map/dot_general | solution.py:72
  371.6 6.7 convolution_convert_fusion
  378.4 11.8 %convolution_convert_fusion.1 = bf16[2048,1024]{1,0:T(8,128)(2,1)} fusion(bf16[1024,1024]{1,0:T(8,128)(2,1)} %bitcast.277, f32[2048,1024]{1,0:T(8,128)} %fusion.81, f32[1024]{0:T(1024)S(1)} %bitcast.330), kind=kOutput, calls=%fused_computation.24 | convolution fusion | flops 4318035968 | bytes 14684160 | tf_op jit(solution)/shard_map/dot_general | solution.py:76
  390.2 41.4 %reduce-scatter.11.cloned.1.call-done = bf16[256,1024]{1,0:T(8,128)(2,1)} async-done(((bf16[2048,1024]{1,0:T(8,128)(2,1)}), bf16[256,1024]{1,0:T(8,128)(2,1)}) %reduce-scatter.11.cloned.1.call-update) | async-done | bytes 524304 | tf_op jit(solution)/shard_map/reduce_scatter | solution.py:991
  431.5 2.1 fusion.40
  436.4 14.5 %shard_map.299 = (bf16[256,1024]{1,0:T(8,128)(2,1)S(1)}, bf16[2,8,512,128]{3,2,1,0:T(8,128)(2,1)S(1)}) custom-call(bf16[256,1024]{1,0:T(8,128)(2,1)S(1)} %copy-done.2, bf16[512,2048]{1,0:T(8,128)(2,1)S(1)} %add_convert_fusion.key_ref.value_ref, bf16[512,2048]{1,0:T(8,128)(2,1)S(1)} %add_convert_fusion.key_ref.value_ref, ...), custom_call_target="tpu_custom_call" | custom-call | flops 1342177280 | bytes 6291456 | tf_op jit(solution)/shard_map/pallas_call | solution.py:837
  452.5 9.4 convolution_convert_fusion.2
  461.9 12.1 %convert_bitcast_fusion = bf16[1024,1024]{0,1:T(8,128)(2,1)} fusion(bf16[1,2048,1024]{2,1,0:T(8,128)(2,1)} %all-gather.32.cloned.1.call-done, f32[2048,1024]{1,0:T(8,128)} %fusion.81, f32[1024]{0:T(1024)S(1)} %bitcast.331), kind=kOutput, calls=%fused_computation.25 | convolution fusion | flops 4316987392 | bytes 14684160 | tf_op jit(solution)/shard_map/dot_general | solution.py:68
  474.4 2.8 multiply_reduce_fusion
  481.1 13.3 %pad_maximum_fusion = bf16[1024,3072]{0,1:T(8,128)(2,1)} fusion(bf16[1024,1024]{0,1:T(8,128)(2,1)S(1)} %convolution_convert_fusion.3, bf16[1024,1024]{0,1:T(8,128)(2,1)S(1)} %convolution_convert_fusion.4, bf16[1024,1024]{0,1:T(8,128)(2,1)S(1)} %convolution_convert_fusion.5), kind=kLoop, calls=%fused_computation.11 | loop fusion | flops 18874368 | bytes 12582912 | tf_op jit(solution)/shard_map/concatenate | solution.py:1083
  494.5 2.5 convert_reduce_fusion.8
  497.1 27.8 %all_to_all.43 = bf16[256,8,128]{2,0,1:T(8,128)(2,1)S(1)} all-to-all(bf16[256,8,128]{2,0,1:T(8,128)(2,1)S(1)} %copy_bitcast_fusion), channel_id=1, replica_groups=mesh['cz'=4,'cy'=2,'fsdp'=4] {'cz','cy'}, dimensions={1} | all-to-all | bytes 1048576 | tf_op jit(solution)/shard_map/all_to_all | solution.py:1029
  524.9 17.7 %shard_map.300 = bf16[2048,384]{1,0:T(8,128)(2,1)S(1)} custom-call(s32[8]{0:T(128)S(1)} %bitcast_subtract_fusion.2.starts_ref, bf16[2048,384]{1,0:T(8,128)(2,1)S(1)} %copy-done.4, bf16[2048,128]{1,0:T(8,128)(2,1)S(1)} %bitcast.258), custom_call_target="tpu_custom_call" | custom-call | flops 5368709120 | bytes 3670016 | tf_op jit(solution)/shard_map/pallas_call | solution.py:791
  543.8 3.3 convolution_convert_fusion.7
  550.1 2.6 convolution_convert_fusion.6
  555.0 4.4 all-to-all-start.2
  559.6 18.6 %reduce-scatter.27.cloned.1.call-done = bf16[256,1024]{1,0:T(8,128)(2,1)} async-done(((bf16[1024,1024]{1,0:T(8,128)(2,1)}), bf16[256,1024]{1,0:T(8,128)(2,1)}) %reduce-scatter.27.cloned.1.call-update) | async-done | bytes 524304 | tf_op jit(solution)/shard_map/reduce_scatter | solution.py:1007
  579.3 56.8 %reduce-scatter.29.cloned.1.call-done = bf16[256,1024]{0,1:T(8,128)(2,1)} async-done(((bf16[1024,1024]{0,1:T(8,128)(2,1)}), bf16[256,1024]{0,1:T(8,128)(2,1)}) %reduce-scatter.29.cloned.1.call-update) | async-done | bytes 524304 | tf_op jit(solution)/shard_map/reduce_scatter | solution.py:1008
  639.6 7.1 collective-permute-done.7
  646.7 4.8 collective-permute-done.8
  655.2 5.8 collective-permute-done.9
  661.0 35.5 %reduce-scatter.21.cloned.1.call-done = bf16[256,3072]{0,1:T(8,128)(2,1)} async-done(((bf16[1024,3072]{0,1:T(8,128)(2,1)}), bf16[256,3072]{0,1:T(8,128)(2,1)}) %reduce-scatter.21.cloned.1.call-update) | async-done | bytes 1572880 | tf_op jit(solution)/shard_map/reduce_scatter | solution.py:1084
  696.6 2.6 copy.173
  700.2 2.6 copy.180
  702.8 19.5 %reduce-scatter.19.cloned.1.call-done = bf16[256,384]{1,0:T(8,128)(2,1)} async-done(((bf16[1024,384]{1,0:T(8,128)(2,1)}), bf16[256,384]{1,0:T(8,128)(2,1)}) %reduce-scatter.19.cloned.1.call-update) | async-done | bytes 196624 | tf_op jit(solution)/shard_map/reduce_scatter | solution.py:1067
  724.3 6.4 collective-permute-start.4
  732.8 4.1 collective-permute-done.5
  740.7 29.5 %all-gather.28.cloned.1.call-done = bf16[1024,3072]{1,0:T(8,128)(2,1)} async-done(((bf16[256,3072]{1,0:T(8,128)(2,1)}), bf16[1024,3072]{1,0:T(8,128)(2,1)}) %all-gather.28.cloned.1.call-update) | async-done | bytes 6291472 | tf_op jit(solution)/shard_map/all_gather | solution.py:1057
  770.2 6.3 fusion.34
  776.6 10.2 %all-gather.4 = f32[8,14,1024]{2,1,0:T(8,128)S(1)} all-gather(f32[1,14,1024]{2,1,0:T(8,128)S(1)} %bitcast.291), channel_id=4, replica_groups=mesh['cz'=4,'cy'=2,'fsdp'=4] {'cy','fsdp'}, dimensions={0}, use_global_device_ids=true | all-gather | bytes 516096 | tf_op jit(solution)/shard_map/all_gather | solution.py:1128
  786.9 14.8 %all-gather.5 = f32[4,21,1024]{2,1,0:T(8,128)S(1)} all-gather(f32[1,21,1024]{2,1,0:T(8,128)S(1)} %maximum_bitcast_fusion), channel_id=5, replica_groups=mesh['cz'=4,'cy'=2,'fsdp'=4] {'cz'}, dimensions={0}, use_global_device_ids=true | all-gather | bytes 430080 | tf_op jit(solution)/shard_map/all_gather | solution.py:1131
  803.6 2.6 fusion.33
  807.9 55.0 %reduce-scatter.17.cloned.1.call-done = bf16[64,1024]{1,0:T(8,128)(2,1)} async-done(((bf16[512,1024]{1,0:T(8,128)(2,1)}), bf16[64,1024]{1,0:T(8,128)(2,1)}) %reduce-scatter.17.cloned.1.call-update) | async-done | bytes 131088 | tf_op jit(solution)/shard_map/reduce_scatter | solution.py:1044
  864.5 52.3 %reduce-scatter.13.cloned.1.call-done = bf16[256,1024]{1,0:T(8,128)(2,1)} async-done(((bf16[2048,1024]{1,0:T(8,128)(2,1)}), bf16[256,1024]{1,0:T(8,128)(2,1)}) %reduce-scatter.13.cloned.1.call-update) | async-done | bytes 524304 | tf_op jit(solution)/shard_map/reduce_scatter | solution.py:1002
  916.8 2.0 fusion.52
  918.8 66.3 %reduce-scatter.23.cloned.1.call-done = bf16[768,128]{1,0:T(8,128)(2,1)} async-done(((bf16[6144,128]{1,0:T(8,128)(2,1)}), bf16[768,128]{1,0:T(8,128)(2,1)}) %reduce-scatter.23.cloned.1.call-update) | async-done | bytes 196624 | tf_op jit(solution)/shard_map/reduce_scatter | solution.py:1089
  (213 shorter events, 70.3 us)
Async XLA Ops:
  7.2 9.8 copy-start.28
  7.2 10.0 %copy-start.17 = (bf16[256,3072]{1,0:T(8,128)(2,1)S(1)}, bf16[256,3072]{1,0:T(8,128)(2,1)}, u32[]{:S(2)}) copy-start(bf16[256,3072]{1,0:T(8,128)(2,1)} %param.25) | copy-start | bytes 4718596
  7.2 81.3 %all-gather.16.cloned.1.call-start = ((), (), s32[]{:S(2)}) async-start(), calls=%async_computation.13 | async-start | bytes 4718592 | tf_op jit(solution)/shard_map/all_gather | solution.py:933
  13.7 15.0 %copy-start.29 = (s32[1,8]{1,0:T(1,128)S(1)}, s32[1,8]{1,0:T(1,128)}, u32[]{:S(2)}) copy-start(s32[1,8]{1,0:T(1,128)} %param.22) | copy-start | bytes 100
  13.7 119.8 %all-gather.30.cloned.1.call-start = ((), (), s32[]{:S(2)}) async-start(), calls=%async_computation.30 | async-start | bytes 1179648 | tf_op jit(solution)/shard_map/all_gather | solution.py:937
  14.5 152.8 %all-gather.22.cloned.1.call-start = ((), (), s32[]{:S(2)}) async-start(), calls=%async_computation.16 | async-start | bytes 5242880 | tf_op jit(solution)/shard_map/all_gather | solution.py:938
  15.2 176.1 %all-gather.18.cloned.1.call-start = ((), (), s32[]{:S(2)}) async-start(), calls=%async_computation.14 | async-start | bytes 2621440 | tf_op jit(solution)/shard_map/all_gather | solution.py:935
  15.8 199.6 %all-gather.20.cloned.1.call-start = ((), (), s32[]{:S(2)}) async-start(), calls=%async_computation.15 | async-start | bytes 2621440 | tf_op jit(solution)/shard_map/all_gather | solution.py:935
  16.4 223.0 %all-gather.24.cloned.1.call-start = ((), (), s32[]{:S(2)}) async-start(), calls=%async_computation.17 | async-start | bytes 2621440 | tf_op jit(solution)/shard_map/all_gather | solution.py:935
  93.6 31.0 %copy-start.24 = (f32[3,1024]{1,0:T(4,128)S(1)}, f32[3,1024]{1,0:T(4,128)}, u32[]{:S(2)}) copy-start(f32[3,1024]{1,0:T(4,128)} %param.30) | copy-start | bytes 36868
  105.3 1.2 copy-start.3
  107.4 83.9 %all-to-all-start = ((bf16[8,256,128]{1,2,0:T(8,128)(2,1)}), bf16[8,256,128]{1,2,0:T(8,128)(2,1)}, u32[]{:S(2)}, u32[]{:S(2)}) async-start(bf16[8,256,128]{1,2,0:T(8,128)(2,1)} %copy.156), calls=%async_computation | async-start | bytes 1048576 | tf_op jit(solution)/shard_map/all_to_all | solution.py:967
  111.6 234.7 %all-gather.26.cloned.1.call-start = ((), (), s32[]{:S(2)}) async-start(), calls=%async_computation.18 | async-start | bytes 4718592 | tf_op jit(solution)/shard_map/all_gather | solution.py:979
  124.7 66.7 %copy-start.14 = (bf16[1,256,1024]{2,1,0:T(8,128)(2,1)S(1)}, bf16[1,256,1024]{2,1,0:T(8,128)(2,1)}, u32[]{:S(2)}) copy-start(bf16[1,256,1024]{2,1,0:T(8,128)(2,1)} %param.18) | copy-start | bytes 1572868
  193.9 1.0 copy-start.9
  227.6 0.8 copy-start.1
  242.1 1.0 copy-start.7
  244.1 112.8 %all-gather.32.cloned.1.call-start = ((), (), s32[]{:S(2)}) async-start(), calls=%async_computation.31 | async-start | bytes 4718592 | tf_op jit(solution)/shard_map/all_gather | solution.py:980
  244.9 186.7 %reduce-scatter.11.cloned.1.call-start = ((), (), s32[]{:S(2)}) async-start(), calls=%async_computation.19 | async-start | bytes 4718592 | tf_op jit(solution)/shard_map/reduce_scatter | solution.py:991
  251.3 3.5 copy-start.22
  260.3 5.5 copy-start.23
  263.9 4.9 collective-permute-start
  264.1 37.5 %collective-permute-start.1 = (bf16[512,1024]{0,1:T(8,128)(2,1)}, bf16[512,1024]{0,1:T(8,128)(2,1)}, u32[]{:S(2)}, u32[]{:S(2)}) collective-permute-start(bf16[512,1024]{0,1:T(8,128)(2,1)} %get-tuple-element.140), channel_id=1, source_target_pairs={{0,2},{1,3},{2,0},{3,1},{4,6},{5,7},{6,4},{7,5},{8,10},{9,11},{10,... | collective-permute-start | bytes 3145736 | tf_op jit(solution)/shard_map/ppermute | solution.py:868
  265.8 68.8 %collective-permute-start.2 = (bf16[512,1024]{0,1:T(8,128)(2,1)}, bf16[512,1024]{0,1:T(8,128)(2,1)}, u32[]{:S(2)}, u32[]{:S(2)}) collective-permute-start(bf16[512,1024]{0,1:T(8,128)(2,1)} %get-tuple-element.138), channel_id=1, source_target_pairs={{0,3},{1,2},{2,1},{3,0},{4,7},{5,6},{6,5},{7,4},{8,11},{9,10},{10,... | collective-permute-start | bytes 3145736 | tf_op jit(solution)/shard_map/ppermute | solution.py:868
  356.9 14.7 %copy-start.21 = (bf16[4,256,1024]{2,1,0:T(8,128)(2,1)S(1)}, bf16[4,256,1024]{2,1,0:T(8,128)(2,1)}, u32[]{:S(2)}) copy-start(bf16[4,256,1024]{2,1,0:T(8,128)(2,1)} %copy.163) | copy-start | bytes 6291460
  369.6 1.9 copy-start.30
  378.3 55.3 %copy-start.18 = (bf16[1,256,1024]{2,1,0:T(8,128)(2,1)S(1)}, bf16[1,256,1024]{2,1,0:T(8,128)(2,1)}, u32[]{:S(2)}) copy-start(bf16[1,256,1024]{2,1,0:T(8,128)(2,1)} %param.20) | copy-start | bytes 1572868
  378.4 169.4 %reduce-scatter.15.cloned.1.call-start = ((), (), s32[]{:S(2)}) async-start(), calls=%async_computation.22 | async-start | bytes 2359296 | tf_op jit(solution)/shard_map/reduce_scatter | solution.py:1037
  431.5 3.9 copy-start.16
  431.5 4.9 copy-start.2
  435.4 1.0 copy-start.11
  450.9 1.4 copy-start
  452.3 125.9 %reduce-scatter.27.cloned.1.call-start = ((), (), s32[]{:S(2)}) async-start(), calls=%async_computation.28 | async-start | bytes 2621440 | tf_op jit(solution)/shard_map/reduce_scatter | solution.py:1007
  461.9 12.5 %copy-start.10 = (f32[256,1024]{1,0:T(8,128)S(1)}, f32[256,1024]{1,0:T(8,128)}, u32[]{:S(2)}) copy-start(f32[256,1024]{1,0:T(8,128)} %copy-done.9) | copy-start | bytes 3145732
  461.9 174.1 %reduce-scatter.29.cloned.1.call-start = ((), (), s32[]{:S(2)}) async-start(), calls=%async_computation.29 | async-start | bytes 2621440 | tf_op jit(solution)/shard_map/reduce_scatter | solution.py:1008
  474.1 3.1 copy-start.12
  474.1 222.5 %reduce-scatter.21.cloned.1.call-start = ((), (), s32[]{:S(2)}) async-start(), calls=%async_computation.25 | async-start | bytes 7864320 | tf_op jit(solution)/shard_map/reduce_scatter | solution.py:1084
  474.4 3.6 copy-start.13
  494.5 30.4 %copy-start.4 = (bf16[2048,384]{1,0:T(8,128)(2,1)S(1)}, bf16[2048,384]{1,0:T(8,128)(2,1)}, u32[]{:S(2)}) copy-start(bf16[2048,384]{1,0:T(8,128)(2,1)} %copy-done.3) | copy-start | bytes 4718596
  494.5 227.8 %reduce-scatter.19.cloned.1.call-start = ((), (), s32[]{:S(2)}) async-start(), calls=%async_computation.24 | async-start | bytes 983040 | tf_op jit(solution)/shard_map/reduce_scatter | solution.py:1067
  524.9 18.9 %copy-start.26 = (bf16[2048,1024]{1,0:T(8,128)(2,1)S(1)}, bf16[2048,1024]{1,0:T(8,128)(2,1)}, u32[]{:S(2)}) copy-start(bf16[2048,1024]{1,0:T(8,128)(2,1)} %all-gather.16.cloned.1.call-done) | copy-start | bytes 12582916
  542.6 1.1 copy-start.5
  543.8 5.0 copy-start.27
  547.1 223.1 %all-gather.28.cloned.1.call-start = ((), (), s32[]{:S(2)}) async-start(), calls=%async_computation.21 | async-start | bytes 7864320 | tf_op jit(solution)/shard_map/all_gather | solution.py:1057
  547.7 258.5 %reduce-scatter.25.cloned.1.call-start = ((), (), s32[]{:S(2)}) async-start(), calls=%async_computation.27 | async-start | bytes 655360 | tf_op jit(solution)/shard_map/reduce_scatter | solution.py:1049
  550.0 3.3 copy-start.6
  550.0 312.9 %reduce-scatter.17.cloned.1.call-start = ((), (), s32[]{:S(2)}) async-start(), calls=%async_computation.23 | async-start | bytes 1179648 | tf_op jit(solution)/shard_map/reduce_scatter | solution.py:1044
  552.7 364.1 %reduce-scatter.13.cloned.1.call-start = ((), (), s32[]{:S(2)}) async-start(), calls=%async_computation.20 | async-start | bytes 4718592 | tf_op jit(solution)/shard_map/reduce_scatter | solution.py:1002
  555.0 82.5 %copy-start.19 = (bf16[1,256,1024]{2,1,0:T(8,128)(2,1)S(1)}, bf16[1,256,1024]{2,1,0:T(8,128)(2,1)}, u32[]{:S(2)}) copy-start(bf16[1,256,1024]{2,1,0:T(8,128)(2,1)} %param.20) | copy-start | bytes 1572868
  555.0 182.7 %all-to-all-start.2 = ((bf16[8,256,384]{1,2,0:T(8,128)(2,1)}), bf16[8,256,384]{1,2,0:T(8,128)(2,1)}, u32[]{:S(2)}, u32[]{:S(2)}) async-start(bf16[8,256,384]{1,2,0:T(8,128)(2,1)} %copy.167), calls=%async_computation.4 | async-start | bytes 3145728 | tf_op jit(solution)/shard_map/all_to_all | solution.py:1054
  559.4 425.7 %reduce-scatter.23.cloned.1.call-start = ((), (), s32[]{:S(2)}) async-start(), calls=%async_computation.26 | async-start | bytes 1769472 | tf_op jit(solution)/shard_map/reduce_scatter | solution.py:1089
  637.4 2.2 collective-permute-start.6
  637.5 9.2 collective-permute-start.7
  638.2 13.3 %collective-permute-start.8 = (bf16[512,256]{1,0:T(8,128)(2,1)S(1)}, bf16[512,256]{1,0:T(8,128)(2,1)S(1)}, u32[]{:S(2)}, u32[]{:S(2)}) collective-permute-start(bf16[512,256]{1,0:T(8,128)(2,1)S(1)} %get-tuple-element.145), channel_id=1, source_target_pairs={{0,3},{1,2},{2,1},{3,0},{4,7},{5,6},{6,5},{7,4},{8,11},{9,10},{10,... | collective-permute-start | bytes 786440 | tf_op jit(solution)/shard_map/ppermute | solution.py:868
  652.3 8.7 collective-permute-start.9
  700.2 70.0 %copy-start.15 = (bf16[1,256,1024]{2,1,0:T(8,128)(2,1)S(1)}, bf16[1,256,1024]{2,1,0:T(8,128)(2,1)}, u32[]{:S(2)}) copy-start(bf16[1,256,1024]{2,1,0:T(8,128)(2,1)} %param.18) | copy-start | bytes 1572868
  723.5 9.3 collective-permute-start.3
  724.3 8.5 collective-permute-start.4
  730.8 6.2 collective-permute-start.5
  739.2 1.2 copy-start.20
  776.5 140.3 %copy-start.8 = (f32[256,1024]{1,0:T(8,128)S(1)}, f32[256,1024]{1,0:T(8,128)}, u32[]{:S(2)}) copy-start(f32[256,1024]{1,0:T(8,128)} %copy-done.7) | copy-start | bytes 3145732
  776.5 140.3 %copy-start.25 = (f32[1024]{0:T(1024)S(1)}, f32[1024]{0:T(1024)}, u32[]{:S(2)}) copy-start(f32[1024]{0:T(1024)} %param.35) | copy-start | bytes 12292
Sparse Core Ops, SparseCore 0:
  13.8 74.6 all-gather.15
  90.6 42.8 all-gather.29
  135.1 32.1 all-gather.21
  168.7 22.5 all-gather.17
  192.7 22.5 all-gather.19
  216.8 22.5 all-gather.23
  244.2 47.7 all-gather.25
  293.9 47.8 all-gather.31
  378.5 53.0 reduce-scatter.10
  452.4 72.9 reduce-scatter.14
  527.8 50.3 reduce-scatter.26
  580.3 55.6 reduce-scatter.28
  638.7 57.8 reduce-scatter.20
  699.0 23.2 reduce-scatter.18
  723.8 46.3 all-gather.27
  773.3 21.6 reduce-scatter.24
  798.2 64.6 reduce-scatter.16
  866.5 50.3 reduce-scatter.12
  920.2 64.8 reduce-scatter.22

commit v2 on v1

--- a/solution.py
+++ b/solution.py
@@ -5,6 +5,7 @@
 import jax.numpy as jnp
 from jax import lax
 from jax.experimental import pallas as pl
+from jax.experimental.layout import Layout, with_layout_constraint
 from jax.experimental.pallas import tpu as pltpu
 from jax.sharding import Mesh
 from jax.sharding import PartitionSpec as P
@@ -539,11 +540,25 @@
 
 
 CTX = ("cz", "cy")
-GRID = ("cy", "fsdp")
+FSDP = ("fx", "fc")
+PLANE = ("fx", "fc", "cy")
+ALL = ("cz", "cy", "fx", "fc")
+ROW_BLOCK = 512
+HIDDEN_BLOCK = 256
 QBLOCK = 256
 HALF = 128
 PAIR = 2 * HEAD_DIM
 MAX_KEY_BLOCKS = 5
+
+
+def kernel_cost(microseconds):
+    return pl.CostEstimate(
+        flops=int(microseconds * 1.15e9), bytes_accessed=1 << 20, transcendentals=0
+    )
+
+
+def row_major(value):
+    return with_layout_constraint(value, Layout(tuple(range(value.ndim))))
 
 
 def doc_start_of(starts_ref, positions):
@@ -568,16 +583,26 @@
     return pl.multiple_of(jnp.where(2 * pos_block < pos_blocks, early, late), HALF)
 
 
+def slot_of(distance):
+    return (distance & 1) + 2 * ((distance >> 2) & 1) + 4 * ((distance >> 1) & 1)
+
+
+def slot_row(row, own):
+    block = row // (2 * HALF)
+    slot = slot_of(block ^ own)
+    return pl.multiple_of(slot * (2 * HALF) + row - block * (2 * HALF), HALF)
+
+
 def lane_mask(rows, head):
     lanes = lax.broadcasted_iota(jnp.int32, (rows, PAIR), 1)
     return (lanes >= head * HEAD_DIM) & (lanes < (head + 1) * HEAD_DIM)
 
 
-def to_positions(src_ref, column, dst_ref):
+def to_positions(own, src_ref, column, dst_ref):
     pos_blocks = src_ref.shape[0] // HALF
 
     def move(block, carry):
-        row = half_row(block, pos_blocks)
+        row = slot_row(half_row(block, pos_blocks), own)
         dst_ref[pl.ds(pl.multiple_of(block * HALF, HALF), HALF), :] = src_ref[
             pl.ds(row, HALF), pl.ds(column, PAIR)
         ]
@@ -586,19 +611,21 @@
     lax.fori_loop(0, pos_blocks, move, 0)
 
 
-def self_forward_kernel(starts_ref, qkv_ref, out_ref, key_ref, value_ref):
+def self_forward_kernel(starts_ref, own_ref, qkv_ref, out_ref, key_ref, value_ref):
     step = pl.program_id(0)
+    own = own_ref[0]
     pos_blocks = qkv_ref.shape[0] // HALF
 
     @pl.when(step == 0)
     def _():
-        to_positions(qkv_ref, PAIR, key_ref)
-        to_positions(qkv_ref, 2 * PAIR, value_ref)
+        to_positions(own, qkv_ref, PAIR, key_ref)
+        to_positions(own, qkv_ref, 2 * PAIR, value_ref)
 
     row_a = half_row(2 * step, pos_blocks)
     row_b = half_row(2 * step + 1, pos_blocks)
+    slot_a, slot_b = slot_row(row_a, own), slot_row(row_b, own)
     queries = jnp.concatenate(
-        [qkv_ref[pl.ds(row_a, HALF), pl.ds(0, PAIR)], qkv_ref[pl.ds(row_b, HALF), pl.ds(0, PAIR)]],
+        [qkv_ref[pl.ds(slot_a, HALF), pl.ds(0, PAIR)], qkv_ref[pl.ds(slot_b, HALF), pl.ds(0, PAIR)]],
         axis=0,
     )
     q_start = step * QBLOCK
@@ -634,22 +661,32 @@
 
 
 def self_backward_kernel(
-    starts_ref, qkv_ref, grad_ref, out_ref, key_ref, value_ref, dkey_ref, dvalue_ref
+    starts_ref,
+    own_ref,
+    qkv_ref,
+    grad_ref,
+    slot_ref,
+    key_ref,
+    value_ref,
+    dkey_ref,
+    dvalue_ref,
 ):
     step = pl.program_id(0)
+    own = own_ref[0]
     pos_blocks = qkv_ref.shape[0] // HALF
 
     @pl.when(step == 0)
     def _():
-        to_positions(qkv_ref, PAIR, key_ref)
-        to_positions(qkv_ref, 2 * PAIR, value_ref)
+        to_positions(own, qkv_ref, PAIR, key_ref)
+        to_positions(own, qkv_ref, 2 * PAIR, value_ref)
         dkey_ref[...] = jnp.zeros_like(dkey_ref)
         dvalue_ref[...] = jnp.zeros_like(dvalue_ref)
 
     row_a = half_row(2 * step, pos_blocks)
     row_b = half_row(2 * step + 1, pos_blocks)
+    slot_a, slot_b = slot_row(row_a, own), slot_row(row_b, own)
     queries = jnp.concatenate(
-        [qkv_ref[pl.ds(row_a, HALF), pl.ds(0, PAIR)], qkv_ref[pl.ds(row_b, HALF), pl.ds(0, PAIR)]],
+        [qkv_ref[pl.ds(slot_a, HALF), pl.ds(0, PAIR)], qkv_ref[pl.ds(slot_b, HALF), pl.ds(0, PAIR)]],
         axis=0,
     )
     grads = jnp.concatenate([grad_ref[pl.ds(row_a, HALF), :], grad_ref[pl.ds(row_b, HALF), :]], axis=0)
@@ -693,8 +730,8 @@
         dvalue_ref[pl.ds(k_start, width), :] += dvalue
         dq = jnp.where(lane_mask(QBLOCK, 0), dq_parts[0], dq_parts[1])
         dq = (dq * (1.0 / math.sqrt(HEAD_DIM))).astype(jnp.bfloat16)
-        out_ref[pl.ds(row_a, HALF), pl.ds(0, PAIR)] = dq[:HALF]
-        out_ref[pl.ds(row_b, HALF), pl.ds(0, PAIR)] = dq[HALF:]
+        slot_ref[pl.ds(slot_a, HALF), pl.ds(0, PAIR)] = dq[:HALF]
+        slot_ref[pl.ds(slot_b, HALF), pl.ds(0, PAIR)] = dq[HALF:]
 
     for blocks in range(1, MAX_KEY_BLOCKS + 1):
         pl.when(count == blocks)(functools.partial(compute, blocks))
@@ -702,20 +739,20 @@
     @pl.when(step == pl.num_programs(0) - 1)
     def _():
         def move(block, carry):
-            row = half_row(block, pos_blocks)
+            slot = slot_row(half_row(block, pos_blocks), own)
             place = pl.ds(pl.multiple_of(block * HALF, HALF), HALF)
-            out_ref[pl.ds(row, HALF), pl.ds(PAIR, PAIR)] = dkey_ref[place, :].astype(jnp.bfloat16)
-            out_ref[pl.ds(row, HALF), pl.ds(2 * PAIR, PAIR)] = dvalue_ref[place, :].astype(
-                jnp.bfloat16
-            )
+            dkey = dkey_ref[place, :].astype(jnp.bfloat16)
+            dvalue = dvalue_ref[place, :].astype(jnp.bfloat16)
+            slot_ref[pl.ds(slot, HALF), pl.ds(PAIR, PAIR)] = dkey
+            slot_ref[pl.ds(slot, HALF), pl.ds(2 * PAIR, PAIR)] = dvalue
             return carry
 
         lax.fori_loop(0, pos_blocks, move, 0)
 
 
 def cross_forward_kernel(q_ref, key_ref, value_ref, low_ref, high_ref, out_ref):
-    rows, width = q_ref.shape[0], key_ref.shape[0]
-    queries, keys, values = q_ref[...], key_ref[...], value_ref[...]
+    rows, width = q_ref.shape[0], key_ref.shape[1]
+    queries, keys, values = q_ref[...], key_ref[0], value_ref[0]
     k_pos = lax.broadcasted_iota(jnp.int32, (rows, width), 1)
     allowed = (k_pos >= low_ref[...]) & (k_pos < high_ref[...])
     parts = []
@@ -732,8 +769,8 @@
 
 
 def cross_backward_kernel(q_ref, key_ref, value_ref, grad_ref, low_ref, high_ref, dq_ref, dkv_ref):
-    rows, width = q_ref.shape[0], key_ref.shape[0]
-    queries, keys, values, grads = q_ref[...], key_ref[...], value_ref[...], grad_ref[...]
+    rows, width = q_ref.shape[0], key_ref.shape[1]
+    queries, keys, values, grads = q_ref[...], key_ref[0], value_ref[0], grad_ref[...]
     k_pos = lax.broadcasted_iota(jnp.int32, (width, rows), 0)
     allowed = (k_pos >= low_ref[...]) & (k_pos < high_ref[...])
     dq_parts = []
@@ -767,12 +804,13 @@
     return pltpu.CompilerParams(vmem_limit_bytes=48 * 1024 * 1024)
 
 
-def self_forward(doc_starts, qkv):
+def self_forward(doc_starts, own, qkv):
     rows = qkv.shape[0]
     return pl.pallas_call(
         self_forward_kernel,
         grid=(rows // QBLOCK,),
         in_specs=[
+            pl.BlockSpec(memory_space=pltpu.SMEM),
             pl.BlockSpec(memory_space=pltpu.SMEM),
             pl.BlockSpec((rows, 3 * PAIR), lambda step: (0, 0)),
         ],
@@ -780,18 +818,17 @@
         out_shape=jax.ShapeDtypeStruct((rows, PAIR), jnp.bfloat16),
         scratch_shapes=[pltpu.VMEM((rows, PAIR), jnp.bfloat16)] * 2,
         compiler_params=kernel_params(),
-        cost_estimate=pl.CostEstimate(
-            flops=2 * rows * 1024 * 256 * 2, bytes_accessed=rows * PAIR * 8, transcendentals=0
-        ),
-    )(doc_starts, qkv)
-
-
-def self_backward(doc_starts, qkv, grads):
+        cost_estimate=kernel_cost(1),
+    )(doc_starts, own, qkv)
+
+
+def self_backward(doc_starts, own, qkv, grads):
     rows = qkv.shape[0]
     return pl.pallas_call(
         self_backward_kernel,
         grid=(rows // QBLOCK,),
         in_specs=[
+            pl.BlockSpec(memory_space=pltpu.SMEM),
             pl.BlockSpec(memory_space=pltpu.SMEM),
             pl.BlockSpec((rows, 3 * PAIR), lambda step: (0, 0)),
             pl.BlockSpec((rows, PAIR), lambda step: (0, 0)),
@@ -801,46 +838,42 @@
         scratch_shapes=[pltpu.VMEM((rows, PAIR), jnp.bfloat16)] * 2
         + [pltpu.VMEM((rows, PAIR), jnp.float32)] * 2,
         compiler_params=kernel_params(),
-        cost_estimate=pl.CostEstimate(
-            flops=5 * rows * 1024 * 256 * 2, bytes_accessed=rows * PAIR * 14, transcendentals=0
-        ),
-    )(doc_starts, qkv, grads)
-
-
-def cross_forward(queries, kv_cross, low, high):
+        cost_estimate=kernel_cost(1),
+    )(doc_starts, own, qkv, grads)
+
+
+def cross_forward(queries, kv_cross, span_low, span_high):
     rows, features = queries.shape
     pairs = features // PAIR
-    src = kv_cross.shape[0]
+    src = kv_cross.shape[1]
     return pl.pallas_call(
         cross_forward_kernel,
         grid=(pairs,),
         in_specs=[
             pl.BlockSpec((rows, PAIR), lambda p: (0, p)),
-            pl.BlockSpec((src, PAIR), lambda p: (0, p)),
-            pl.BlockSpec((src, PAIR), lambda p: (0, p + pairs)),
+            pl.BlockSpec((1, src, PAIR), lambda p: (p // 2, 0, p % 2)),
+            pl.BlockSpec((1, src, PAIR), lambda p: (p // 2 + pairs // 2, 0, p % 2)),
             pl.BlockSpec((rows, 1), lambda p: (0, 0)),
             pl.BlockSpec((rows, 1), lambda p: (0, 0)),
         ],
         out_specs=pl.BlockSpec((rows, PAIR), lambda p: (0, p)),
         out_shape=jax.ShapeDtypeStruct((rows, features), jnp.bfloat16),
         compiler_params=kernel_params(),
-        cost_estimate=pl.CostEstimate(
-            flops=4 * rows * src * features, bytes_accessed=3 << 20, transcendentals=0
-        ),
-    )(queries, kv_cross, kv_cross, low[:, None], high[:, None])
-
-
-def cross_backward(queries, kv_cross, grads, low, high):
+        cost_estimate=kernel_cost(1),
+    )(queries, kv_cross, kv_cross, span_low[:, None], span_high[:, None])
+
+
+def cross_backward(queries, kv_cross, grads, span_low, span_high):
     rows, features = queries.shape
     pairs = features // PAIR
-    src = kv_cross.shape[0]
+    src = kv_cross.shape[1]
     return pl.pallas_call(
         cross_backward_kernel,
         grid=(pairs,),
         in_specs=[
             pl.BlockSpec((rows, PAIR), lambda p: (0, p)),
-            pl.BlockSpec((src, PAIR), lambda p: (0, p)),
-            pl.BlockSpec((src, PAIR), lambda p: (0, p + pairs)),
+            pl.BlockSpec((1, src, PAIR), lambda p: (p // 2, 0, p % 2)),
+            pl.BlockSpec((1, src, PAIR), lambda p: (p // 2 + pairs // 2, 0, p % 2)),
             pl.BlockSpec((rows, PAIR), lambda p: (0, p)),
             pl.BlockSpec((1, rows), lambda p: (0, 0)),
             pl.BlockSpec((1, rows), lambda p: (0, 0)),
@@ -854,24 +887,160 @@
             jax.ShapeDtypeStruct((2, pairs, src, PAIR), jnp.bfloat16),
         ],
         compiler_params=kernel_params(),
-        cost_estimate=pl.CostEstimate(
-            flops=10 * rows * src * features, bytes_accessed=6 << 20, transcendentals=0
-        ),
-    )(queries, kv_cross, kv_cross, grads, low[None, :], high[None, :])
-
-
-def swap_fsdp(pieces):
-    own = lax.axis_index("fsdp")
-    count = pieces.shape[0]
-    whole = pieces
-    for distance in range(1, count):
-        moved = lax.ppermute(
-            lax.dynamic_index_in_dim(pieces, own ^ distance, 0, keepdims=False),
-            "fsdp",
-            [(i, i ^ distance) for i in range(count)],
-        )
-        whole = lax.dynamic_update_index_in_dim(whole, moved, own ^ distance, 0)
-    return whole
+        cost_estimate=kernel_cost(1),
+    )(queries, kv_cross, kv_cross, grads, span_low[None, :], span_high[None, :])
+
+
+def mlp_kernel(act_ref, grad_ref, up_ref, down_ref, bias_ref, gelu_ref, pre_ref, out_ref, sum_ref):
+    @pl.when(pl.program_id(0) == 0)
+    def _():
+        sum_ref[...] = jnp.zeros_like(sum_ref)
+
+    act, grad = act_ref[...], grad_ref[...]
+    total = jnp.zeros(out_ref.shape, jnp.float32)
+    for begin in range(0, up_ref.shape[1], HIDDEN_BLOCK):
+        place = pl.ds(begin, HIDDEN_BLOCK)
+        pre = jnp.dot(act, up_ref[:, place], preferred_element_type=jnp.float32) + bias_ref[:, place]
+        square = pre * pre
+        tangent = jnp.tanh(GELU_C * (pre + GELU_A * pre * square))
+        half = 0.5 * (1.0 + tangent)
+        gelu_ref[:, place] = (pre * half).astype(jnp.bfloat16)
+        slope = half + 0.5 * pre * (1.0 - tangent * tangent) * (
+            GELU_C + (3.0 * GELU_A * GELU_C) * square
+        )
+        back = lax.dot_general(
+            grad, down_ref[place, :], CONTRACT_COLS, preferred_element_type=jnp.float32
+        )
+        pre_grad = (back * slope).astype(jnp.bfloat16)
+        pre_ref[:, place] = pre_grad
+        sum_ref[:, place] += jnp.sum(pre_grad.astype(jnp.float32), axis=0, keepdims=True)
+        total = total + lax.dot_general(
+            pre_grad, up_ref[:, place], CONTRACT_COLS, preferred_element_type=jnp.float32
+        )
+    out_ref[...] = total.astype(jnp.bfloat16)
+
+
+def mlp_forward_back(act, grad, up_own, down_own, bias_own):
+    rows, features = act.shape
+    hidden = up_own.shape[1]
+    return pl.pallas_call(
+        mlp_kernel,
+        grid=(rows // ROW_BLOCK,),
+        in_specs=[
+            pl.BlockSpec((ROW_BLOCK, features), lambda step: (step, 0)),
+            pl.BlockSpec((ROW_BLOCK, features), lambda step: (step, 0)),
+            pl.BlockSpec((features, hidden), lambda step: (0, 0)),
+            pl.BlockSpec((hidden, features), lambda step: (0, 0)),
+            pl.BlockSpec((1, hidden), lambda step: (0, 0)),
+        ],
+        out_specs=[
+            pl.BlockSpec((ROW_BLOCK, hidden), lambda step: (step, 0)),
+            pl.BlockSpec((ROW_BLOCK, hidden), lambda step: (step, 0)),
+            pl.BlockSpec((ROW_BLOCK, features), lambda step: (step, 0)),
+            pl.BlockSpec((1, hidden), lambda step: (0, 0)),
+        ],
+        out_shape=[
+            jax.ShapeDtypeStruct((rows, hidden), jnp.bfloat16),
+            jax.ShapeDtypeStruct((rows, hidden), jnp.bfloat16),
+            jax.ShapeDtypeStruct((rows, features), jnp.bfloat16),
+            jax.ShapeDtypeStruct((1, hidden), jnp.float32),
+        ],
+        compiler_params=kernel_params(),
+        cost_estimate=kernel_cost(1),
+    )(act, grad, up_own, down_own, bias_own)
+
+
+def outer_kernel(left_ref, right_ref, left_two_ref, right_two_ref, out_ref, total_ref):
+    step = pl.program_id(0)
+    half = pl.num_programs(0) // 2
+
+    def add(left, right):
+        total_ref[...] += lax.dot_general(
+            left[...], right[...], CONTRACT_ROWS, preferred_element_type=jnp.float32
+        )
+
+    @pl.when(step == 0)
+    def _():
+        total_ref[...] = jnp.zeros_like(total_ref)
+
+    pl.when(step < half)(lambda: add(left_ref, right_ref))
+    pl.when(step >= half)(lambda: add(left_two_ref, right_two_ref))
+
+    @pl.when(step == 2 * half - 1)
+    def _():
+        out_ref[...] = total_ref[...].astype(out_ref.dtype)
+
+
+def outer_pair(left, right, left_two, right_two):
+    rows, width = left.shape
+    columns = right.shape[1]
+    half = rows // ROW_BLOCK
+    first = lambda step: (jnp.minimum(step, half - 1), 0)
+    second = lambda step: (jnp.maximum(step - half, 0), 0)
+    return pl.pallas_call(
+        outer_kernel,
+        grid=(2 * half,),
+        in_specs=[
+            pl.BlockSpec((ROW_BLOCK, width), first),
+            pl.BlockSpec((ROW_BLOCK, columns), first),
+            pl.BlockSpec((ROW_BLOCK, width), second),
+            pl.BlockSpec((ROW_BLOCK, columns), second),
+        ],
+        out_specs=pl.BlockSpec((width, columns), lambda step: (0, 0)),
+        out_shape=jax.ShapeDtypeStruct((width, columns), jnp.bfloat16),
+        scratch_shapes=[pltpu.VMEM((width, columns), jnp.float32)],
+        compiler_params=kernel_params(),
+        cost_estimate=kernel_cost(1),
+    )(left, right, left_two, right_two)
+
+
+def square_grads_kernel(core_ref, *refs):
+    step = pl.program_id(0)
+    side, x = step // 2, step % 2
+    core = jnp.where(side == 0, 1 - core_ref[0], core_ref[0])
+    pairs, (send_ref, keep_ref) = refs[:-2], refs[-2:]
+    n_y, n_z, _, rows, width = send_ref.shape[1:]
+    begin = pl.multiple_of((2 * x + core) * rows, rows)
+
+    def compute(out_ref):
+        for which in range(len(pairs) // 2):
+            grad = lax.dot_general(
+                pairs[2 * which][:, pl.ds(begin, rows)],
+                pairs[2 * which + 1][...],
+                CONTRACT_ROWS,
+                preferred_element_type=jnp.float32,
+            ).astype(jnp.bfloat16)
+            for y in range(n_y):
+                for z in range(n_z):
+                    source = (z * n_y + y) * width
+                    out_ref[0, y, z, which] = grad[:, source : source + width]
+
+    pl.when(side == 0)(lambda: compute(send_ref))
+    pl.when(side == 1)(lambda: compute(keep_ref))
+
+
+def square_grads(core, pairs, n_y, n_z):
+    flat = [array for pair in pairs for array in pair]
+    tokens, features = flat[0].shape
+    rows = features // 4
+    block = (1, n_y, n_z, len(pairs), rows, features // (n_y * n_z))
+    shape = jax.ShapeDtypeStruct((2,) + block[1:], jnp.bfloat16)
+    return pl.pallas_call(
+        square_grads_kernel,
+        grid=(4,),
+        in_specs=[pl.BlockSpec(memory_space=pltpu.SMEM)]
+        + [pl.BlockSpec((tokens, features), lambda step: (0, 0))] * len(flat),
+        out_specs=[
+            pl.BlockSpec(block, lambda step: (jnp.minimum(step, 1), 0, 0, 0, 0, 0)),
+            pl.BlockSpec(block, lambda step: (jnp.maximum(step - 2, 0), 0, 0, 0, 0, 0)),
+        ],
+        out_shape=[shape, shape],
+        compiler_params=kernel_params(),
+        cost_estimate=kernel_cost(15),
+    )(core, *flat)
+
+
+tie = lax.optimization_barrier
 
 
 def low(value):
@@ -880,6 +1049,177 @@
 
 def wide(value):
     return value.astype(jnp.float32)
+
+
+def plus(left, right):
+    return low(wide(left) + wide(right))
+
+
+def over(axis, distance, value):
+    count = lax.axis_size(axis)
+    return lax.ppermute(value, axis, [(i, i ^ distance) for i in range(count)])
+
+
+def over_core(value):
+    return over("fc", 1, value)
+
+
+def over_x(value):
+    return over("fx", 1, value)
+
+
+def over_y(value):
+    return over("cy", 1, value)
+
+
+def trade_places(value):
+    n_z, n_y, n_f = lax.axis_size("cz"), lax.axis_size("cy"), lax.axis_size(FSDP)
+    pairs = [
+        ((z * n_y + y) * n_f + f, (f * n_y + y) * n_f + z)
+        for z in range(n_z)
+        for y in range(n_y)
+        for f in range(n_f)
+    ]
+    return lax.ppermute(value, ALL, pairs)
+
+
+def at(value, index, axis):
+    return lax.dynamic_index_in_dim(value, index, axis, keepdims=False)
+
+
+def pack_kernel(index_ref, *refs):
+    begin = 0
+    for ref in refs[:-1]:
+        size = ref.shape[1]
+        refs[-1][:, begin : begin + size] = ref[...]
+        begin += size
+
+
+def swap_columns(w_qkv, w_cross_kv, w_up):
+    own, me_y, n_y = lax.axis_index(FSDP), lax.axis_index("cy"), lax.axis_size("cy")
+    rows = w_up.shape[0]
+    count = lax.axis_size(FSDP) * n_y
+    owners = jnp.stack([(own ^ distance) * n_y + me_y for distance in (2, 3, 1, 0)])
+    sizes = [PAIR] * 3 + [w_cross_kv.shape[1] // count, w_up.shape[1] // count]
+    pieces = pl.pallas_call(
+        pack_kernel,
+        grid_spec=pltpu.PrefetchScalarGridSpec(
+            num_scalar_prefetch=1,
+            grid=(4,),
+            in_specs=[
+                pl.BlockSpec(
+                    (rows, PAIR), lambda step, index, part=part: (0, part * count + index[step])
+                )
+                for part in range(3)
+            ]
+            + [pl.BlockSpec((rows, size), lambda step, index: (0, index[step])) for size in sizes[3:]],
+            out_specs=pl.BlockSpec((rows, sum(sizes)), lambda step, index: (step, 0)),
+        ),
+        out_shape=jax.ShapeDtypeStruct((4 * rows, sum(sizes)), w_up.dtype),
+        compiler_params=kernel_params(),
+        cost_estimate=kernel_cost(1),
+    )(owners.astype(jnp.int32), w_qkv, w_qkv, w_qkv, w_cross_kv, w_up)
+    from_x = over_x(pieces[: 2 * rows])
+    from_core = over_core(
+        row_major(jnp.concatenate([pieces[2 * rows : 3 * rows], from_x[rows:]], axis=0))
+    )
+    return [pieces[3 * rows :], from_core[:rows], from_x[:rows], from_core[rows:]]
+
+
+def rows_in_order(pieces, begin, size):
+    own = lax.axis_index(FSDP)
+    rows = pieces[0].shape[0]
+    whole = jnp.zeros((len(pieces) * rows, size), pieces[0].dtype)
+    for distance, piece in enumerate(pieces):
+        whole = lax.dynamic_update_slice_in_dim(
+            whole, piece[:, begin : begin + size], (own ^ distance) * rows, 0
+        )
+    return whole
+
+
+def gather_rows(shard):
+    own, me_y = lax.axis_index(FSDP), lax.axis_index("cy")
+    rows, columns = shard.shape
+    half = rows // 2
+    from_x = over_x(lax.dynamic_slice_in_dim(shard, me_y * half, half, 0))
+    from_y = over_y(from_x)
+    both = jnp.concatenate(
+        [shard, jnp.where(me_y == 0, from_x, from_y), jnp.where(me_y == 0, from_y, from_x)], axis=0
+    )
+    from_core = over_core(row_major(both))
+    whole = jnp.zeros((4 * rows, columns), shard.dtype)
+    for distance, piece in (
+        (0, both[:rows]),
+        (2, both[rows:]),
+        (1, from_core[:rows]),
+        (3, from_core[rows:]),
+    ):
+        whole = lax.dynamic_update_slice_in_dim(whole, piece, (own ^ distance) * rows, 0)
+    return whole
+
+
+def gather_rest(block, from_y, from_x):
+    half = block.shape[0] // 2
+    top = over_x(from_y[:half])
+    bottom = over_y(from_x[half:])
+    mine = jnp.concatenate([block, from_y, from_x, top, bottom], axis=0)
+    return mine, over_core(mine)
+
+
+def gather_plane(block):
+    return gather_rest(block, over_y(block), over_x(block))
+
+
+def scatter_plane(mine, theirs, fill=(None, None, None)):
+    rows = mine.shape[0] // 4
+    half = rows // 2
+    done = []
+
+    def beside(received, work):
+        if work is None:
+            return received
+        received, result = tie((received, work()))
+        done.append(result)
+        return received
+
+    total = plus(mine, beside(over_core(theirs), fill[0]))
+    own, for_y, for_x, diag = (total[i * rows : (i + 1) * rows] for i in range(4))
+    top, bottom = beside((over_x(diag[:half]), over_y(diag[half:])), fill[1])
+    for_y = jnp.concatenate([plus(for_y[:half], top), for_y[half:]], axis=0)
+    for_x = jnp.concatenate([for_x[:half], plus(for_x[half:], bottom)], axis=0)
+    from_y, from_x = beside((over_y(for_y), over_x(for_x)), fill[2])
+    return wide(own) + wide(from_y) + wide(from_x), done
+
+
+def sum_everywhere(value, event):
+    value = later(value, event)
+    for step in (over_core, over_x, over_y):
+        value = value + step(value)
+    for distance in (1, 2):
+        value = value + over("cz", distance, value)
+    return value
+
+
+def after(value, *events):
+    return lax.optimization_barrier((value,) + events)[0]
+
+
+def later(value, event):
+    scalar = event[(0,) * event.ndim]
+    nothing = jnp.where(scalar != scalar, scalar, jnp.zeros_like(scalar))
+    return value + nothing.astype(value.dtype)
+
+
+def scatter_bits(value, axes=(0, 1, 2)):
+    me_f, me_y = lax.axis_index(FSDP), lax.axis_index("cy")
+    me_x, me_core = me_f // 2, me_f % 2
+    axis_x, axis_core, axis_y = axes
+    value = plus(at(value, me_core, axis_core), over_core(at(value, 1 - me_core, axis_core)))
+    axis_x -= axis_x > axis_core
+    axis_y -= axis_y > axis_core
+    value = plus(at(value, me_x, axis_x), over_x(at(value, 1 - me_x, axis_x)))
+    axis_y -= axis_y > axis_x
+    return plus(at(value, me_y, axis_y), over_y(at(value, 1 - me_y, axis_y)))
 
 
 def planned_device(
@@ -904,120 +1244,118 @@
 ):
     q_scale = 1.0 / math.sqrt(HEAD_DIM)
     rows, features = tokens.shape[1:]
-    n_z, n_y, n_f = lax.axis_size("cz"), lax.axis_size("cy"), lax.axis_size("fsdp")
+    src_own = encoded.shape[1]
+    n_z, n_y, n_f = lax.axis_size("cz"), lax.axis_size("cy"), lax.axis_size(FSDP)
     n_ctx = n_z * n_y
-    me_y, me_f = lax.axis_index("cy"), lax.axis_index("fsdp")
-    me_c = lax.axis_index(CTX)
-    shard = w_up.shape[0]
-    hidden = w_up.shape[1]
-    slab = hidden // (n_z * n_y * n_f)
-
-    own_rows = me_c * rows + jnp.arange(rows, dtype=jnp.int32)
+    me_y, me_f = lax.axis_index("cy"), lax.axis_index(FSDP)
+    own = me_f * n_y + me_y
+    shard, hidden = w_up.shape
+    slab = hidden // n_ctx
+    width = features // n_ctx
+    column = 2 * features // n_ctx
+
+    moved = trade_places(jnp.concatenate([tokens[0], encoded[0]], axis=0))
+    tok_low, enc_low = moved[:rows], moved[rows:]
+    lengths = trade_places(jnp.concatenate([doc_lengths, src_lengths], axis=0))
+    head_w = swap_columns(w_qkv, w_cross_kv, w_up)
+    tok_low, enc_low, lengths = tie((tok_low, enc_low, lengths))
+    qkv_own = rows_in_order(head_w, 0, 3 * PAIR)
+    kv_own = rows_in_order(head_w, 3 * PAIR, column)
+    up_own = rows_in_order(head_w, 3 * PAIR + column, slab)
+    square = gather_rows(jnp.concatenate([w_self_out, w_cross_q, w_cross_out], axis=1))
+
+    own_rows = own * rows + jnp.arange(rows, dtype=jnp.int32)
     tok_pos = stream_position(own_rows, rows, n_ctx)
-    lengths_row = doc_lengths[0]
-    doc_starts = jnp.cumsum(lengths_row) - lengths_row
+    doc_starts = jnp.cumsum(lengths[0]) - lengths[0]
     tok_doc = doc_index(doc_starts, tok_pos)
-    src_row = src_lengths[0]
-    src_ends = jnp.cumsum(src_row)
-    span_low = pick_doc(src_ends - src_row, tok_doc)
+    src_ends = jnp.cumsum(lengths[1])
+    span_low = pick_doc(src_ends - lengths[1], tok_doc)
     span_high = pick_doc(src_ends, tok_doc)
-
-    qkv_cols = lax.dynamic_index_in_dim(
-        w_qkv.reshape(shard, 3, n_ctx, PAIR), me_c, 2, keepdims=False
-    ).reshape(shard, 3 * PAIR)
-    qkv_own = lax.all_gather(qkv_cols, "fsdp", axis=0, tiled=True)
-
-    tok_f32 = wide(tokens[0])
+    own_index = own.astype(jnp.int32)[None]
+
+    tok_f32 = wide(tok_low)
     ln_one, normed_one, inverse_one = layer_norm(tok_f32, norm_gain[0], norm_bias[0])
     act_one = low(ln_one)
-    act_one_all = lax.all_gather(act_one, CTX, axis=0, tiled=True)
+    from_y, from_x = over_y(act_one), over_x(act_one)
+    enc_all = lax.all_gather(enc_low, PLANE, axis=0, tiled=True)
+    act_mine, act_theirs = gather_rest(act_one, from_y, from_x)
+    down_grad_low = trade_places(grad_out[0])
+    grad_all = lax.all_gather(down_grad_low, PLANE, axis=0, tiled=False)
     full_self_out, full_cross_q, full_cross_out = (
-        lax.all_gather(w, "fsdp", axis=0, tiled=True) for w in (w_self_out, w_cross_q, w_cross_out)
-    )
-    enc_all = lax.all_gather(encoded[0], CTX, axis=0, tiled=True)
-    full_cross_kv = lax.all_gather(w_cross_kv, "fsdp", axis=0, tiled=True)
-
-    up_pieces = jnp.moveaxis(
-        lax.dynamic_index_in_dim(
-            w_up.reshape(shard, n_z, n_y, n_f, slab), me_y, 2, keepdims=False
-        ),
-        2,
-        0,
-    ).reshape(n_f, shard, n_z * slab)
-    down_pieces = lax.dynamic_index_in_dim(
-        w_down.reshape(n_y, n_f, slab, features), me_y, 0, keepdims=False
-    )
-    mlp_w = swap_fsdp(jnp.concatenate([up_pieces, down_pieces], axis=1))
-    up_own = mlp_w[:, :shard].reshape(n_f * shard, n_z * slab)
-    down_own = mlp_w[:, shard:].reshape(n_f * slab, features)
-
-    head_bias = lax.dynamic_slice_in_dim(self_bias, me_c * PAIR, PAIR, 1)
-    projected = plain_dot(act_one_all, qkv_own)
-    qkv_heads = low(
-        jnp.concatenate(
-            [
-                (projected[:, :PAIR] + head_bias[0]) * q_scale,
-                projected[:, PAIR : 2 * PAIR],
-                projected[:, 2 * PAIR :] + head_bias[1],
-            ],
-            axis=1,
-        )
-    )
-    att_heads = self_forward(doc_starts, qkv_heads)
-    att_self = lax.all_to_all(att_heads, CTX, 0, 1, tiled=True)
+        square[:, i * features : (i + 1) * features] for i in range(3)
+    )
+
+    head_bias = lax.dynamic_slice_in_dim(self_bias, own * PAIR, PAIR, 1)
+    qkv_bias = jnp.concatenate([head_bias[0], jnp.zeros_like(head_bias[0]), head_bias[1]])
+    qkv_factor = jnp.concatenate([jnp.full((PAIR,), q_scale), jnp.ones((2 * PAIR,))])
+
+    def project(acts):
+        return low((plain_dot(acts, qkv_own) + qkv_bias) * qkv_factor.astype(jnp.float32))
+
+    qkv_heads = jnp.concatenate([project(act_mine), project(act_theirs)], axis=0)
+    kv_bias = jnp.concatenate([jnp.zeros((features,), jnp.float32), cross_bias[1]])
+    kv_columns = low(
+        plain_dot(enc_all, kv_own) + lax.dynamic_slice_in_dim(kv_bias, own * column, column, 0)
+    )
+    kv_cross = lax.all_gather(after(kv_columns, grad_all), PLANE, axis=0, tiled=False)
+    down_own = lax.dynamic_slice_in_dim(w_down, me_y * slab, slab, 0)
+    att_heads = self_forward(doc_starts, own_index, qkv_heads)
+    att_heads, down_own, up_own = tie((att_heads, down_own, up_own))
+    att_self = lax.all_to_all(att_heads, PLANE, 0, 1, tiled=True)
+    order = (0, 1, 4, 5, 2, 3, 6, 7)
+    grad_mine = jnp.concatenate([at(grad_all, own ^ k, 0) for k in order[:4]], axis=0)
+    grad_theirs = jnp.concatenate([at(grad_all, own ^ k, 0) for k in order[4:]], axis=0)
+
     hidden_one = tok_f32 + plain_dot(att_self, full_self_out) + self_bias[2]
-
     ln_two, normed_two, inverse_two = layer_norm(hidden_one, norm_gain[1], norm_bias[1])
     act_two = low(ln_two)
     q_cross = low((plain_dot(act_two, full_cross_q) + cross_bias[0]) * q_scale)
-    kv_bias = jnp.concatenate([jnp.zeros((features,), jnp.float32), cross_bias[1]])
-    kv_cross = low(plain_dot(enc_all, full_cross_kv) + kv_bias)
     att_cross = cross_forward(q_cross, kv_cross, span_low, span_high)
     hidden_two = hidden_one + plain_dot(att_cross, full_cross_out) + cross_bias[2]
 
     ln_three, normed_three, inverse_three = layer_norm(hidden_two, norm_gain[2], norm_bias[2])
-    act_three = lax.all_gather(low(ln_three), GRID, axis=0, tiled=True)
-    grad_all = lax.all_gather(grad_out[0], GRID, axis=0, tiled=True)
-    up_bias_own = lax.dynamic_index_in_dim(
-        lax.dynamic_index_in_dim(up_bias.reshape(n_z, n_y, n_f, slab), me_f, 2, keepdims=False),
-        me_y,
-        1,
-        keepdims=False,
-    ).reshape(-1)
-    pre_act = plain_dot(act_three, up_own) + up_bias_own
-    gelu_low = low(gelu_value(pre_act))
-    slope = gelu_slope(pre_act)
-    pre_grad = low(times_transpose(grad_all, down_own) * slope)
-    act_grad = lax.psum_scatter(
-        low(times_transpose(pre_grad, up_own)), GRID, scatter_dimension=0, tiled=True
-    )
-    down_part = low(plain_dot(gelu_low, down_own))
-
-    upstream = wide(grad_out[0])
-    norm_in_three, gain_grad_three, shift_grad_three = norm_back(
-        wide(act_grad), normed_three, inverse_three, norm_gain[2]
-    )
-    grad_two = upstream + norm_in_three
-    down_part, grad_two = lax.optimization_barrier((down_part, grad_two))
-    mlp_out = lax.psum_scatter(down_part, GRID, scatter_dimension=0, tiled=True)
-    layer_out = low(hidden_two + wide(mlp_out) + down_bias)
-
-    up_grad = low(outer_rows(pre_grad, act_three))
-    down_grad = low(outer_rows(grad_all, gelu_low))
+    three_mine, three_theirs = gather_plane(low(ln_three))
+    bias_own = lax.dynamic_slice_in_dim(up_bias, own * slab, slab, 0).reshape(1, -1)
+    gelu_theirs, pre_theirs, part_theirs, sum_theirs = mlp_forward_back(
+        three_theirs, grad_theirs, up_own, down_own, bias_own
+    )
+    gelu_mine, pre_mine, part_mine, sum_mine = mlp_forward_back(
+        three_mine, grad_mine, up_own, down_own, bias_own
+    )
+
+    part_mine, three_mine, three_theirs, grad_mine, grad_theirs, act_mine, act_theirs = tie(
+        (part_mine, three_mine, three_theirs, grad_mine, grad_theirs, act_mine, act_theirs)
+    )
+    act_grad, (up_grad, down_grad, out_sent) = scatter_plane(
+        part_mine,
+        part_theirs,
+        (
+            lambda: outer_pair(three_mine, pre_mine, three_theirs, pre_theirs),
+            lambda: outer_pair(grad_mine, gelu_mine, grad_theirs, gelu_theirs),
+            lambda: low(plain_dot(gelu_theirs, down_own)),
+        ),
+    )
     up_grad = lax.psum_scatter(up_grad, "cz", scatter_dimension=0, tiled=True)
     down_grad = lax.psum_scatter(down_grad, "cz", scatter_dimension=0, tiled=True)
-    up_bias_grad = jnp.sum(wide(pre_grad), axis=0)
+    out_mine = low(plain_dot(gelu_mine, down_own))
+
+    upstream = wide(down_grad_low)
     grad_down_bias = jnp.sum(upstream, axis=0)
-
+    norm_in_three, gain_grad_three, shift_grad_three = norm_back(
+        act_grad, normed_three, inverse_three, norm_gain[2]
+    )
+    grad_two = upstream + norm_in_three
     cross_grad_low = low(grad_two)
-    grad_w_cross_out = low(outer_rows(att_cross, cross_grad_low))
     cross_out_bias_grad = jnp.sum(wide(cross_grad_low), axis=0)
     cross_att_grad = low(times_transpose(cross_grad_low, full_cross_out))
     cross_v_bias_grad = jnp.sum(wide(cross_att_grad), axis=0)
+
+    up_bias_grad = (sum_mine + sum_theirs)[0]
+
+    me_x, me_core = me_f // 2, me_f % 2
     cross_q_low, cross_kv_part = cross_backward(
         q_cross, kv_cross, cross_att_grad, span_low, span_high
     )
-    grad_w_cross_q = low(outer_rows(act_two, cross_q_low))
     cross_q_bias_grad = jnp.sum(wide(cross_q_low), axis=0)
     norm_in_two, gain_grad_two, shift_grad_two = norm_back(
         times_transpose(cross_q_low, full_cross_q), normed_two, inverse_two, norm_gain[1]
@@ -1026,88 +1364,126 @@
     self_grad_low = low(grad_one)
     self_att_grad = low(times_transpose(self_grad_low, full_self_out))
     self_v_bias_grad = jnp.sum(wide(self_att_grad), axis=0)
-    att_grad_heads = lax.all_to_all(self_att_grad, CTX, 1, 0, tiled=True)
-    proj_grad_heads = self_backward(doc_starts, qkv_heads, att_grad_heads)
-
-    grad_w_self_out = low(outer_rows(att_self, self_grad_low))
+    kv_part = cross_kv_part.reshape(2, 2, 2, 2, enc_all.shape[0], PAIR)
+    kv_other = over_core(at(kv_part, 1 - me_core, 1))
+    self_att_grad, up_grad, kv_other = tie((self_att_grad, up_grad, kv_other))
+    att_grad_heads = lax.all_to_all(self_att_grad, PLANE, 1, 0, tiled=True)
+    kv_part = plus(at(kv_part, me_core, 1), kv_other)
+    kv_other = over_x(at(kv_part, 1 - me_x, 0))
+
+    send, keep = square_grads(
+        me_core.astype(jnp.int32)[None],
+        (
+            (att_self, after(self_grad_low, self_att_grad)),
+            (act_two, cross_q_low),
+            (att_cross, cross_grad_low),
+        ),
+        n_y,
+        n_z,
+    )
     self_out_bias_grad = jnp.sum(wide(self_grad_low), axis=0)
-
-    blocks = 2 * features // PAIR
-    src_rows = enc_all.shape[0]
-    cross_kv_grad = lax.psum_scatter(
-        cross_kv_part.reshape(blocks, src_rows, PAIR), CTX, scatter_dimension=0, tiled=True
-    )
-    per = blocks // n_ctx
-    cross_kv_grad = jnp.concatenate([cross_kv_grad[i] for i in range(per)], axis=1)
-    kv_w_own = lax.dynamic_slice_in_dim(full_cross_kv, me_c * per * PAIR, per * PAIR, 1)
+    three = plus(keep, over_core(send))
+    out_sum = plus(out_mine, over_core(after(out_sent, self_att_grad)))
+    att_grad_heads, kv_other, three, out_sum = tie((att_grad_heads, kv_other, three, out_sum))
+    kv_part = plus(at(kv_part, me_x, 0), kv_other)
+    kv_other = over_y(at(kv_part, 1 - me_y, 0))
+    left, right = three[:, :, : n_z // 2], three[:, :, n_z // 2 :]
+    left_other = over_x(at(left, 1 - me_x, 0))
+    right_other = over_y(at(right, 1 - me_y, 1))
+    out_own, out_y, out_x, out_diag = (out_sum[i * rows : (i + 1) * rows] for i in range(4))
+    half_rows = rows // 2
+    out_top, out_bottom = over_x(out_diag[:half_rows]), over_y(out_diag[half_rows:])
+
+    proj_grad = self_backward(doc_starts, own_index, qkv_heads, att_grad_heads)
+    half = proj_grad.shape[0] // 2
+
+    def lane_blocks(value):
+        return [
+            value[:, i : i + PAIR].reshape(n_z, 1, shard, PAIR)
+            for i in range(0, value.shape[1], PAIR)
+        ]
+
+    def project_back():
+        weight = outer_rows(act_mine, proj_grad[:half]) + outer_rows(act_theirs, proj_grad[half:])
+        sums = jnp.sum(wide(proj_grad), axis=0)[None]
+        shift = jnp.sum(wide(qkv_own) * sums, axis=1)
+        gain = jnp.sum(wide(qkv_own) * weight, axis=1) - norm_bias[0] * shift
+        return row_major(low(weight)), sums[0], gain / norm_gain[0], shift
+
+    act_grad, ((qkv_grad, proj_sums, gain_grad_one, shift_grad_one),) = scatter_plane(
+        low(times_transpose(proj_grad[:half], qkv_own)),
+        low(times_transpose(proj_grad[half:], qkv_own)),
+        (project_back, None, None),
+    )
+    down_cols = later(down_grad, act_grad).reshape(n_y, width, slab)
+    other = over_y(at(down_cols, 1 - me_y, 0))
+    mine = at(down_cols, me_y, 0)
+
+    left = later(plus(at(left, me_x, 0), left_other), act_grad)
+    right = later(plus(at(right, me_y, 1), right_other), act_grad)
+    left, left_send = at(left, me_y, 0), at(left, 1 - me_y, 0)
+    right, right_send = at(right, me_x, 0), at(right, 1 - me_x, 0)
+    out_y = jnp.concatenate([plus(out_y[:half_rows], out_top), out_y[half_rows:]], axis=0)
+    out_x = jnp.concatenate([out_x[:half_rows], plus(out_x[half_rows:], out_bottom)], axis=0)
+    out_y, out_x = later(out_y, act_grad), later(out_x, act_grad)
+    mlp_out = wide(out_own) + wide(over_y(out_y)) + wide(over_x(out_x))
+    layer_out = trade_places(low(hidden_two + mlp_out + down_bias))
+    self_q_bias_grad = proj_sums[:PAIR]
+    cross_kv_grad = plus(at(kv_part, me_y, 0), kv_other)
+    cross_kv_grad = jnp.concatenate([cross_kv_grad[0], cross_kv_grad[1]], axis=1)
     grad_encoded = wide(
-        lax.psum_scatter(
-            low(times_transpose(cross_kv_grad, kv_w_own)), CTX, scatter_dimension=0, tiled=True
-        )
-    )
-    grad_w_cross_kv = wide(
-        lax.psum_scatter(
-            low(outer_rows(enc_all, cross_kv_grad)), "fsdp", scatter_dimension=0, tiled=True
-        )
-    )
-
-    proj_grad = lax.all_to_all(
-        proj_grad_heads.reshape(n_ctx, rows, 3 * PAIR), CTX, 0, 0, tiled=False
-    )
-    full_qkv = lax.all_gather(w_qkv, "fsdp", axis=0, tiled=True)
-    proj_grad = jnp.transpose(proj_grad.reshape(n_ctx, rows, 3, PAIR), (1, 2, 0, 3)).reshape(
-        rows, 3 * features
-    )
-    self_q_bias_grad = jnp.sum(wide(proj_grad[:, :features]), axis=0)
-    norm_in_one, gain_grad_one, shift_grad_one = norm_back(
-        times_transpose(proj_grad, full_qkv), normed_one, inverse_one, norm_gain[0]
-    )
-    grad_tokens = grad_one + norm_in_one
-
-    qkv_grad = lax.psum_scatter(
-        low(outer_rows(act_one_all, proj_grad_heads)), "fsdp", scatter_dimension=0, tiled=True
-    ).reshape(shard, 3, PAIR)
+        trade_places(
+            scatter_bits(
+                after(low(times_transpose(cross_kv_grad, kv_own)), act_grad).reshape(
+                    2, 2, 2, src_own, features
+                )
+            )
+        )
+    )
+    cross_kv_grad = low(outer_rows(enc_all, cross_kv_grad))
+    rest = jnp.concatenate(lane_blocks(cross_kv_grad) + lane_blocks(qkv_grad), axis=1)
+    rest = lax.psum_scatter(row_major(rest), "cz", scatter_dimension=0, tiled=False)
+    three = jnp.concatenate(
+        [
+            later(plus(left, over_y(left_send)), rest),
+            later(plus(right, over_x(right_send)), rest),
+        ],
+        axis=0,
+    )
+    three = wide(lax.psum_scatter(row_major(three), "cz", scatter_dimension=0, tiled=False))
+    kv_blocks = trade_places(rest[:2])
+    grad_w_cross_kv = wide(jnp.concatenate([kv_blocks[0], kv_blocks[1]], axis=1))
+    qkv_grad = rest[2:]
+
+    norm_in_one, _, _ = norm_back(act_grad, normed_one, inverse_one, norm_gain[0])
+    grad_tokens = low(grad_one + norm_in_one)
+    grad_w_up = wide(trade_places(later(up_grad, proj_grad)))
+    grad_tokens = wide(trade_places(grad_tokens))
+
+    down_halves = jnp.stack([jnp.where(me_y == 0, mine, other), jnp.where(me_y == 0, other, mine)])
+    grad_w_down = wide(jnp.transpose(down_halves, (0, 2, 1)).reshape(n_y * slab, width))
+
     qkv_blocks = []
     inverse_of_three = pow(3, -1, n_ctx)
     for slot in range(3):
-        pairs = [((3 * dest + slot) % n_ctx, dest) for dest in range(n_ctx)]
-        dest = (inverse_of_three * (me_c - slot)) % n_ctx
-        part = (3 * dest + slot) // n_ctx
-        qkv_blocks.append(
-            lax.ppermute(
-                lax.dynamic_index_in_dim(qkv_grad, part, 1, keepdims=False), CTX, pairs
-            )
-        )
+        pairs = []
+        for dest in range(n_ctx):
+            source = (3 * dest + slot) % n_ctx
+            for z in range(n_z):
+                pairs.append(
+                    ((z * n_y + source % n_y) * n_f + source // n_y, dest * n_f + z)
+                )
+        part = (3 * ((inverse_of_three * (own - slot)) % n_ctx) + slot) // n_ctx
+        qkv_blocks.append(lax.ppermute(at(qkv_grad, part, 0), ALL, pairs))
     grad_w_qkv = wide(jnp.concatenate(qkv_blocks, axis=1))
 
-    three = jnp.concatenate([grad_w_self_out, grad_w_cross_q, grad_w_cross_out], axis=1)
-    three = lax.psum_scatter(three, "fsdp", scatter_dimension=0, tiled=True)
-    width = features // n_ctx
-    three = jnp.transpose(three.reshape(shard, 3, n_ctx, width), (2, 1, 0, 3)).reshape(
-        n_ctx * 3 * shard, width
-    )
-    three = wide(lax.psum_scatter(three, CTX, scatter_dimension=0, tiled=True)).reshape(
-        3, shard, width
-    )
-
-    mlp_pieces = jnp.concatenate(
-        [
-            jnp.moveaxis(up_grad.reshape(slab, n_f, shard), 1, 0),
-            jnp.moveaxis(down_grad.reshape(features // n_z, n_f, slab), 1, 0),
-        ],
-        axis=1,
-    )
-    mlp_pieces = swap_fsdp(mlp_pieces)
-    grad_w_up = wide(jnp.transpose(mlp_pieces[:, :slab].reshape(n_f * slab, shard)))
-    down_cols = mlp_pieces[:, slab:].reshape(n_f, n_y, width, slab)
-    other = lax.ppermute(
-        lax.dynamic_index_in_dim(down_cols, 1 - me_y, 1, keepdims=False), "cy", [(0, 1), (1, 0)]
-    )
-    mine = lax.dynamic_index_in_dim(down_cols, me_y, 1, keepdims=False)
-    down_halves = jnp.stack([jnp.where(me_y == 0, mine, other), jnp.where(me_y == 0, other, mine)])
-    grad_w_down = wide(jnp.transpose(down_halves, (0, 1, 3, 2)).reshape(n_y * n_f * slab, width))
-
-    vectors = jnp.stack(
+    def placed(part):
+        whole = jnp.zeros((n_ctx * part.shape[0],), jnp.float32)
+        return lax.dynamic_update_slice_in_dim(whole, part, own * part.shape[0], 0).reshape(
+            -1, features
+        )
+
+    level = jnp.stack(
         [
             gain_grad_one,
             gain_grad_two,
@@ -1115,23 +1491,18 @@
             shift_grad_one,
             shift_grad_two,
             shift_grad_three,
-            self_q_bias_grad,
             self_v_bias_grad,
             self_out_bias_grad,
             cross_q_bias_grad,
             cross_v_bias_grad,
             cross_out_bias_grad,
             grad_down_bias,
-            up_bias_grad,
         ]
     )
-    gathered = lax.all_gather(vectors, GRID, axis=0, tiled=False)
-    up_rows = gathered[:, -1]
-    level = jnp.concatenate([jnp.sum(gathered[:, :-1], axis=0), up_rows], axis=0)
-    level = jnp.sum(lax.all_gather(level, "cz", axis=0, tiled=False), axis=0)
-    grad_up_bias = jnp.transpose(
-        level[13:].reshape(n_y, n_f, n_z, slab), (2, 0, 1, 3)
-    ).reshape(hidden)
+    level = sum_everywhere(
+        jnp.concatenate([level, placed(self_q_bias_grad), placed(up_bias_grad)], axis=0), act_grad
+    )
+    grad_up_bias = level[13:].reshape(hidden)
 
     return (
         layer_out[None],
@@ -1140,25 +1511,25 @@
         level[0:3],
         level[3:6],
         grad_w_qkv,
-        level[6:9],
+        jnp.concatenate([level[12:13], level[6:8]], axis=0),
         three[0],
         three[1],
         grad_w_cross_kv,
-        level[9:12],
+        level[8:11],
         three[2],
         grad_w_up,
         grad_up_bias,
         grad_w_down,
-        level[12],
+        level[11],
     )
 
 
 def planned_solution(mesh):
     n_ctx, n_f = mesh.shape["ctx"], mesh.shape["fsdp"]
-    split = Mesh(mesh.devices.reshape(n_ctx // 2, 2, n_f), ("cz", "cy", "fsdp"))
-    token = P("fsdp", CTX, None)
-    row = P("fsdp", None)
-    owned = P("fsdp", CTX)
+    split = Mesh(mesh.devices.reshape(n_ctx // 2, 2, n_f // 2, 2), ALL)
+    token = P(FSDP, CTX, None)
+    row = P(FSDP, None)
+    owned = P(FSDP, CTX)
     return jax.shard_map(
         planned_device,
         mesh=split,

time: 1000 us -> 602 us (0.60)
  waiting for transfers between devices: 617 us -> 159 us
  starting transfers between devices: 36 us -> 97.4 us
  blocking collectives: 60.9 us -> 0 us
  Pallas kernels: 53.3 us -> 104 us
  matrix products: 104 us -> 54.9 us
  local copies, waits for them, and re-layouts: 67 us -> 96.3 us
  other arithmetic: 40.3 us -> 63.8 us
    reduce_scatter x8 -> x2, waiting for transfers between devices: 270 us -> 0.02 us  [the longest x1 0.02 us: planned_device(): lax.psum_scatter(row_major(rest), 'cz', scatter_dimension=0, tiled=False)]
    all_gather x9 -> x3, waiting for transfers between devices: 182 us -> 0.04 us  [the longest x1 0.02 us: planned_device(): lax.all_gather(after(kv_columns, grad_all), PLANE, axis=0, tiled=False)]
    ppermute x10 -> x58, starting transfers between devices: 14.4 us -> 87.8 us  [the longest x8 46.5 us: trade_places(): return lax.ppermute(value, ALL, pairs)]
    ppermute x10 -> x58, waiting for transfers between devices: 84.8 us -> 152 us  [the longest x47 92.1 us: over(): return lax.ppermute(value, axis, [(i, i ^ distance) for i in range(count)])]
    reduce_scatter x1, waiting for transfers between devices: 56.8 us -> 0.02 us  [planned_device(): lax.psum_scatter(down_grad, 'cz', scatter_dimension=0, tiled=True)]
    pallas_call x0 -> x6, Pallas kernels: none -> 51.5 us  [the longest x2 25.7 us: mlp_forward_back(): pl.pallas_call(mlp_kernel, grid=(rows // ROW_BLOCK,), in_specs=[pl.BlockS...]
    all_gather x3 -> x0, blocking collectives: 33.1 us -> none  [the longest x1 14.8 us: planned_device(): level = jnp.sum(lax.all_gather(level, 'cz', axis=0, tiled=False), axis=0)]
    all_to_all x1 -> x0, blocking collectives: 27.8 us -> none  [planned_device(): att_grad_heads = lax.all_to_all(self_att_grad, CTX, 1, 0, tiled=True)]
  transfers between devices with their start and end apart: 31 -> 67, of which waited for: 21 -> 24; matrix products, arithmetic and copies ran while one was open for 17% -> 30% of each run, Pallas kernels for 4% -> 13%
where the time goes in v2:
time: 602 us; the launch traced here: 597 us
  waiting for transfers between devices  159 us (26%)
  Pallas kernels  104 us (17%)
  starting transfers between devices  97.4 us (16%)
  local copies, waits for them, and re-layouts  96.3 us (16%)
  other arithmetic  63.8 us (11%)
  matrix products  54.9 us (9%)
  between operations  21.7 us (4%)
    ppermute x47, waiting for transfers between devices, over(): return lax.ppermute(value, axis, [(i, i ^ distance) for i in range(count)])  92.1 us
    ppermute x8, waiting for transfers between devices, trade_places(): return lax.ppermute(value, ALL, pairs)  58.9 us
    ppermute x8, starting transfers between devices, trade_places(): return lax.ppermute(value, ALL, pairs)  46.5 us
    ppermute x47, starting transfers between devices, over(): return lax.ppermute(value, axis, [(i, i ^ distance) for i in range(count)])  32.5 us
    unnamed x153, local copies, waits for them, and re-layouts  28.2 us
    dot_general x8, matrix products, plain_dot(): return jnp.dot(left, right, preferred_element_type=jnp.float32)  27.2 us
    pallas_call x2, Pallas kernels, mlp_forward_back(): pl.pallas_call(mlp_kernel, grid=(rows // ROW_BLOCK,), in_specs=[pl.BlockS...  25.7 us
    convert_element_type x15, other arithmetic, low(): return value.astype(jnp.bfloat16)  20.7 us
  transfers between devices with their start and end apart: 67, of which 24 were waited for; matrix products, arithmetic and copies ran while one was open for 30% of the time, Pallas kernels for 13%

profile of v2, /device:TPU:2, one launch (start us, length us, event | category | flops | bytes accessed | tf_op | source)
XLA Modules:
  0.0 596.8 jit_solution(11615883003866380598)
XLA Ops:
  16.1 5.9 collective-permute-start
  24.1 3.3 shard_map.297
  30.7 5.7 collective-permute-start.12
  37.1 26.2 %collective-permute-done = bf16[320,1024]{1,0:T(8,128)(2,1)S(1)} collective-permute-done((bf16[320,1024]{1,0:T(8,128)(2,1)}, bf16[320,1024]{1,0:T(8,128)(2,1)S(1)}, u32[]{:S(2)}, u32[]{:S(2)}) %collective-permute-start) | collective-permute-done | bytes 655392 | tf_op jit(solution)/shard_map/ppermute | solution.py:1083
  73.4 3.4 broadcast_in_dim.102
  76.7 2.6 constant_dynamic-update-slice_fusion.19
  79.7 3.2 constant_dynamic-slice_fusion.1.down_ref
  87.3 6.2 %collective-permute-done.2 = bf16[256,1024]{1,0:T(8,128)(2,1)S(1)} collective-permute-done((bf16[256,1024]{1,0:T(8,128)(2,1)S(1)}, bf16[256,1024]{1,0:T(8,128)(2,1)S(1)}, u32[]{:S(2)}, u32[]{:S(2)}) %collective-permute-start.2) | collective-permute-done | bytes 524320 | tf_op jit(solution)/shard_map/ppermute | solution.py:1060
  93.6 24.1 %collective-permute-done.3 = bf16[256,1024]{1,0:T(8,128)(2,1)S(1)} collective-permute-done((bf16[256,1024]{1,0:T(8,128)(2,1)S(1)}, bf16[256,1024]{1,0:T(8,128)(2,1)S(1)}, u32[]{:S(2)}, u32[]{:S(2)}) %collective-permute-start.3) | collective-permute-done | bytes 524320 | tf_op jit(solution)/shard_map/ppermute | solution.py:1060
  123.5 3.3 collective-permute-done.5
  128.8 3.0 pad_maximum_fusion
  143.0 2.5 fusion.48
  145.5 3.0 multiply_convert_fusion.1
  148.6 3.0 multiply_convert_fusion
  151.8 11.8 %shard_map.298 = bf16[2048,128]{1,0:T(8,128)(2,1)} custom-call(s32[8]{0:T(128)S(1)} %bitcast_subtract_fusion.2.starts_ref, s32[1]{0:T(128)} %bitcast.5.own_ref, bf16[2048,384]{1,0:T(8,128)(2,1)S(1)} %pad_maximum_fusion.4.qkv_ref), custom_call_target="tpu_custom_call" | custom-call | flops 1150000000 | bytes 1048576 | tf_op jit(solution)/shard_map/pallas_call | solution.py:809
  163.7 5.3 all-to-all-start
  169.0 2.7 slice_dynamic-update-slice_fusion.1
  171.7 2.6 slice_dynamic-update-slice_fusion
  174.3 6.5 %all-to-all-done = bf16[8,256,128]{2,1,0:T(8,128)(2,1)S(1)} async-done(((bf16[8,256,128]{2,1,0:T(8,128)(2,1)}), bf16[8,256,128]{2,1,0:T(8,128)(2,1)S(1)}, u32[]{:S(2)}, u32[]{:S(2)}) %all-to-all-start) | async-done | bytes 524320 | tf_op jit(solution)/shard_map/all_to_all | solution.py:1304
  180.9 2.6 fusion.93
  188.0 9.9 %shard_map.299.refs_4_ = bf16[256,1024]{1,0:T(8,128)(2,1)S(1)} custom-call(bf16[256,1024]{1,0:T(8,128)(2,1)S(1)} %fusion.34.q_ref, bf16[8,512,256]{2,1,0:T(8,128)(2,1)S(1)} %bitcast.238, bf16[8,512,256]{2,1,0:T(8,128)(2,1)S(1)} %bitcast.239, s32[256,1]{1,0:T(8,128)S(1)} %copy.71.low_ref, s32[256,1]{1,0:T(8,128)S(1)} %copy.72.high_ref), custom_call_target="tpu_custom_call" | custom-call | flops 1150000000 | bytes 1048576 | tf_op jit(solution)/shard_map/pallas_call | solution.py:849
  197.9 2.6 fusion.94
  204.4 10.1 %collective-permute-done.13 = bf16[256,1024]{1,0:T(8,128)(2,1)S(1)} collective-permute-done((bf16[256,1024]{1,0:T(8,128)(2,1)S(1)}, bf16[256,1024]{1,0:T(8,128)(2,1)S(1)}, u32[]{:S(2)}, u32[]{:S(2)}) %collective-permute-start.13) | collective-permute-done | bytes 524320 | tf_op jit(solution)/shard_map/ppermute | solution.py:1060
  217.3 4.3 collective-permute-done.15
  223.1 2.6 dynamic-slice_bitcast_fusion.12
  225.7 2.3 pad_maximum_fusion.1
  228.0 12.8 %shard_map.301 = (bf16[1024,1024]{1,0:T(8,128)(2,1)S(1)}, bf16[1024,1024]{1,0:T(8,128)(2,1)S(1)}, bf16[1024,1024]{1,0:T(8,128)(2,1)}, f32[1,1024]{1,0:T(1,128)S(1)}) custom-call(bf16[1024,1024]{1,0:T(8,128)(2,1)} %collective-permute-done.17.act_ref.left_two_ref, bf16[1024,1024]{1,0:T(8,128)(2,1)} %get-tuple-element.82.grad_ref.left_two_ref, ...), custom_call_target="tpu_custom_call" | custom-call | flops 1150000000 | bytes 1048576 | tf_op jit(solution)/shard_map/pallas_call | solution.py:926
  243.9 12.9 %shard_map.300 = (bf16[1024,1024]{1,0:T(8,128)(2,1)S(1)}, bf16[1024,1024]{1,0:T(8,128)(2,1)S(1)}, bf16[1024,1024]{1,0:T(8,128)(2,1)}, f32[1,1024]{1,0:T(1,128)S(1)}) custom-call(bf16[1024,1024]{1,0:T(8,128)(2,1)} %copy-done.6, bf16[1024,1024]{1,0:T(8,128)(2,1)} %get-tuple-element.80.grad_ref.left_ref, ...), custom_call_target="tpu_custom_call" | custom-call | flops 1150000000 | bytes 1048576 | tf_op jit(solution)/shard_map/pallas_call | solution.py:926
  259.5 8.0 %shard_map.302 = bf16[1024,1024]{1,0:T(8,128)(2,1)S(1)} custom-call(bf16[1024,1024]{1,0:T(8,128)(2,1)S(1)} %copy-done.7, bf16[1024,1024]{1,0:T(8,128)(2,1)} %copy-done.14, bf16[1024,1024]{1,0:T(8,128)(2,1)} %collective-permute-done.17.act_ref.left_two_ref, bf16[1024,1024]{1,0:T(8,128)(2,1)} %copy-done.13), custom_call_target="tpu_custom_call" | custom-call | flops 1150000000 | bytes 1048576 | tf_op jit(solution)/shard_map/pallas_call | solution.py:980
  268.8 2.5 add_convert_fusion.3
  276.7 9.1 %shard_map.303 = bf16[1024,1024]{1,0:T(8,128)(2,1)} custom-call(bf16[1024,1024]{1,0:T(8,128)(2,1)S(1)} %copy-done.2, bf16[1024,1024]{1,0:T(8,128)(2,1)} %copy-done.9, bf16[1024,1024]{1,0:T(8,128)(2,1)} %get-tuple-element.82.grad_ref.left_two_ref, bf16[1024,1024]{1,0:T(8,128)(2,1)} %copy-done.11), custom_call_target="tpu_custom_call" | custom-call | flops 1150000000 | bytes 1048576 | tf_op jit(solution)/shard_map/pallas_call | solution.py:980
  290.6 5.6 convolution_convert_fusion.1
  296.1 5.7 collective-permute-done.21
  304.3 2.3 convert_reduce_fusion.3
  306.7 3.1 convert_reduce_fusion.4
  309.8 14.5 %shard_map.304 = (bf16[256,1024]{1,0:T(8,128)(2,1)S(1)}, bf16[2,8,512,128]{3,2,1,0:T(8,128)(2,1)S(1)}) custom-call(bf16[256,1024]{1,0:T(8,128)(2,1)S(1)} %fusion.34.q_ref, bf16[8,512,256]{2,1,0:T(8,128)(2,1)S(1)} %bitcast.240, bf16[8,512,256]{2,1,0:T(8,128)(2,1)S(1)} %bitcast.241, bf16[256,1024]{1,0:T(8,128)(2,1)S(1)} %get-tuple-element.217.grad_ref, ...), custom_call_target="tpu_custom_call" | custom-call | flops 1150000000 | bytes 1048576 | tf_op jit(solution)/shard_map/pallas_call | solution.py:870
  326.3 3.2 multiply_reduce_fusion.1
  331.5 3.8 convert_reduce_fusion.7
  335.3 5.3 shard_map.305
  340.6 3.9 copy.75
  346.9 3.9 all-to-all-start.1
  354.9 5.6 add_convert_fusion.2
  360.4 4.9 add_convert_fusion
  365.3 4.0 collective-permute-done.24
  369.3 16.1 %shard_map.306 = bf16[2048,384]{1,0:T(8,128)(2,1)S(1)} custom-call(s32[8]{0:T(128)S(1)} %bitcast_subtract_fusion.2.starts_ref, s32[1]{0:T(128)} %bitcast.5.own_ref, bf16[2048,384]{1,0:T(8,128)(2,1)S(1)} %copy-done.17, bf16[2048,128]{1,0:T(8,128)(2,1)S(1)} %bitcast.244), custom_call_target="tpu_custom_call" | custom-call | flops 1150000000 | bytes 1048576 | tf_op jit(solution)/shard_map/pallas_call | solution.py:827
  385.4 3.7 convolution_convert_fusion
  389.5 3.9 fusion.67
  397.4 3.0 fusion.63
  404.7 4.0 fusion.14
  415.8 11.5 %collective-permute-start.56 = (bf16[256,1024]{1,0:T(8,128)(2,1)S(1)}, bf16[256,1024]{1,0:T(8,128)(2,1)S(1)}, u32[]{:S(2)}, u32[]{:S(2)}) collective-permute-start(bf16[256,1024]{1,0:T(8,128)(2,1)S(1)} %broadcast_add_fusion), channel_id=1, source_target_pairs={{0,0},{1,8},{2,16},{3,24},{4,4},{5,12},{6,20},{7,28},{8,1},{9,9},{... | collective-permute-start | bytes 1572872 | tf_op jit(solution)/shard_map/ppermute | solution.py:1083
  428.7 2.5 convolution_convert_fusion.2
  432.5 2.5 add_convert_fusion.1
  436.6 13.4 %collective-permute-done.56 = bf16[256,1024]{1,0:T(8,128)(2,1)S(1)} collective-permute-done((bf16[256,1024]{1,0:T(8,128)(2,1)S(1)}, bf16[256,1024]{1,0:T(8,128)(2,1)S(1)}, u32[]{:S(2)}, u32[]{:S(2)}) %collective-permute-start.56) | collective-permute-done | bytes 524320 | tf_op jit(solution)/shard_map/ppermute | solution.py:1083
  458.4 3.6 collective-permute-done.32
  474.9 12.4 %collective-permute-start.37 = (bf16[256,1024]{1,0:T(8,128)(2,1)}, bf16[256,1024]{1,0:T(8,128)(2,1)}, u32[]{:S(2)}, u32[]{:S(2)}) collective-permute-start(bf16[256,1024]{1,0:T(8,128)(2,1)} %fusion.55), channel_id=1, source_target_pairs={{0,0},{1,8},{2,16},{3,24},{4,4},{5,12},{6,20},{7,28},{8,1},{9,9},{... | collective-permute-start | bytes 1572872 | tf_op jit(solution)/shard_map/ppermute | solution.py:1083
  494.7 7.0 %collective-permute-done.44 = f32[21,1024]{1,0:T(8,128)S(1)} collective-permute-done((f32[21,1024]{1,0:T(8,128)S(1)}, f32[21,1024]{1,0:T(8,128)S(1)}, u32[]{:S(2)}, u32[]{:S(2)}) %collective-permute-start.44) | collective-permute-done | bytes 86048 | tf_op jit(solution)/shard_map/ppermute | solution.py:1060
  503.5 2.8 collective-permute-done.45
  506.5 5.1 collective-permute-done.46
  514.1 5.9 collective-permute-done.47
  531.5 5.3 collective-permute-done.40
  548.4 5.2 collective-permute-start.42
  557.2 5.3 collective-permute-start.48
  562.5 14.4 %collective-permute-done.42 = bf16[64,1024]{1,0:T(8,128)(2,1)S(1)} collective-permute-done((bf16[64,1024]{1,0:T(8,128)(2,1)S(1)}, bf16[64,1024]{1,0:T(8,128)(2,1)S(1)}, u32[]{:S(2)}, u32[]{:S(2)}) %collective-permute-start.42) | collective-permute-done | bytes 131104 | tf_op jit(solution)/shard_map/ppermute | solution.py:1083
  581.5 4.9 collective-permute-done.55
  (431 shorter events, 172.5 us)
Async XLA Ops:
  7.2 135.9 %all-gather.6.cloned.1.call-start = ((), (), s32[]{:S(2)}) async-start(), calls=%async_computation.6 | async-start | bytes 1179648 | tf_op jit(solution)/shard_map/all_gather | solution.py:1280
  14.2 72.1 %collective-permute-start.9 = (bf16[128,3072]{1,0:T(8,128)(2,1)}, bf16[128,3072]{1,0:T(8,128)(2,1)}, u32[]{:S(2)}, u32[]{:S(2)}) collective-permute-start(bf16[128,3072]{1,0:T(8,128)(2,1)} %constant_dynamic-slice_fusion), channel_id=1, source_target_pairs={{0,2},{2,0},{1,3},{3,1},{4,6},{6,4},{5,7},{7,5},{8,10},{10,8},{9,1... | collective-permute-start | bytes 2359304 | tf_op jit(solution)/shard_map/ppermute | solution.py:1060
  16.1 47.1 %collective-permute-start = (bf16[320,1024]{1,0:T(8,128)(2,1)}, bf16[320,1024]{1,0:T(8,128)(2,1)S(1)}, u32[]{:S(2)}, u32[]{:S(2)}) collective-permute-start(bf16[320,1024]{1,0:T(8,128)(2,1)} %pad_maximum_fusion.6), channel_id=1, source_target_pairs={{0,0},{1,8},{2,16},{3,24},{4,4},{5,12},{6,20},{7,28},{8,1},{9,9},{... | collective-permute-start | bytes 1966088 | tf_op jit(solution)/shard_map/ppermute | solution.py:1083
  22.1 42.7 %collective-permute-start.1 = (s32[2,8]{1,0:T(2,128)S(1)}, s32[2,8]{1,0:T(2,128)S(1)}, u32[]{:S(2)}, u32[]{:S(2)}) collective-permute-start(s32[2,8]{1,0:T(2,128)S(1)} %pad_add_fusion), channel_id=1, source_target_pairs={{0,0},{1,8},{2,16},{3,24},{4,4},{5,12},{6,20},{7,28},{8,1},{9,9},{... | collective-permute-start | bytes 200 | tf_op jit(solution)/shard_map/ppermute | solution.py:1083
  30.7 90.3 %collective-permute-start.6 = (bf16[512,1664]{1,0:T(8,128)(2,1)}, bf16[512,1664]{1,0:T(8,128)(2,1)}, u32[]{:S(2)}, u32[]{:S(2)}) collective-permute-start(bf16[512,1664]{1,0:T(8,128)(2,1)} %slice.434), channel_id=1, source_target_pairs={{0,2},{2,0},{1,3},{3,1},{4,6},{6,4},{5,7},{7,5},{8,10},{10,8},{9,1... | collective-permute-start | bytes 5111816 | tf_op jit(solution)/shard_map/ppermute | solution.py:1060
  30.7 48.7 %collective-permute-start.12 = (bf16[256,1024]{1,0:T(8,128)(2,1)}, bf16[256,1024]{1,0:T(8,128)(2,1)}, u32[]{:S(2)}, u32[]{:S(2)}) collective-permute-start(bf16[256,1024]{1,0:T(8,128)(2,1)} %bitcast.20), channel_id=1, source_target_pairs={{0,0},{1,8},{2,16},{3,24},{4,4},{5,12},{6,20},{7,28},{8,1},{9,9},{... | collective-permute-start | bytes 1572872 | tf_op jit(solution)/shard_map/ppermute | solution.py:1083
  64.8 83.8 %all-gather.8.cloned.1.call-start = ((), (), s32[]{:S(2)}) async-start(), calls=%async_computation.11 | async-start | bytes 4718592 | tf_op jit(solution)/shard_map/all_gather | solution.py:1283
  79.4 106.9 %all-gather.10.cloned.1.call-start = ((), (), s32[]{:S(2)}) async-start(), calls=%async_computation.12 | async-start | bytes 2359296 | tf_op jit(solution)/shard_map/all_gather | solution.py:1300
  84.3 9.2 %collective-permute-start.2 = (bf16[256,1024]{1,0:T(8,128)(2,1)S(1)}, bf16[256,1024]{1,0:T(8,128)(2,1)S(1)}, u32[]{:S(2)}, u32[]{:S(2)}) collective-permute-start(bf16[256,1024]{1,0:T(8,128)(2,1)S(1)} %get-tuple-element.138), channel_id=1, source_target_pairs={{0,4},{4,0},{1,5},{5,1},{2,6},{6,2},{3,7},{7,3},{8,12},{12,8},{9,1... | collective-permute-start | bytes 1572872 | tf_op jit(solution)/shard_map/ppermute | solution.py:1060
  85.9 31.9 %collective-permute-start.3 = (bf16[256,1024]{1,0:T(8,128)(2,1)S(1)}, bf16[256,1024]{1,0:T(8,128)(2,1)S(1)}, u32[]{:S(2)}, u32[]{:S(2)}) collective-permute-start(bf16[256,1024]{1,0:T(8,128)(2,1)S(1)} %get-tuple-element.138), channel_id=1, source_target_pairs={{0,2},{2,0},{1,3},{3,1},{4,6},{6,4},{5,7},{7,5},{8,10},{10,8},{9,1... | collective-permute-start | bytes 1572872 | tf_op jit(solution)/shard_map/ppermute | solution.py:1060
  86.3 41.2 %collective-permute-start.10 = (bf16[128,3072]{1,0:T(8,128)(2,1)}, bf16[128,3072]{1,0:T(8,128)(2,1)S(1)}, u32[]{:S(2)}, u32[]{:S(2)}) collective-permute-start(bf16[128,3072]{1,0:T(8,128)(2,1)} %collective-permute-done.9), channel_id=1, source_target_pairs={{0,4},{4,0},{1,5},{5,1},{2,6},{6,2},{3,7},{7,3},{8,12},{12,8},{9,1... | collective-permute-start | bytes 2359304 | tf_op jit(solution)/shard_map/ppermute | solution.py:1060
  93.5 29.2 %collective-permute-start.4 = (bf16[128,1024]{1,0:T(8,128)(2,1)S(1)}, bf16[128,1024]{1,0:T(8,128)(2,1)S(1)}, u32[]{:S(2)}, u32[]{:S(2)}) collective-permute-start(bf16[128,1024]{1,0:T(8,128)(2,1)S(1)} %slice.430), channel_id=1, source_target_pairs={{0,2},{2,0},{1,3},{3,1},{4,6},{6,4},{5,7},{7,5},{8,10},{10,8},{9,1... | collective-permute-start | bytes 786440 | tf_op jit(solution)/shard_map/ppermute | solution.py:1060
  117.7 9.0 %collective-permute-start.5 = (bf16[128,1024]{1,0:T(8,128)(2,1)S(1)}, bf16[128,1024]{1,0:T(8,128)(2,1)S(1)}, u32[]{:S(2)}, u32[]{:S(2)}) collective-permute-start(bf16[128,1024]{1,0:T(8,128)(2,1)S(1)} %slice.431), channel_id=1, source_target_pairs={{0,4},{4,0},{1,5},{5,1},{2,6},{6,2},{3,7},{7,3},{8,12},{12,8},{9,1... | collective-permute-start | bytes 786440 | tf_op jit(solution)/shard_map/ppermute | solution.py:1060
  122.6 10.9 %collective-permute-start.7 = (bf16[512,1664]{1,0:T(8,128)(2,1)S(1)}, bf16[512,1664]{1,0:T(8,128)(2,1)S(1)}, u32[]{:S(2)}, u32[]{:S(2)}) collective-permute-start(bf16[512,1664]{1,0:T(8,128)(2,1)S(1)} %pad_maximum_fusion.3), channel_id=1, source_target_pairs={{0,1},{1,0},{2,3},{3,2},{4,5},{5,4},{6,7},{7,6},{8,9},{9,8},{10,11... | collective-permute-start | bytes 5111816 | tf_op jit(solution)/shard_map/ppermute | solution.py:1060
  127.5 21.1 %collective-permute-start.8 = (bf16[1024,1024]{1,0:T(8,128)(2,1)}, bf16[1024,1024]{1,0:T(8,128)(2,1)}, u32[]{:S(2)}, u32[]{:S(2)}) collective-permute-start(bf16[1024,1024]{1,0:T(8,128)(2,1)} %constant_dynamic-update-slice_fusion), channel_id=1, source_target_pairs={{0,1},{1,0},{2,3},{3,2},{4,5},{5,4},{6,7},{7,6},{8,9},{9,8},{10,11... | collective-permute-start | bytes 6291464 | tf_op jit(solution)/shard_map/ppermute | solution.py:1060
  131.7 37.2 %collective-permute-start.11 = (bf16[512,3072]{1,0:T(8,128)(2,1)}, bf16[512,3072]{1,0:T(8,128)(2,1)}, u32[]{:S(2)}, u32[]{:S(2)}) collective-permute-start(bf16[512,3072]{1,0:T(8,128)(2,1)} %pad_maximum_fusion), channel_id=1, source_target_pairs={{0,1},{1,0},{2,3},{3,2},{4,5},{5,4},{6,7},{7,6},{8,9},{9,8},{10,11... | collective-permute-start | bytes 9437192 | tf_op jit(solution)/shard_map/ppermute | solution.py:1060
  163.7 17.2 %all-to-all-start = ((bf16[8,256,128]{2,1,0:T(8,128)(2,1)}), bf16[8,256,128]{2,1,0:T(8,128)(2,1)S(1)}, u32[]{:S(2)}, u32[]{:S(2)}) async-start(bf16[8,256,128]{2,1,0:T(8,128)(2,1)} %bitcast.13), calls=%async_computation | async-start | bytes 1048576 | tf_op jit(solution)/shard_map/all_to_all | solution.py:1304
  169.0 166.3 %reduce-scatter.5.cloned.1.call-start = ((), (), s32[]{:S(2)}) async-start(), calls=%async_computation.7 | async-start | bytes 2621440 | tf_op jit(solution)/shard_map/reduce_scatter | solution.py:1338
  201.0 13.6 %collective-permute-start.13 = (bf16[256,1024]{1,0:T(8,128)(2,1)S(1)}, bf16[256,1024]{1,0:T(8,128)(2,1)S(1)}, u32[]{:S(2)}, u32[]{:S(2)}) collective-permute-start(bf16[256,1024]{1,0:T(8,128)(2,1)S(1)} %get-tuple-element.136), channel_id=1, source_target_pairs={{0,4},{4,0},{1,5},{5,1},{2,6},{6,2},{3,7},{7,3},{8,12},{12,8},{9,1... | collective-permute-start | bytes 1572872 | tf_op jit(solution)/shard_map/ppermute | solution.py:1060
  203.0 12.7 %collective-permute-start.14 = (bf16[256,1024]{1,0:T(8,128)(2,1)S(1)}, bf16[256,1024]{1,0:T(8,128)(2,1)S(1)}, u32[]{:S(2)}, u32[]{:S(2)}) collective-permute-start(bf16[256,1024]{1,0:T(8,128)(2,1)S(1)} %get-tuple-element.136), channel_id=1, source_target_pairs={{0,2},{2,0},{1,3},{3,1},{4,6},{6,4},{5,7},{7,5},{8,10},{10,8},{9,1... | collective-permute-start | bytes 1572872 | tf_op jit(solution)/shard_map/ppermute | solution.py:1060
  214.6 7.0 %collective-permute-start.15 = (bf16[128,1024]{1,0:T(8,128)(2,1)S(1)}, bf16[128,1024]{1,0:T(8,128)(2,1)S(1)}, u32[]{:S(2)}, u32[]{:S(2)}) collective-permute-start(bf16[128,1024]{1,0:T(8,128)(2,1)S(1)} %slice.452), channel_id=1, source_target_pairs={{0,2},{2,0},{1,3},{3,1},{4,6},{6,4},{5,7},{7,5},{8,10},{10,8},{9,1... | collective-permute-start | bytes 786440 | tf_op jit(solution)/shard_map/ppermute | solution.py:1060
  215.7 6.4 %collective-permute-start.16 = (bf16[128,1024]{1,0:T(8,128)(2,1)S(1)}, bf16[128,1024]{1,0:T(8,128)(2,1)S(1)}, u32[]{:S(2)}, u32[]{:S(2)}) collective-permute-start(bf16[128,1024]{1,0:T(8,128)(2,1)S(1)} %slice.453), channel_id=1, source_target_pairs={{0,4},{4,0},{1,5},{5,1},{2,6},{6,2},{3,7},{7,3},{8,12},{12,8},{9,1... | collective-permute-start | bytes 786440 | tf_op jit(solution)/shard_map/ppermute | solution.py:1060
  222.2 5.8 collective-permute-start.17
  243.5 25.3 %collective-permute-start.18 = (bf16[1024,1024]{1,0:T(8,128)(2,1)}, bf16[1024,1024]{1,0:T(8,128)(2,1)S(1)}, u32[]{:S(2)}, u32[]{:S(2)}) collective-permute-start(bf16[1024,1024]{1,0:T(8,128)(2,1)} %get-tuple-element.74), channel_id=1, source_target_pairs={{0,1},{1,0},{2,3},{3,2},{4,5},{5,4},{6,7},{7,6},{8,9},{9,8},{10,11... | collective-permute-start | bytes 6291464 | tf_op jit(solution)/shard_map/ppermute | solution.py:1060
  273.6 12.2 %collective-permute-start.19 = (bf16[128,1024]{1,0:T(8,128)(2,1)}, bf16[128,1024]{1,0:T(8,128)(2,1)}, u32[]{:S(2)}, u32[]{:S(2)}) collective-permute-start(bf16[128,1024]{1,0:T(8,128)(2,1)} %get-tuple-element.164), channel_id=1, source_target_pairs={{0,2},{2,0},{1,3},{3,1},{4,6},{6,4},{5,7},{7,5},{8,10},{10,8},{9,1... | collective-permute-start | bytes 786440 | tf_op jit(solution)/shard_map/ppermute | solution.py:1060
  275.1 10.7 %collective-permute-start.20 = (bf16[128,1024]{1,0:T(8,128)(2,1)}, bf16[128,1024]{1,0:T(8,128)(2,1)}, u32[]{:S(2)}, u32[]{:S(2)}) collective-permute-start(bf16[128,1024]{1,0:T(8,128)(2,1)} %get-tuple-element.163), channel_id=1, source_target_pairs={{0,4},{4,0},{1,5},{5,1},{2,6},{6,2},{3,7},{7,3},{8,12},{12,8},{9,1... | collective-permute-start | bytes 786440 | tf_op jit(solution)/shard_map/ppermute | solution.py:1060
  276.6 210.7 %reduce-scatter.11.cloned.1.call-start = ((), (), s32[]{:S(2)}) async-start(), calls=%async_computation.10 | async-start | bytes 2621440 | tf_op jit(solution)/shard_map/reduce_scatter | solution.py:1339
  288.3 13.5 %collective-permute-start.21 = (bf16[256,1024]{1,0:T(8,128)(2,1)S(1)}, bf16[256,1024]{1,0:T(8,128)(2,1)S(1)}, u32[]{:S(2)}, u32[]{:S(2)}) collective-permute-start(bf16[256,1024]{1,0:T(8,128)(2,1)S(1)} %pad_maximum_fusion.7), channel_id=1, source_target_pairs={{0,4},{4,0},{1,5},{5,1},{2,6},{6,2},{3,7},{7,3},{8,12},{12,8},{9,1... | collective-permute-start | bytes 1572872 | tf_op jit(solution)/shard_map/ppermute | solution.py:1060
  290.0 13.2 %collective-permute-start.22 = (bf16[256,1024]{1,0:T(8,128)(2,1)S(1)}, bf16[256,1024]{1,0:T(8,128)(2,1)S(1)}, u32[]{:S(2)}, u32[]{:S(2)}) collective-permute-start(bf16[256,1024]{1,0:T(8,128)(2,1)S(1)} %pad_maximum_fusion.8), channel_id=1, source_target_pairs={{0,2},{2,0},{1,3},{3,1},{4,6},{6,4},{5,7},{7,5},{8,10},{10,8},{9,1... | collective-permute-start | bytes 1572872 | tf_op jit(solution)/shard_map/ppermute | solution.py:1060
  324.4 10.9 %collective-permute-start.23 = (bf16[2,2,2,512,128]{4,3,2,1,0:T(8,128)(2,1)S(1)}, bf16[2,2,2,512,128]{4,3,2,1,0:T(8,128)(2,1)}, u32[]{:S(2)}, u32[]{:S(2)}) collective-permute-start(bf16[2,2,2,512,128]{4,3,2,1,0:T(8,128)(2,1)S(1)} %dynamic-slice_bitcast_fusion), channel_id=1, source_target_pairs={{0,1},{1,0},{2,3},{3,2},{4,5},{5,4},{6,7},{7,6},{8,9},{9,8},{10,11... | collective-permute-start | bytes 3145736 | tf_op jit(solution)/shard_map/ppermute | solution.py:1060
  344.5 15.9 %collective-permute-start.25 = (bf16[2,2,4,3,256,128]{5,4,3,2,0,1:T(8,128)(2,1)}, bf16[2,2,4,3,256,128]{5,4,3,2,0,1:T(8,128)(2,1)}, u32[]{:S(2)}, u32[]{:S(2)}) collective-permute-start(bf16[2,2,4,3,256,128]{5,4,3,2,0,1:T(8,128)(2,1)} %copy.75), channel_id=1, source_target_pairs={{0,1},{1,0},{2,3},{3,2},{4,5},{5,4},{6,7},{7,6},{8,9},{9,8},{10,11... | collective-permute-start | bytes 9437192 | tf_op jit(solution)/shard_map/ppermute | solution.py:1060
  344.5 10.3 %collective-permute-start.26 = (bf16[1024,1024]{1,0:T(8,128)(2,1)}, bf16[1024,1024]{1,0:T(8,128)(2,1)}, u32[]{:S(2)}, u32[]{:S(2)}) collective-permute-start(bf16[1024,1024]{1,0:T(8,128)(2,1)} %convolution_convert_fusion.1), channel_id=1, source_target_pairs={{0,1},{1,0},{2,3},{3,2},{4,5},{5,4},{6,7},{7,6},{8,9},{9,8},{10,11... | collective-permute-start | bytes 6291464 | tf_op jit(solution)/shard_map/ppermute | solution.py:1060
  346.9 18.4 %all-to-all-start.1 = ((bf16[256,8,128]{2,0,1:T(8,128)(2,1)}), bf16[256,8,128]{2,0,1:T(8,128)(2,1)S(1)}, u32[]{:S(2)}, u32[]{:S(2)}) async-start(bf16[256,8,128]{2,0,1:T(8,128)(2,1)} %copy_bitcast_fusion.1), calls=%async_computation.2 | async-start | bytes 1048576 | tf_op jit(solution)/shard_map/all_to_all | solution.py:1370
  350.9 186.0 %reduce-scatter.7.cloned.1.call-start = ((), (), s32[]{:S(2)}) async-start(), calls=%async_computation.8 | async-start | bytes 1638400 | tf_op jit(solution)/shard_map/reduce_scatter | solution.py:1445
  354.7 14.6 %collective-permute-start.24 = (bf16[2,2,512,128]{3,2,1,0:T(8,128)(2,1)}, bf16[2,2,512,128]{3,2,1,0:T(8,128)(2,1)S(1)}, u32[]{:S(2)}, u32[]{:S(2)}) collective-permute-start(bf16[2,2,512,128]{3,2,1,0:T(8,128)(2,1)} %dynamic-slice_bitcast_fusion.4), channel_id=1, source_target_pairs={{0,2},{2,0},{1,3},{3,1},{4,6},{6,4},{5,7},{7,5},{8,10},{10,8},{9,1... | collective-permute-start | bytes 1572872 | tf_op jit(solution)/shard_map/ppermute | solution.py:1060
  394.2 21.5 %collective-permute-start.27 = (bf16[128,1024]{1,0:T(8,128)(2,1)}, bf16[128,1024]{1,0:T(8,128)(2,1)}, u32[]{:S(2)}, u32[]{:S(2)}) collective-permute-start(bf16[128,1024]{1,0:T(8,128)(2,1)} %get-tuple-element.151), channel_id=1, source_target_pairs={{0,2},{2,0},{1,3},{3,1},{4,6},{6,4},{5,7},{7,5},{8,10},{10,8},{9,1... | collective-permute-start | bytes 786440 | tf_op jit(solution)/shard_map/ppermute | solution.py:1060
  395.9 31.3 %collective-permute-start.34 = (bf16[128,1024]{1,0:T(8,128)(2,1)}, bf16[128,1024]{1,0:T(8,128)(2,1)}, u32[]{:S(2)}, u32[]{:S(2)}) collective-permute-start(bf16[128,1024]{1,0:T(8,128)(2,1)} %get-tuple-element.152), channel_id=1, source_target_pairs={{0,4},{4,0},{1,5},{5,1},{2,6},{6,2},{3,7},{7,3},{8,12},{12,8},{9,1... | collective-permute-start | bytes 786440 | tf_op jit(solution)/shard_map/ppermute | solution.py:1060
  397.4 33.8 %collective-permute-start.28 = (bf16[1024,1024]{1,0:T(8,128)(2,1)}, bf16[1024,1024]{1,0:T(8,128)(2,1)S(1)}, u32[]{:S(2)}, u32[]{:S(2)}) collective-permute-start(bf16[1024,1024]{1,0:T(8,128)(2,1)} %convolution_convert_fusion), channel_id=1, source_target_pairs={{0,1},{1,0},{2,3},{3,2},{4,5},{5,4},{6,7},{7,6},{8,9},{9,8},{10,11... | collective-permute-start | bytes 6291464 | tf_op jit(solution)/shard_map/ppermute | solution.py:1060
  401.3 11.5 %collective-permute-start.38 = (bf16[2,512,128]{2,1,0:T(8,128)(2,1)}, bf16[2,512,128]{2,1,0:T(8,128)(2,1)}, u32[]{:S(2)}, u32[]{:S(2)}) collective-permute-start(bf16[2,512,128]{2,1,0:T(8,128)(2,1)} %dynamic-slice_bitcast_fusion.17), channel_id=1, source_target_pairs={{0,4},{4,0},{1,5},{5,1},{2,6},{6,2},{3,7},{7,3},{8,12},{12,8},{9,1... | collective-permute-start | bytes 786440 | tf_op jit(solution)/shard_map/ppermute | solution.py:1060
  403.3 87.2 %collective-permute-start.53 = (bf16[2,2,3,256,128]{4,3,2,1,0:T(8,128)(2,1)}, bf16[2,2,3,256,128]{4,3,2,1,0:T(8,128)(2,1)}, u32[]{:S(2)}, u32[]{:S(2)}) collective-permute-start(bf16[2,2,3,256,128]{4,3,2,1,0:T(8,128)(2,1)} %dynamic-slice_bitcast_fusion.1), channel_id=1, source_target_pairs={{0,4},{4,0},{1,5},{5,1},{2,6},{6,2},{3,7},{7,3},{8,12},{12,8},{9,1... | collective-permute-start | bytes 2359304 | tf_op jit(solution)/shard_map/ppermute | solution.py:1060
  412.8 79.2 %collective-permute-start.51 = (bf16[2,2,3,256,128]{4,3,2,1,0:T(8,128)(2,1)}, bf16[2,2,3,256,128]{4,3,2,1,0:T(8,128)(2,1)}, u32[]{:S(2)}, u32[]{:S(2)}) collective-permute-start(bf16[2,2,3,256,128]{4,3,2,1,0:T(8,128)(2,1)} %dynamic-slice_bitcast_fusion.2), channel_id=1, source_target_pairs={{0,2},{2,0},{1,3},{3,1},{4,6},{6,4},{5,7},{7,5},{8,10},{10,8},{9,1... | collective-permute-start | bytes 2359304 | tf_op jit(solution)/shard_map/ppermute | solution.py:1060
  415.8 34.2 %collective-permute-start.56 = (bf16[256,1024]{1,0:T(8,128)(2,1)S(1)}, bf16[256,1024]{1,0:T(8,128)(2,1)S(1)}, u32[]{:S(2)}, u32[]{:S(2)}) collective-permute-start(bf16[256,1024]{1,0:T(8,128)(2,1)S(1)} %broadcast_add_fusion), channel_id=1, source_target_pairs={{0,0},{1,8},{2,16},{3,24},{4,4},{5,12},{6,20},{7,28},{8,1},{9,9},{... | collective-permute-start | bytes 1572872 | tf_op jit(solution)/shard_map/ppermute | solution.py:1083
  435.1 16.1 %collective-permute-start.29 = (bf16[128,1024]{1,0:T(8,128)(2,1)S(1)}, bf16[128,1024]{1,0:T(8,128)(2,1)S(1)}, u32[]{:S(2)}, u32[]{:S(2)}) collective-permute-start(bf16[128,1024]{1,0:T(8,128)(2,1)S(1)} %get-tuple-element.157), channel_id=1, source_target_pairs={{0,2},{2,0},{1,3},{3,1},{4,6},{6,4},{5,7},{7,5},{8,10},{10,8},{9,1... | collective-permute-start | bytes 786440 | tf_op jit(solution)/shard_map/ppermute | solution.py:1060
  435.2 16.0 %collective-permute-start.31 = (bf16[128,1024]{1,0:T(8,128)(2,1)S(1)}, bf16[128,1024]{1,0:T(8,128)(2,1)S(1)}, u32[]{:S(2)}, u32[]{:S(2)}) collective-permute-start(bf16[128,1024]{1,0:T(8,128)(2,1)S(1)} %get-tuple-element.158), channel_id=1, source_target_pairs={{0,4},{4,0},{1,5},{5,1},{2,6},{6,2},{3,7},{7,3},{8,12},{12,8},{9,1... | collective-permute-start | bytes 786440 | tf_op jit(solution)/shard_map/ppermute | solution.py:1060
  452.3 9.6 %collective-permute-start.32 = (bf16[256,1024]{1,0:T(8,128)(2,1)}, bf16[256,1024]{1,0:T(8,128)(2,1)}, u32[]{:S(2)}, u32[]{:S(2)}) collective-permute-start(bf16[256,1024]{1,0:T(8,128)(2,1)} %pad_maximum_fusion.10), channel_id=1, source_target_pairs={{0,2},{2,0},{1,3},{3,1},{4,6},{6,4},{5,7},{7,5},{8,10},{10,8},{9,1... | collective-permute-start | bytes 1572872 | tf_op jit(solution)/shard_map/ppermute | solution.py:1060
  453.1 9.6 %collective-permute-start.30 = (bf16[256,1024]{1,0:T(8,128)(2,1)}, bf16[256,1024]{1,0:T(8,128)(2,1)}, u32[]{:S(2)}, u32[]{:S(2)}) collective-permute-start(bf16[256,1024]{1,0:T(8,128)(2,1)} %pad_maximum_fusion.9), channel_id=1, source_target_pairs={{0,4},{4,0},{1,5},{5,1},{2,6},{6,2},{3,7},{7,3},{8,12},{12,8},{9,1... | collective-permute-start | bytes 1572872 | tf_op jit(solution)/shard_map/ppermute | solution.py:1060
  456.0 131.2 %reduce-scatter.9.cloned.1.call-start = ((), (), s32[]{:S(2)}) async-start(), calls=%async_computation.9 | async-start | bytes 983040 | tf_op jit(solution)/shard_map/reduce_scatter | solution.py:1453
  469.9 56.3 %collective-permute-start.35 = (bf16[256,1024]{1,0:T(8,128)(2,1)}, bf16[256,1024]{1,0:T(8,128)(2,1)}, u32[]{:S(2)}, u32[]{:S(2)}) collective-permute-start(bf16[256,1024]{1,0:T(8,128)(2,1)} %maximum_add_fusion.1), channel_id=1, source_target_pairs={{0,2},{2,0},{1,3},{3,1},{4,6},{6,4},{5,7},{7,5},{8,10},{10,8},{9,1... | collective-permute-start | bytes 1572872 | tf_op jit(solution)/shard_map/ppermute | solution.py:1060
  472.7 55.2 %collective-permute-start.33 = (bf16[256,1024]{1,0:T(8,128)(2,1)}, bf16[256,1024]{1,0:T(8,128)(2,1)}, u32[]{:S(2)}, u32[]{:S(2)}) collective-permute-start(bf16[256,1024]{1,0:T(8,128)(2,1)} %maximum_add_fusion), channel_id=1, source_target_pairs={{0,4},{4,0},{1,5},{5,1},{2,6},{6,2},{3,7},{7,3},{8,12},{12,8},{9,1... | collective-permute-start | bytes 1572872 | tf_op jit(solution)/shard_map/ppermute | solution.py:1060
  474.9 69.5 %collective-permute-start.37 = (bf16[256,1024]{1,0:T(8,128)(2,1)}, bf16[256,1024]{1,0:T(8,128)(2,1)}, u32[]{:S(2)}, u32[]{:S(2)}) collective-permute-start(bf16[256,1024]{1,0:T(8,128)(2,1)} %fusion.55), channel_id=1, source_target_pairs={{0,0},{1,8},{2,16},{3,24},{4,4},{5,12},{6,20},{7,28},{8,1},{9,9},{... | collective-permute-start | bytes 1572872 | tf_op jit(solution)/shard_map/ppermute | solution.py:1083
  492.0 14.3 %collective-permute-start.57 = (bf16[128,1024]{1,0:T(8,128)(2,1)S(1)}, bf16[128,1024]{1,0:T(8,128)(2,1)S(1)}, u32[]{:S(2)}, u32[]{:S(2)}) collective-permute-start(bf16[128,1024]{1,0:T(8,128)(2,1)S(1)} %dynamic-slice_bitcast_fusion.15), channel_id=1, source_target_pairs={{0,4},{4,0},{1,5},{5,1},{2,6},{6,2},{3,7},{7,3},{8,12},{12,8},{9,1... | collective-permute-start | bytes 786440 | tf_op jit(solution)/shard_map/ppermute | solution.py:1060
  494.5 7.1 %collective-permute-start.44 = (f32[21,1024]{1,0:T(8,128)S(1)}, f32[21,1024]{1,0:T(8,128)S(1)}, u32[]{:S(2)}, u32[]{:S(2)}) collective-permute-start(f32[21,1024]{1,0:T(8,128)S(1)} %fusion.116), channel_id=1, source_target_pairs={{0,2},{2,0},{1,3},{3,1},{4,6},{6,4},{5,7},{7,5},{8,10},{10,8},{9,1... | collective-permute-start | bytes 258056 | tf_op jit(solution)/shard_map/ppermute | solution.py:1060
  506.3 17.5 %collective-permute-start.39 = (bf16[2,2,64,1024]{3,2,1,0:T(8,128)(2,1)}, bf16[2,2,64,1024]{3,2,1,0:T(8,128)(2,1)}, u32[]{:S(2)}, u32[]{:S(2)}) collective-permute-start(bf16[2,2,64,1024]{3,2,1,0:T(8,128)(2,1)} %dynamic-slice_bitcast_fusion.3), channel_id=1, source_target_pairs={{0,1},{1,0},{2,3},{3,2},{4,5},{5,4},{6,7},{7,6},{8,9},{9,8},{10,11... | collective-permute-start | bytes 1572872 | tf_op jit(solution)/shard_map/ppermute | solution.py:1060
  506.4 5.3 collective-permute-start.46
  512.3 7.8 %collective-permute-start.47 = (f32[21,1024]{1,0:T(8,128)}, f32[21,1024]{1,0:T(8,128)}, u32[]{:S(2)}, u32[]{:S(2)}) collective-permute-start(f32[21,1024]{1,0:T(8,128)} %add.607), channel_id=1, source_target_pairs={{0,16},{8,24},{16,0},{24,8},{1,17},{9,25},{17,1},{25,9},{2,18},{10... | collective-permute-start | bytes 258056 | tf_op jit(solution)/shard_map/ppermute | solution.py:1060
  520.1 20.0 %collective-permute-start.54 = (bf16[2,3,256,128]{3,2,1,0:T(8,128)(2,1)S(1)}, bf16[2,3,256,128]{3,2,1,0:T(8,128)(2,1)}, u32[]{:S(2)}, u32[]{:S(2)}) collective-permute-start(bf16[2,3,256,128]{3,2,1,0:T(8,128)(2,1)S(1)} %dynamic-slice_bitcast_fusion.13), channel_id=1, source_target_pairs={{0,2},{2,0},{1,3},{3,1},{4,6},{6,4},{5,7},{7,5},{8,10},{10,8},{9,1... | collective-permute-start | bytes 1179656 | tf_op jit(solution)/shard_map/ppermute | solution.py:1060
  523.8 17.4 %collective-permute-start.52 = (bf16[2,3,256,128]{3,2,1,0:T(8,128)(2,1)}, bf16[2,3,256,128]{3,2,1,0:T(8,128)(2,1)}, u32[]{:S(2)}, u32[]{:S(2)}) collective-permute-start(bf16[2,3,256,128]{3,2,1,0:T(8,128)(2,1)} %dynamic-slice_bitcast_fusion.14), channel_id=1, source_target_pairs={{0,4},{4,0},{1,5},{5,1},{2,6},{6,2},{3,7},{7,3},{8,12},{12,8},{9,1... | collective-permute-start | bytes 1179656 | tf_op jit(solution)/shard_map/ppermute | solution.py:1060
  526.2 10.6 %collective-permute-start.40 = (bf16[2,64,1024]{2,1,0:T(8,128)(2,1)S(1)}, bf16[2,64,1024]{2,1,0:T(8,128)(2,1)S(1)}, u32[]{:S(2)}, u32[]{:S(2)}) collective-permute-start(bf16[2,64,1024]{2,1,0:T(8,128)(2,1)S(1)} %dynamic-slice_bitcast_fusion.16), channel_id=1, source_target_pairs={{0,2},{2,0},{1,3},{3,1},{4,6},{6,4},{5,7},{7,5},{8,10},{10,8},{9,1... | collective-permute-start | bytes 786440 | tf_op jit(solution)/shard_map/ppermute | solution.py:1060
  529.6 49.9 %collective-permute-start.36 = (bf16[256,1024]{1,0:T(8,128)(2,1)S(1)}, bf16[256,1024]{1,0:T(8,128)(2,1)S(1)}, u32[]{:S(2)}, u32[]{:S(2)}) collective-permute-start(bf16[256,1024]{1,0:T(8,128)(2,1)S(1)} %add_convert_fusion.4), channel_id=1, source_target_pairs={{0,0},{1,8},{2,16},{3,24},{4,4},{5,12},{6,20},{7,28},{8,1},{9,9},{... | collective-permute-start | bytes 1572872 | tf_op jit(solution)/shard_map/ppermute | solution.py:1083
  548.4 28.4 %collective-permute-start.42 = (bf16[64,1024]{1,0:T(8,128)(2,1)S(1)}, bf16[64,1024]{1,0:T(8,128)(2,1)S(1)}, u32[]{:S(2)}, u32[]{:S(2)}) collective-permute-start(bf16[64,1024]{1,0:T(8,128)(2,1)S(1)} %fusion.73), channel_id=1, source_target_pairs={{0,0},{1,8},{2,16},{3,24},{4,4},{5,12},{6,20},{7,28},{8,1},{9,9},{... | collective-permute-start | bytes 393224 | tf_op jit(solution)/shard_map/ppermute | solution.py:1083
  553.7 25.8 %collective-permute-start.50 = (bf16[256,128]{1,0:T(8,128)(2,1)S(1)}, bf16[256,128]{1,0:T(8,128)(2,1)S(1)}, u32[]{:S(2)}, u32[]{:S(2)}) collective-permute-start(bf16[256,128]{1,0:T(8,128)(2,1)S(1)} %get-tuple-element.184), channel_id=1, source_target_pairs={{1,0},{9,1},{17,2},{25,3},{6,4},{14,5},{22,6},{30,7},{0,8},{8,9},{... | collective-permute-start | bytes 196616 | tf_op jit(solution)/shard_map/ppermute | solution.py:1477
  555.6 24.0 %collective-permute-start.49 = (bf16[256,128]{1,0:T(8,128)(2,1)S(1)}, bf16[256,128]{1,0:T(8,128)(2,1)S(1)}, u32[]{:S(2)}, u32[]{:S(2)}) collective-permute-start(bf16[256,128]{1,0:T(8,128)(2,1)S(1)} %get-tuple-element.185), channel_id=1, source_target_pairs={{4,0},{12,1},{20,2},{28,3},{2,4},{10,5},{18,6},{26,7},{7,8},{15,9}... | collective-permute-start | bytes 196616 | tf_op jit(solution)/shard_map/ppermute | solution.py:1477
  557.2 23.6 %collective-permute-start.48 = (bf16[256,128]{1,0:T(8,128)(2,1)S(1)}, bf16[256,128]{1,0:T(8,128)(2,1)S(1)}, u32[]{:S(2)}, u32[]{:S(2)}) collective-permute-start(bf16[256,128]{1,0:T(8,128)(2,1)S(1)} %get-tuple-element.183), channel_id=1, source_target_pairs={{0,0},{8,1},{16,2},{24,3},{5,4},{13,5},{21,6},{29,7},{3,8},{11,9},... | collective-permute-start | bytes 196616 | tf_op jit(solution)/shard_map/ppermute | solution.py:1477
  576.9 9.6 %collective-permute-start.55 = (bf16[2,256,128]{2,1,0:T(8,128)(2,1)S(1)}, bf16[2,256,128]{2,1,0:T(8,128)(2,1)S(1)}, u32[]{:S(2)}, u32[]{:S(2)}) collective-permute-start(bf16[2,256,128]{2,1,0:T(8,128)(2,1)S(1)} %slice_bitcast_fusion.1), channel_id=1, source_target_pairs={{0,0},{1,8},{2,16},{3,24},{4,4},{5,12},{6,20},{7,28},{8,1},{9,9},{... | collective-permute-start | bytes 393224 | tf_op jit(solution)/shard_map/ppermute | solution.py:1083
  (73 other events, 591.8 us)
Sparse Core Ops, SparseCore 0:
  64.9 26.0 all-gather.5
  92.9 45.4 all-gather.7
  148.7 35.7 all-gather.9
  276.7 48.1 reduce-scatter.4
  345.5 47.1 reduce-scatter.10
  456.1 38.2 reduce-scatter.6
  543.5 33.0 reduce-scatter.8

commit v3 on v2

--- a/solution.py
+++ b/solution.py
@@ -1382,7 +1382,7 @@
         n_z,
     )
     self_out_bias_grad = jnp.sum(wide(self_grad_low), axis=0)
-    three = plus(keep, over_core(send))
+    three = plus(keep, row_major(over_core(send)))
     out_sum = plus(out_mine, over_core(after(out_sent, self_att_grad)))
     att_grad_heads, kv_other, three, out_sum = tie((att_grad_heads, kv_other, three, out_sum))
     kv_part = plus(at(kv_part, me_x, 0), kv_other)

time: 602 us -> 597 us (level)
  starting transfers between devices: 97.4 us -> 83.7 us
  waiting for transfers between devices: 159 us -> 168 us
    ppermute x8, starting transfers between devices: 46.5 us -> 30.7 us  [trade_places(): return lax.ppermute(value, ALL, pairs)]
where the time goes in v3:
time: 597 us; the launch traced here: 591 us
  waiting for transfers between devices  168 us (28%)
  Pallas kernels  106 us (18%)
  local copies, waits for them, and re-layouts  92.9 us (16%)
  starting transfers between devices  83.7 us (14%)
  other arithmetic  64 us (11%)
  matrix products  54.5 us (9%)
  between operations  21.6 us (4%)
    ppermute x47, waiting for transfers between devices, over(): return lax.ppermute(value, axis, [(i, i ^ distance) for i in range(count)])  97.7 us
    ppermute x8, waiting for transfers between devices, trade_places(): return lax.ppermute(value, ALL, pairs)  61.4 us
    ppermute x47, starting transfers between devices, over(): return lax.ppermute(value, axis, [(i, i ^ distance) for i in range(count)])  34.9 us
    ppermute x8, starting transfers between devices, trade_places(): return lax.ppermute(value, ALL, pairs)  30.7 us
    unnamed x153, local copies, waits for them, and re-layouts  28.2 us
    dot_general x8, matrix products, plain_dot(): return jnp.dot(left, right, preferred_element_type=jnp.float32)  26.8 us
    pallas_call x2, Pallas kernels, mlp_forward_back(): pl.pallas_call(mlp_kernel, grid=(rows // ROW_BLOCK,), in_specs=[pl.BlockS...  25.7 us
    convert_element_type x15, other arithmetic, low(): return value.astype(jnp.bfloat16)  20.9 us
  transfers between devices with their start and end apart: 67, of which 24 were waited for; matrix products, arithmetic and copies ran while one was open for 30% of the time, Pallas kernels for 13%

profile of v3, /device:TPU:2, one launch (start us, length us, event | category | flops | bytes accessed | tf_op | source)
XLA Modules:
  0.0 591.3 jit_solution(15650806377122425532)
XLA Ops:
  16.1 5.9 %collective-permute-start = (bf16[320,1024]{1,0:T(8,128)(2,1)}, bf16[320,1024]{1,0:T(8,128)(2,1)S(1)}, u32[]{:S(2)}, u32[]{:S(2)}) collective-permute-start(bf16[320,1024]{1,0:T(8,128)(2,1)} %pad_maximum_fusion.6), channel_id=1, source_target_pairs={{0,0},{1,8},{2,16},{3,24},{4,4},{5,12},{6,20},{7,28},{8,1},{9,9},{... | collective-permute-start | bytes 1966088 | tf_op jit(solution)/shard_map/ppermute | solution.py:1083
  24.1 3.3 shard_map.297
  30.7 5.7 collective-permute-start.12
  37.1 26.2 %collective-permute-done = bf16[320,1024]{1,0:T(8,128)(2,1)S(1)} collective-permute-done((bf16[320,1024]{1,0:T(8,128)(2,1)}, bf16[320,1024]{1,0:T(8,128)(2,1)S(1)}, u32[]{:S(2)}, u32[]{:S(2)}) %collective-permute-start) | collective-permute-done | bytes 655392 | tf_op jit(solution)/shard_map/ppermute | solution.py:1083
  73.4 3.4 broadcast_in_dim.102
  76.7 2.6 constant_dynamic-update-slice_fusion.19
  79.7 3.2 constant_dynamic-slice_fusion.1.down_ref
  87.3 6.2 %collective-permute-done.2 = bf16[256,1024]{1,0:T(8,128)(2,1)S(1)} collective-permute-done((bf16[256,1024]{1,0:T(8,128)(2,1)S(1)}, bf16[256,1024]{1,0:T(8,128)(2,1)S(1)}, u32[]{:S(2)}, u32[]{:S(2)}) %collective-permute-start.2) | collective-permute-done | bytes 524320 | tf_op jit(solution)/shard_map/ppermute | solution.py:1060
  93.6 24.1 %collective-permute-done.3 = bf16[256,1024]{1,0:T(8,128)(2,1)S(1)} collective-permute-done((bf16[256,1024]{1,0:T(8,128)(2,1)S(1)}, bf16[256,1024]{1,0:T(8,128)(2,1)S(1)}, u32[]{:S(2)}, u32[]{:S(2)}) %collective-permute-start.3) | collective-permute-done | bytes 524320 | tf_op jit(solution)/shard_map/ppermute | solution.py:1060
  123.5 3.3 collective-permute-done.5
  128.8 3.0 pad_maximum_fusion
  143.0 2.5 fusion.48
  145.5 3.0 multiply_convert_fusion.1
  148.6 3.0 multiply_convert_fusion
  151.8 12.8 %shard_map.298 = bf16[2048,128]{1,0:T(8,128)(2,1)} custom-call(s32[8]{0:T(128)S(1)} %bitcast_subtract_fusion.2.starts_ref, s32[1]{0:T(128)} %bitcast.5.own_ref, bf16[2048,384]{1,0:T(8,128)(2,1)S(1)} %pad_maximum_fusion.4.qkv_ref), custom_call_target="tpu_custom_call" | custom-call | flops 1150000000 | bytes 1048576 | tf_op jit(solution)/shard_map/pallas_call | solution.py:809
  164.7 5.3 all-to-all-start
  169.9 2.9 slice_dynamic-update-slice_fusion.1
  172.8 2.6 slice_dynamic-update-slice_fusion
  175.4 7.3 %all-to-all-done = bf16[8,256,128]{2,1,0:T(8,128)(2,1)S(1)} async-done(((bf16[8,256,128]{2,1,0:T(8,128)(2,1)}), bf16[8,256,128]{2,1,0:T(8,128)(2,1)S(1)}, u32[]{:S(2)}, u32[]{:S(2)}) %all-to-all-start) | async-done | bytes 524320 | tf_op jit(solution)/shard_map/all_to_all | solution.py:1304
  182.7 2.6 fusion.93
  189.8 9.9 %shard_map.299.refs_4_ = bf16[256,1024]{1,0:T(8,128)(2,1)S(1)} custom-call(bf16[256,1024]{1,0:T(8,128)(2,1)S(1)} %fusion.34.q_ref, bf16[8,512,256]{2,1,0:T(8,128)(2,1)S(1)} %bitcast.238, bf16[8,512,256]{2,1,0:T(8,128)(2,1)S(1)} %bitcast.239, s32[256,1]{1,0:T(8,128)S(1)} %copy.71.low_ref, s32[256,1]{1,0:T(8,128)S(1)} %copy.72.high_ref), custom_call_target="tpu_custom_call" | custom-call | flops 1150000000 | bytes 1048576 | tf_op jit(solution)/shard_map/pallas_call | solution.py:849
  199.7 2.6 fusion.94
  206.1 10.5 %collective-permute-done.13 = bf16[256,1024]{1,0:T(8,128)(2,1)S(1)} collective-permute-done((bf16[256,1024]{1,0:T(8,128)(2,1)S(1)}, bf16[256,1024]{1,0:T(8,128)(2,1)S(1)}, u32[]{:S(2)}, u32[]{:S(2)}) %collective-permute-start.13) | collective-permute-done | bytes 524320 | tf_op jit(solution)/shard_map/ppermute | solution.py:1060
  219.8 4.0 collective-permute-done.15
  225.9 2.6 dynamic-slice_bitcast_fusion.12
  230.8 12.8 %shard_map.301 = (bf16[1024,1024]{1,0:T(8,128)(2,1)S(1)}, bf16[1024,1024]{1,0:T(8,128)(2,1)S(1)}, bf16[1024,1024]{1,0:T(8,128)(2,1)}, f32[1,1024]{1,0:T(1,128)S(1)}) custom-call(bf16[1024,1024]{1,0:T(8,128)(2,1)} %collective-permute-done.17.act_ref.left_two_ref, bf16[1024,1024]{1,0:T(8,128)(2,1)} %get-tuple-element.82.grad_ref.left_two_ref, ...), custom_call_target="tpu_custom_call" | custom-call | flops 1150000000 | bytes 1048576 | tf_op jit(solution)/shard_map/pallas_call | solution.py:926
  246.8 12.9 %shard_map.300 = (bf16[1024,1024]{1,0:T(8,128)(2,1)S(1)}, bf16[1024,1024]{1,0:T(8,128)(2,1)S(1)}, bf16[1024,1024]{1,0:T(8,128)(2,1)}, f32[1,1024]{1,0:T(1,128)S(1)}) custom-call(bf16[1024,1024]{1,0:T(8,128)(2,1)} %copy-done.6, bf16[1024,1024]{1,0:T(8,128)(2,1)} %get-tuple-element.80.grad_ref.left_ref, ...), custom_call_target="tpu_custom_call" | custom-call | flops 1150000000 | bytes 1048576 | tf_op jit(solution)/shard_map/pallas_call | solution.py:926
  262.3 8.0 %shard_map.302 = bf16[1024,1024]{1,0:T(8,128)(2,1)S(1)} custom-call(bf16[1024,1024]{1,0:T(8,128)(2,1)S(1)} %copy-done.7, bf16[1024,1024]{1,0:T(8,128)(2,1)} %copy-done.14, bf16[1024,1024]{1,0:T(8,128)(2,1)} %collective-permute-done.17.act_ref.left_two_ref, bf16[1024,1024]{1,0:T(8,128)(2,1)} %copy-done.13), custom_call_target="tpu_custom_call" | custom-call | flops 1150000000 | bytes 1048576 | tf_op jit(solution)/shard_map/pallas_call | solution.py:980
  271.7 2.5 add_convert_fusion.3
  279.5 9.1 %shard_map.303 = bf16[1024,1024]{1,0:T(8,128)(2,1)} custom-call(bf16[1024,1024]{1,0:T(8,128)(2,1)S(1)} %copy-done.2, bf16[1024,1024]{1,0:T(8,128)(2,1)} %copy-done.9, bf16[1024,1024]{1,0:T(8,128)(2,1)} %get-tuple-element.82.grad_ref.left_two_ref, bf16[1024,1024]{1,0:T(8,128)(2,1)} %copy-done.11), custom_call_target="tpu_custom_call" | custom-call | flops 1150000000 | bytes 1048576 | tf_op jit(solution)/shard_map/pallas_call | solution.py:980
  293.4 5.2 convolution_convert_fusion.1
  298.7 5.9 %collective-permute-done.21 = bf16[256,1024]{1,0:T(8,128)(2,1)S(1)} collective-permute-done((bf16[256,1024]{1,0:T(8,128)(2,1)S(1)}, bf16[256,1024]{1,0:T(8,128)(2,1)S(1)}, u32[]{:S(2)}, u32[]{:S(2)}) %collective-permute-start.21) | collective-permute-done | bytes 524320 | tf_op jit(solution)/shard_map/ppermute | solution.py:1060
  309.0 3.1 convert_reduce_fusion.4
  312.1 14.5 %shard_map.304 = (bf16[256,1024]{1,0:T(8,128)(2,1)S(1)}, bf16[2,8,512,128]{3,2,1,0:T(8,128)(2,1)S(1)}) custom-call(bf16[256,1024]{1,0:T(8,128)(2,1)S(1)} %fusion.34.q_ref, bf16[8,512,256]{2,1,0:T(8,128)(2,1)S(1)} %bitcast.240, bf16[8,512,256]{2,1,0:T(8,128)(2,1)S(1)} %bitcast.241, bf16[256,1024]{1,0:T(8,128)(2,1)S(1)} %get-tuple-element.217.grad_ref, ...), custom_call_target="tpu_custom_call" | custom-call | flops 1150000000 | bytes 1048576 | tf_op jit(solution)/shard_map/pallas_call | solution.py:870
  328.6 3.3 multiply_reduce_fusion.1
  333.8 3.8 convert_reduce_fusion.7
  337.7 4.8 shard_map.305
  345.3 4.4 all-to-all-start.1
  354.0 5.5 add_convert_fusion.2
  359.5 4.8 add_convert_fusion
  364.4 3.8 collective-permute-done.24
  368.2 18.3 %shard_map.306 = bf16[2048,384]{1,0:T(8,128)(2,1)S(1)} custom-call(s32[8]{0:T(128)S(1)} %bitcast_subtract_fusion.2.starts_ref, s32[1]{0:T(128)} %bitcast.5.own_ref, bf16[2048,384]{1,0:T(8,128)(2,1)S(1)} %copy-done.17, bf16[2048,128]{1,0:T(8,128)(2,1)S(1)} %bitcast.244), custom_call_target="tpu_custom_call" | custom-call | flops 1150000000 | bytes 1048576 | tf_op jit(solution)/shard_map/pallas_call | solution.py:827
  386.5 3.7 convolution_convert_fusion
  390.6 3.9 fusion.67
  398.5 3.0 fusion.63
  405.8 4.0 fusion.14
  416.9 3.8 collective-permute-start.56
  422.1 2.5 convolution_convert_fusion.2
  425.9 2.5 add_convert_fusion.1
  430.0 15.7 %collective-permute-done.56 = bf16[256,1024]{1,0:T(8,128)(2,1)S(1)} collective-permute-done((bf16[256,1024]{1,0:T(8,128)(2,1)S(1)}, bf16[256,1024]{1,0:T(8,128)(2,1)S(1)}, u32[]{:S(2)}, u32[]{:S(2)}) %collective-permute-start.56) | collective-permute-done | bytes 524320 | tf_op jit(solution)/shard_map/ppermute | solution.py:1083
  447.0 3.4 collective-permute-done.29
  457.7 7.0 %collective-permute-done.32 = bf16[256,1024]{1,0:T(8,128)(2,1)} collective-permute-done((bf16[256,1024]{1,0:T(8,128)(2,1)}, bf16[256,1024]{1,0:T(8,128)(2,1)}, u32[]{:S(2)}, u32[]{:S(2)}) %collective-permute-start.32) | collective-permute-done | bytes 524320 | tf_op jit(solution)/shard_map/ppermute | solution.py:1060
  477.4 3.3 collective-permute-start.37
  488.0 2.8 collective-permute-start.44
  490.8 5.2 collective-permute-done.44
  497.8 3.0 collective-permute-done.45
  500.9 5.1 collective-permute-done.46
  508.6 5.9 %collective-permute-done.47 = f32[21,1024]{1,0:T(8,128)} collective-permute-done((f32[21,1024]{1,0:T(8,128)}, f32[21,1024]{1,0:T(8,128)}, u32[]{:S(2)}, u32[]{:S(2)}) %collective-permute-start.47) | collective-permute-done | bytes 86048 | tf_op jit(solution)/shard_map/ppermute | solution.py:1060
  523.9 2.6 collective-permute-start.36
  526.5 4.9 collective-permute-done.40
  543.0 5.5 collective-permute-start.42
  551.5 5.2 collective-permute-start.48
  556.7 14.7 %collective-permute-done.42 = bf16[64,1024]{1,0:T(8,128)(2,1)S(1)} collective-permute-done((bf16[64,1024]{1,0:T(8,128)(2,1)S(1)}, bf16[64,1024]{1,0:T(8,128)(2,1)S(1)}, u32[]{:S(2)}, u32[]{:S(2)}) %collective-permute-start.42) | collective-permute-done | bytes 131104 | tf_op jit(solution)/shard_map/ppermute | solution.py:1083
  576.1 4.9 collective-permute-done.55
  (430 shorter events, 175.4 us)
Async XLA Ops:
  7.2 135.9 %all-gather.6.cloned.1.call-start = ((), (), s32[]{:S(2)}) async-start(), calls=%async_computation.6 | async-start | bytes 1179648 | tf_op jit(solution)/shard_map/all_gather | solution.py:1280
  14.2 72.1 %collective-permute-start.9 = (bf16[128,3072]{1,0:T(8,128)(2,1)}, bf16[128,3072]{1,0:T(8,128)(2,1)}, u32[]{:S(2)}, u32[]{:S(2)}) collective-permute-start(bf16[128,3072]{1,0:T(8,128)(2,1)} %constant_dynamic-slice_fusion), channel_id=1, source_target_pairs={{0,2},{2,0},{1,3},{3,1},{4,6},{6,4},{5,7},{7,5},{8,10},{10,8},{9,1... | collective-permute-start | bytes 2359304 | tf_op jit(solution)/shard_map/ppermute | solution.py:1060
  16.1 47.1 %collective-permute-start = (bf16[320,1024]{1,0:T(8,128)(2,1)}, bf16[320,1024]{1,0:T(8,128)(2,1)S(1)}, u32[]{:S(2)}, u32[]{:S(2)}) collective-permute-start(bf16[320,1024]{1,0:T(8,128)(2,1)} %pad_maximum_fusion.6), channel_id=1, source_target_pairs={{0,0},{1,8},{2,16},{3,24},{4,4},{5,12},{6,20},{7,28},{8,1},{9,9},{... | collective-permute-start | bytes 1966088 | tf_op jit(solution)/shard_map/ppermute | solution.py:1083
  22.1 42.7 %collective-permute-start.1 = (s32[2,8]{1,0:T(2,128)S(1)}, s32[2,8]{1,0:T(2,128)S(1)}, u32[]{:S(2)}, u32[]{:S(2)}) collective-permute-start(s32[2,8]{1,0:T(2,128)S(1)} %pad_add_fusion), channel_id=1, source_target_pairs={{0,0},{1,8},{2,16},{3,24},{4,4},{5,12},{6,20},{7,28},{8,1},{9,9},{... | collective-permute-start | bytes 200 | tf_op jit(solution)/shard_map/ppermute | solution.py:1083
  30.7 90.3 %collective-permute-start.6 = (bf16[512,1664]{1,0:T(8,128)(2,1)}, bf16[512,1664]{1,0:T(8,128)(2,1)}, u32[]{:S(2)}, u32[]{:S(2)}) collective-permute-start(bf16[512,1664]{1,0:T(8,128)(2,1)} %slice.434), channel_id=1, source_target_pairs={{0,2},{2,0},{1,3},{3,1},{4,6},{6,4},{5,7},{7,5},{8,10},{10,8},{9,1... | collective-permute-start | bytes 5111816 | tf_op jit(solution)/shard_map/ppermute | solution.py:1060
  30.7 48.7 %collective-permute-start.12 = (bf16[256,1024]{1,0:T(8,128)(2,1)}, bf16[256,1024]{1,0:T(8,128)(2,1)}, u32[]{:S(2)}, u32[]{:S(2)}) collective-permute-start(bf16[256,1024]{1,0:T(8,128)(2,1)} %bitcast.20), channel_id=1, source_target_pairs={{0,0},{1,8},{2,16},{3,24},{4,4},{5,12},{6,20},{7,28},{8,1},{9,9},{... | collective-permute-start | bytes 1572872 | tf_op jit(solution)/shard_map/ppermute | solution.py:1083
  64.8 83.8 %all-gather.8.cloned.1.call-start = ((), (), s32[]{:S(2)}) async-start(), calls=%async_computation.11 | async-start | bytes 4718592 | tf_op jit(solution)/shard_map/all_gather | solution.py:1283
  79.4 108.8 %all-gather.10.cloned.1.call-start = ((), (), s32[]{:S(2)}) async-start(), calls=%async_computation.12 | async-start | bytes 2359296 | tf_op jit(solution)/shard_map/all_gather | solution.py:1300
  84.3 9.2 %collective-permute-start.2 = (bf16[256,1024]{1,0:T(8,128)(2,1)S(1)}, bf16[256,1024]{1,0:T(8,128)(2,1)S(1)}, u32[]{:S(2)}, u32[]{:S(2)}) collective-permute-start(bf16[256,1024]{1,0:T(8,128)(2,1)S(1)} %get-tuple-element.138), channel_id=1, source_target_pairs={{0,4},{4,0},{1,5},{5,1},{2,6},{6,2},{3,7},{7,3},{8,12},{12,8},{9,1... | collective-permute-start | bytes 1572872 | tf_op jit(solution)/shard_map/ppermute | solution.py:1060
  85.9 31.9 %collective-permute-start.3 = (bf16[256,1024]{1,0:T(8,128)(2,1)S(1)}, bf16[256,1024]{1,0:T(8,128)(2,1)S(1)}, u32[]{:S(2)}, u32[]{:S(2)}) collective-permute-start(bf16[256,1024]{1,0:T(8,128)(2,1)S(1)} %get-tuple-element.138), channel_id=1, source_target_pairs={{0,2},{2,0},{1,3},{3,1},{4,6},{6,4},{5,7},{7,5},{8,10},{10,8},{9,1... | collective-permute-start | bytes 1572872 | tf_op jit(solution)/shard_map/ppermute | solution.py:1060
  86.3 41.2 %collective-permute-start.10 = (bf16[128,3072]{1,0:T(8,128)(2,1)}, bf16[128,3072]{1,0:T(8,128)(2,1)S(1)}, u32[]{:S(2)}, u32[]{:S(2)}) collective-permute-start(bf16[128,3072]{1,0:T(8,128)(2,1)} %collective-permute-done.9), channel_id=1, source_target_pairs={{0,4},{4,0},{1,5},{5,1},{2,6},{6,2},{3,7},{7,3},{8,12},{12,8},{9,1... | collective-permute-start | bytes 2359304 | tf_op jit(solution)/shard_map/ppermute | solution.py:1060
  93.5 29.2 %collective-permute-start.4 = (bf16[128,1024]{1,0:T(8,128)(2,1)S(1)}, bf16[128,1024]{1,0:T(8,128)(2,1)S(1)}, u32[]{:S(2)}, u32[]{:S(2)}) collective-permute-start(bf16[128,1024]{1,0:T(8,128)(2,1)S(1)} %slice.430), channel_id=1, source_target_pairs={{0,2},{2,0},{1,3},{3,1},{4,6},{6,4},{5,7},{7,5},{8,10},{10,8},{9,1... | collective-permute-start | bytes 786440 | tf_op jit(solution)/shard_map/ppermute | solution.py:1060
  117.7 9.0 %collective-permute-start.5 = (bf16[128,1024]{1,0:T(8,128)(2,1)S(1)}, bf16[128,1024]{1,0:T(8,128)(2,1)S(1)}, u32[]{:S(2)}, u32[]{:S(2)}) collective-permute-start(bf16[128,1024]{1,0:T(8,128)(2,1)S(1)} %slice.431), channel_id=1, source_target_pairs={{0,4},{4,0},{1,5},{5,1},{2,6},{6,2},{3,7},{7,3},{8,12},{12,8},{9,1... | collective-permute-start | bytes 786440 | tf_op jit(solution)/shard_map/ppermute | solution.py:1060
  122.6 10.9 %collective-permute-start.7 = (bf16[512,1664]{1,0:T(8,128)(2,1)S(1)}, bf16[512,1664]{1,0:T(8,128)(2,1)S(1)}, u32[]{:S(2)}, u32[]{:S(2)}) collective-permute-start(bf16[512,1664]{1,0:T(8,128)(2,1)S(1)} %pad_maximum_fusion.3), channel_id=1, source_target_pairs={{0,1},{1,0},{2,3},{3,2},{4,5},{5,4},{6,7},{7,6},{8,9},{9,8},{10,11... | collective-permute-start | bytes 5111816 | tf_op jit(solution)/shard_map/ppermute | solution.py:1060
  127.5 21.1 %collective-permute-start.8 = (bf16[1024,1024]{1,0:T(8,128)(2,1)}, bf16[1024,1024]{1,0:T(8,128)(2,1)}, u32[]{:S(2)}, u32[]{:S(2)}) collective-permute-start(bf16[1024,1024]{1,0:T(8,128)(2,1)} %constant_dynamic-update-slice_fusion), channel_id=1, source_target_pairs={{0,1},{1,0},{2,3},{3,2},{4,5},{5,4},{6,7},{7,6},{8,9},{9,8},{10,11... | collective-permute-start | bytes 6291464 | tf_op jit(solution)/shard_map/ppermute | solution.py:1060
  131.7 38.2 %collective-permute-start.11 = (bf16[512,3072]{1,0:T(8,128)(2,1)}, bf16[512,3072]{1,0:T(8,128)(2,1)}, u32[]{:S(2)}, u32[]{:S(2)}) collective-permute-start(bf16[512,3072]{1,0:T(8,128)(2,1)} %pad_maximum_fusion), channel_id=1, source_target_pairs={{0,1},{1,0},{2,3},{3,2},{4,5},{5,4},{6,7},{7,6},{8,9},{9,8},{10,11... | collective-permute-start | bytes 9437192 | tf_op jit(solution)/shard_map/ppermute | solution.py:1060
  164.7 18.1 %all-to-all-start = ((bf16[8,256,128]{2,1,0:T(8,128)(2,1)}), bf16[8,256,128]{2,1,0:T(8,128)(2,1)S(1)}, u32[]{:S(2)}, u32[]{:S(2)}) async-start(bf16[8,256,128]{2,1,0:T(8,128)(2,1)} %bitcast.13), calls=%async_computation | async-start | bytes 1048576 | tf_op jit(solution)/shard_map/all_to_all | solution.py:1304
  169.9 167.7 %reduce-scatter.5.cloned.1.call-start = ((), (), s32[]{:S(2)}) async-start(), calls=%async_computation.7 | async-start | bytes 2621440 | tf_op jit(solution)/shard_map/reduce_scatter | solution.py:1338
  202.9 13.7 %collective-permute-start.13 = (bf16[256,1024]{1,0:T(8,128)(2,1)S(1)}, bf16[256,1024]{1,0:T(8,128)(2,1)S(1)}, u32[]{:S(2)}, u32[]{:S(2)}) collective-permute-start(bf16[256,1024]{1,0:T(8,128)(2,1)S(1)} %get-tuple-element.136), channel_id=1, source_target_pairs={{0,4},{4,0},{1,5},{5,1},{2,6},{6,2},{3,7},{7,3},{8,12},{12,8},{9,1... | collective-permute-start | bytes 1572872 | tf_op jit(solution)/shard_map/ppermute | solution.py:1060
  204.6 13.6 %collective-permute-start.14 = (bf16[256,1024]{1,0:T(8,128)(2,1)S(1)}, bf16[256,1024]{1,0:T(8,128)(2,1)S(1)}, u32[]{:S(2)}, u32[]{:S(2)}) collective-permute-start(bf16[256,1024]{1,0:T(8,128)(2,1)S(1)} %get-tuple-element.136), channel_id=1, source_target_pairs={{0,2},{2,0},{1,3},{3,1},{4,6},{6,4},{5,7},{7,5},{8,10},{10,8},{9,1... | collective-permute-start | bytes 1572872 | tf_op jit(solution)/shard_map/ppermute | solution.py:1060
  216.6 7.2 %collective-permute-start.15 = (bf16[128,1024]{1,0:T(8,128)(2,1)S(1)}, bf16[128,1024]{1,0:T(8,128)(2,1)S(1)}, u32[]{:S(2)}, u32[]{:S(2)}) collective-permute-start(bf16[128,1024]{1,0:T(8,128)(2,1)S(1)} %slice.452), channel_id=1, source_target_pairs={{0,2},{2,0},{1,3},{3,1},{4,6},{6,4},{5,7},{7,5},{8,10},{10,8},{9,1... | collective-permute-start | bytes 786440 | tf_op jit(solution)/shard_map/ppermute | solution.py:1060
  218.3 6.8 %collective-permute-start.16 = (bf16[128,1024]{1,0:T(8,128)(2,1)S(1)}, bf16[128,1024]{1,0:T(8,128)(2,1)S(1)}, u32[]{:S(2)}, u32[]{:S(2)}) collective-permute-start(bf16[128,1024]{1,0:T(8,128)(2,1)S(1)} %slice.453), channel_id=1, source_target_pairs={{0,4},{4,0},{1,5},{5,1},{2,6},{6,2},{3,7},{7,3},{8,12},{12,8},{9,1... | collective-permute-start | bytes 786440 | tf_op jit(solution)/shard_map/ppermute | solution.py:1060
  225.1 5.8 collective-permute-start.17
  246.4 25.3 %collective-permute-start.18 = (bf16[1024,1024]{1,0:T(8,128)(2,1)}, bf16[1024,1024]{1,0:T(8,128)(2,1)S(1)}, u32[]{:S(2)}, u32[]{:S(2)}) collective-permute-start(bf16[1024,1024]{1,0:T(8,128)(2,1)} %get-tuple-element.74), channel_id=1, source_target_pairs={{0,1},{1,0},{2,3},{3,2},{4,5},{5,4},{6,7},{7,6},{8,9},{9,8},{10,11... | collective-permute-start | bytes 6291464 | tf_op jit(solution)/shard_map/ppermute | solution.py:1060
  276.5 12.1 %collective-permute-start.19 = (bf16[128,1024]{1,0:T(8,128)(2,1)}, bf16[128,1024]{1,0:T(8,128)(2,1)}, u32[]{:S(2)}, u32[]{:S(2)}) collective-permute-start(bf16[128,1024]{1,0:T(8,128)(2,1)} %get-tuple-element.164), channel_id=1, source_target_pairs={{0,2},{2,0},{1,3},{3,1},{4,6},{6,4},{5,7},{7,5},{8,10},{10,8},{9,1... | collective-permute-start | bytes 786440 | tf_op jit(solution)/shard_map/ppermute | solution.py:1060
  277.5 11.1 %collective-permute-start.20 = (bf16[128,1024]{1,0:T(8,128)(2,1)}, bf16[128,1024]{1,0:T(8,128)(2,1)}, u32[]{:S(2)}, u32[]{:S(2)}) collective-permute-start(bf16[128,1024]{1,0:T(8,128)(2,1)} %get-tuple-element.163), channel_id=1, source_target_pairs={{0,4},{4,0},{1,5},{5,1},{2,6},{6,2},{3,7},{7,3},{8,12},{12,8},{9,1... | collective-permute-start | bytes 786440 | tf_op jit(solution)/shard_map/ppermute | solution.py:1060
  279.4 201.4 %reduce-scatter.11.cloned.1.call-start = ((), (), s32[]{:S(2)}) async-start(), calls=%async_computation.10 | async-start | bytes 2621440 | tf_op jit(solution)/shard_map/reduce_scatter | solution.py:1339
  291.2 13.4 %collective-permute-start.21 = (bf16[256,1024]{1,0:T(8,128)(2,1)S(1)}, bf16[256,1024]{1,0:T(8,128)(2,1)S(1)}, u32[]{:S(2)}, u32[]{:S(2)}) collective-permute-start(bf16[256,1024]{1,0:T(8,128)(2,1)S(1)} %pad_maximum_fusion.7), channel_id=1, source_target_pairs={{0,4},{4,0},{1,5},{5,1},{2,6},{6,2},{3,7},{7,3},{8,12},{12,8},{9,1... | collective-permute-start | bytes 1572872 | tf_op jit(solution)/shard_map/ppermute | solution.py:1060
  292.3 13.2 %collective-permute-start.22 = (bf16[256,1024]{1,0:T(8,128)(2,1)S(1)}, bf16[256,1024]{1,0:T(8,128)(2,1)S(1)}, u32[]{:S(2)}, u32[]{:S(2)}) collective-permute-start(bf16[256,1024]{1,0:T(8,128)(2,1)S(1)} %pad_maximum_fusion.8), channel_id=1, source_target_pairs={{0,2},{2,0},{1,3},{3,1},{4,6},{6,4},{5,7},{7,5},{8,10},{10,8},{9,1... | collective-permute-start | bytes 1572872 | tf_op jit(solution)/shard_map/ppermute | solution.py:1060
  326.7 10.9 %collective-permute-start.23 = (bf16[2,2,2,512,128]{4,3,2,1,0:T(8,128)(2,1)S(1)}, bf16[2,2,2,512,128]{4,3,2,1,0:T(8,128)(2,1)}, u32[]{:S(2)}, u32[]{:S(2)}) collective-permute-start(bf16[2,2,2,512,128]{4,3,2,1,0:T(8,128)(2,1)S(1)} %dynamic-slice_bitcast_fusion), channel_id=1, source_target_pairs={{0,1},{1,0},{2,3},{3,2},{4,5},{5,4},{6,7},{7,6},{8,9},{9,8},{10,11... | collective-permute-start | bytes 3145736 | tf_op jit(solution)/shard_map/ppermute | solution.py:1060
  342.5 17.0 %collective-permute-start.25 = (bf16[2,2,4,3,256,128]{5,4,3,2,1,0:T(8,128)(2,1)}, bf16[2,2,4,3,256,128]{5,4,3,2,1,0:T(8,128)(2,1)}, u32[]{:S(2)}, u32[]{:S(2)}) collective-permute-start(bf16[2,2,4,3,256,128]{5,4,3,2,1,0:T(8,128)(2,1)} %get-tuple-element.95), channel_id=1, source_target_pairs={{0,1},{1,0},{2,3},{3,2},{4,5},{5,4},{6,7},{7,6},{8,9},{9,8},{10,11... | collective-permute-start | bytes 9437192 | tf_op jit(solution)/shard_map/ppermute | solution.py:1060
  342.5 11.5 %collective-permute-start.26 = (bf16[1024,1024]{1,0:T(8,128)(2,1)}, bf16[1024,1024]{1,0:T(8,128)(2,1)}, u32[]{:S(2)}, u32[]{:S(2)}) collective-permute-start(bf16[1024,1024]{1,0:T(8,128)(2,1)} %convolution_convert_fusion.1), channel_id=1, source_target_pairs={{0,1},{1,0},{2,3},{3,2},{4,5},{5,4},{6,7},{7,6},{8,9},{9,8},{10,11... | collective-permute-start | bytes 6291464 | tf_op jit(solution)/shard_map/ppermute | solution.py:1060
  345.3 19.0 %all-to-all-start.1 = ((bf16[256,8,128]{2,0,1:T(8,128)(2,1)}), bf16[256,8,128]{2,0,1:T(8,128)(2,1)S(1)}, u32[]{:S(2)}, u32[]{:S(2)}) async-start(bf16[256,8,128]{2,0,1:T(8,128)(2,1)} %copy_bitcast_fusion.1), calls=%async_computation.2 | async-start | bytes 1048576 | tf_op jit(solution)/shard_map/all_to_all | solution.py:1370
  349.8 181.7 %reduce-scatter.7.cloned.1.call-start = ((), (), s32[]{:S(2)}) async-start(), calls=%async_computation.8 | async-start | bytes 1638400 | tf_op jit(solution)/shard_map/reduce_scatter | solution.py:1445
  353.8 14.4 %collective-permute-start.24 = (bf16[2,2,512,128]{3,2,1,0:T(8,128)(2,1)}, bf16[2,2,512,128]{3,2,1,0:T(8,128)(2,1)S(1)}, u32[]{:S(2)}, u32[]{:S(2)}) collective-permute-start(bf16[2,2,512,128]{3,2,1,0:T(8,128)(2,1)} %dynamic-slice_bitcast_fusion.4), channel_id=1, source_target_pairs={{0,2},{2,0},{1,3},{3,1},{4,6},{6,4},{5,7},{7,5},{8,10},{10,8},{9,1... | collective-permute-start | bytes 1572872 | tf_op jit(solution)/shard_map/ppermute | solution.py:1060
  395.3 21.5 %collective-permute-start.27 = (bf16[128,1024]{1,0:T(8,128)(2,1)}, bf16[128,1024]{1,0:T(8,128)(2,1)}, u32[]{:S(2)}, u32[]{:S(2)}) collective-permute-start(bf16[128,1024]{1,0:T(8,128)(2,1)} %get-tuple-element.151), channel_id=1, source_target_pairs={{0,2},{2,0},{1,3},{3,1},{4,6},{6,4},{5,7},{7,5},{8,10},{10,8},{9,1... | collective-permute-start | bytes 786440 | tf_op jit(solution)/shard_map/ppermute | solution.py:1060
  397.0 23.7 %collective-permute-start.34 = (bf16[128,1024]{1,0:T(8,128)(2,1)}, bf16[128,1024]{1,0:T(8,128)(2,1)}, u32[]{:S(2)}, u32[]{:S(2)}) collective-permute-start(bf16[128,1024]{1,0:T(8,128)(2,1)} %get-tuple-element.152), channel_id=1, source_target_pairs={{0,4},{4,0},{1,5},{5,1},{2,6},{6,2},{3,7},{7,3},{8,12},{12,8},{9,1... | collective-permute-start | bytes 786440 | tf_op jit(solution)/shard_map/ppermute | solution.py:1060
  398.5 26.1 %collective-permute-start.28 = (bf16[1024,1024]{1,0:T(8,128)(2,1)}, bf16[1024,1024]{1,0:T(8,128)(2,1)S(1)}, u32[]{:S(2)}, u32[]{:S(2)}) collective-permute-start(bf16[1024,1024]{1,0:T(8,128)(2,1)} %convolution_convert_fusion), channel_id=1, source_target_pairs={{0,1},{1,0},{2,3},{3,2},{4,5},{5,4},{6,7},{7,6},{8,9},{9,8},{10,11... | collective-permute-start | bytes 6291464 | tf_op jit(solution)/shard_map/ppermute | solution.py:1060
  402.4 11.5 %collective-permute-start.38 = (bf16[2,512,128]{2,1,0:T(8,128)(2,1)}, bf16[2,512,128]{2,1,0:T(8,128)(2,1)}, u32[]{:S(2)}, u32[]{:S(2)}) collective-permute-start(bf16[2,512,128]{2,1,0:T(8,128)(2,1)} %dynamic-slice_bitcast_fusion.17), channel_id=1, source_target_pairs={{0,4},{4,0},{1,5},{5,1},{2,6},{6,2},{3,7},{7,3},{8,12},{12,8},{9,1... | collective-permute-start | bytes 786440 | tf_op jit(solution)/shard_map/ppermute | solution.py:1060
  404.4 79.6 %collective-permute-start.53 = (bf16[2,2,3,256,128]{4,3,2,1,0:T(8,128)(2,1)}, bf16[2,2,3,256,128]{4,3,2,1,0:T(8,128)(2,1)}, u32[]{:S(2)}, u32[]{:S(2)}) collective-permute-start(bf16[2,2,3,256,128]{4,3,2,1,0:T(8,128)(2,1)} %dynamic-slice_bitcast_fusion.1), channel_id=1, source_target_pairs={{0,4},{4,0},{1,5},{5,1},{2,6},{6,2},{3,7},{7,3},{8,12},{12,8},{9,1... | collective-permute-start | bytes 2359304 | tf_op jit(solution)/shard_map/ppermute | solution.py:1060
  413.9 71.6 %collective-permute-start.51 = (bf16[2,2,3,256,128]{4,3,2,1,0:T(8,128)(2,1)}, bf16[2,2,3,256,128]{4,3,2,1,0:T(8,128)(2,1)}, u32[]{:S(2)}, u32[]{:S(2)}) collective-permute-start(bf16[2,2,3,256,128]{4,3,2,1,0:T(8,128)(2,1)} %dynamic-slice_bitcast_fusion.2), channel_id=1, source_target_pairs={{0,2},{2,0},{1,3},{3,1},{4,6},{6,4},{5,7},{7,5},{8,10},{10,8},{9,1... | collective-permute-start | bytes 2359304 | tf_op jit(solution)/shard_map/ppermute | solution.py:1060
  416.9 28.9 %collective-permute-start.56 = (bf16[256,1024]{1,0:T(8,128)(2,1)S(1)}, bf16[256,1024]{1,0:T(8,128)(2,1)S(1)}, u32[]{:S(2)}, u32[]{:S(2)}) collective-permute-start(bf16[256,1024]{1,0:T(8,128)(2,1)S(1)} %broadcast_add_fusion), channel_id=1, source_target_pairs={{0,0},{1,8},{2,16},{3,24},{4,4},{5,12},{6,20},{7,28},{8,1},{9,9},{... | collective-permute-start | bytes 1572872 | tf_op jit(solution)/shard_map/ppermute | solution.py:1083
  428.6 21.9 %collective-permute-start.29 = (bf16[128,1024]{1,0:T(8,128)(2,1)S(1)}, bf16[128,1024]{1,0:T(8,128)(2,1)S(1)}, u32[]{:S(2)}, u32[]{:S(2)}) collective-permute-start(bf16[128,1024]{1,0:T(8,128)(2,1)S(1)} %get-tuple-element.157), channel_id=1, source_target_pairs={{0,2},{2,0},{1,3},{3,1},{4,6},{6,4},{5,7},{7,5},{8,10},{10,8},{9,1... | collective-permute-start | bytes 786440 | tf_op jit(solution)/shard_map/ppermute | solution.py:1060
  428.6 21.8 %collective-permute-start.31 = (bf16[128,1024]{1,0:T(8,128)(2,1)S(1)}, bf16[128,1024]{1,0:T(8,128)(2,1)S(1)}, u32[]{:S(2)}, u32[]{:S(2)}) collective-permute-start(bf16[128,1024]{1,0:T(8,128)(2,1)S(1)} %get-tuple-element.158), channel_id=1, source_target_pairs={{0,4},{4,0},{1,5},{5,1},{2,6},{6,2},{3,7},{7,3},{8,12},{12,8},{9,1... | collective-permute-start | bytes 786440 | tf_op jit(solution)/shard_map/ppermute | solution.py:1060
  451.5 13.2 %collective-permute-start.32 = (bf16[256,1024]{1,0:T(8,128)(2,1)}, bf16[256,1024]{1,0:T(8,128)(2,1)}, u32[]{:S(2)}, u32[]{:S(2)}) collective-permute-start(bf16[256,1024]{1,0:T(8,128)(2,1)} %pad_maximum_fusion.10), channel_id=1, source_target_pairs={{0,2},{2,0},{1,3},{3,1},{4,6},{6,4},{5,7},{7,5},{8,10},{10,8},{9,1... | collective-permute-start | bytes 1572872 | tf_op jit(solution)/shard_map/ppermute | solution.py:1060
  452.3 13.2 %collective-permute-start.30 = (bf16[256,1024]{1,0:T(8,128)(2,1)}, bf16[256,1024]{1,0:T(8,128)(2,1)}, u32[]{:S(2)}, u32[]{:S(2)}) collective-permute-start(bf16[256,1024]{1,0:T(8,128)(2,1)} %pad_maximum_fusion.9), channel_id=1, source_target_pairs={{0,4},{4,0},{1,5},{5,1},{2,6},{6,2},{3,7},{7,3},{8,12},{12,8},{9,1... | collective-permute-start | bytes 1572872 | tf_op jit(solution)/shard_map/ppermute | solution.py:1060
  455.3 126.4 %reduce-scatter.9.cloned.1.call-start = ((), (), s32[]{:S(2)}) async-start(), calls=%async_computation.9 | async-start | bytes 983040 | tf_op jit(solution)/shard_map/reduce_scatter | solution.py:1453
  472.7 48.0 %collective-permute-start.35 = (bf16[256,1024]{1,0:T(8,128)(2,1)}, bf16[256,1024]{1,0:T(8,128)(2,1)}, u32[]{:S(2)}, u32[]{:S(2)}) collective-permute-start(bf16[256,1024]{1,0:T(8,128)(2,1)} %maximum_add_fusion.1), channel_id=1, source_target_pairs={{0,2},{2,0},{1,3},{3,1},{4,6},{6,4},{5,7},{7,5},{8,10},{10,8},{9,1... | collective-permute-start | bytes 1572872 | tf_op jit(solution)/shard_map/ppermute | solution.py:1060
  475.3 46.9 %collective-permute-start.33 = (bf16[256,1024]{1,0:T(8,128)(2,1)}, bf16[256,1024]{1,0:T(8,128)(2,1)}, u32[]{:S(2)}, u32[]{:S(2)}) collective-permute-start(bf16[256,1024]{1,0:T(8,128)(2,1)} %maximum_add_fusion), channel_id=1, source_target_pairs={{0,4},{4,0},{1,5},{5,1},{2,6},{6,2},{3,7},{7,3},{8,12},{12,8},{9,1... | collective-permute-start | bytes 1572872 | tf_op jit(solution)/shard_map/ppermute | solution.py:1060
  477.4 61.3 %collective-permute-start.37 = (bf16[256,1024]{1,0:T(8,128)(2,1)}, bf16[256,1024]{1,0:T(8,128)(2,1)}, u32[]{:S(2)}, u32[]{:S(2)}) collective-permute-start(bf16[256,1024]{1,0:T(8,128)(2,1)} %fusion.55), channel_id=1, source_target_pairs={{0,0},{1,8},{2,16},{3,24},{4,4},{5,12},{6,20},{7,28},{8,1},{9,9},{... | collective-permute-start | bytes 1572872 | tf_op jit(solution)/shard_map/ppermute | solution.py:1083
  485.5 15.3 %collective-permute-start.57 = (bf16[128,1024]{1,0:T(8,128)(2,1)S(1)}, bf16[128,1024]{1,0:T(8,128)(2,1)S(1)}, u32[]{:S(2)}, u32[]{:S(2)}) collective-permute-start(bf16[128,1024]{1,0:T(8,128)(2,1)S(1)} %dynamic-slice_bitcast_fusion.15), channel_id=1, source_target_pairs={{0,4},{4,0},{1,5},{5,1},{2,6},{6,2},{3,7},{7,3},{8,12},{12,8},{9,1... | collective-permute-start | bytes 786440 | tf_op jit(solution)/shard_map/ppermute | solution.py:1060
  488.0 8.1 %collective-permute-start.44 = (f32[21,1024]{1,0:T(8,128)S(1)}, f32[21,1024]{1,0:T(8,128)S(1)}, u32[]{:S(2)}, u32[]{:S(2)}) collective-permute-start(f32[21,1024]{1,0:T(8,128)S(1)} %fusion.116), channel_id=1, source_target_pairs={{0,2},{2,0},{1,3},{3,1},{4,6},{6,4},{5,7},{7,5},{8,10},{10,8},{9,1... | collective-permute-start | bytes 258056 | tf_op jit(solution)/shard_map/ppermute | solution.py:1060
  500.8 17.8 %collective-permute-start.39 = (bf16[2,2,64,1024]{3,2,1,0:T(8,128)(2,1)}, bf16[2,2,64,1024]{3,2,1,0:T(8,128)(2,1)}, u32[]{:S(2)}, u32[]{:S(2)}) collective-permute-start(bf16[2,2,64,1024]{3,2,1,0:T(8,128)(2,1)} %dynamic-slice_bitcast_fusion.3), channel_id=1, source_target_pairs={{0,1},{1,0},{2,3},{3,2},{4,5},{5,4},{6,7},{7,6},{8,9},{9,8},{10,11... | collective-permute-start | bytes 1572872 | tf_op jit(solution)/shard_map/ppermute | solution.py:1060
  500.8 5.3 collective-permute-start.46
  506.7 7.8 %collective-permute-start.47 = (f32[21,1024]{1,0:T(8,128)}, f32[21,1024]{1,0:T(8,128)}, u32[]{:S(2)}, u32[]{:S(2)}) collective-permute-start(f32[21,1024]{1,0:T(8,128)} %add.607), channel_id=1, source_target_pairs={{0,16},{8,24},{16,0},{24,8},{1,17},{9,25},{17,1},{25,9},{2,18},{10... | collective-permute-start | bytes 258056 | tf_op jit(solution)/shard_map/ppermute | solution.py:1060
  514.5 20.1 %collective-permute-start.54 = (bf16[2,3,256,128]{3,2,1,0:T(8,128)(2,1)S(1)}, bf16[2,3,256,128]{3,2,1,0:T(8,128)(2,1)}, u32[]{:S(2)}, u32[]{:S(2)}) collective-permute-start(bf16[2,3,256,128]{3,2,1,0:T(8,128)(2,1)S(1)} %dynamic-slice_bitcast_fusion.13), channel_id=1, source_target_pairs={{0,2},{2,0},{1,3},{3,1},{4,6},{6,4},{5,7},{7,5},{8,10},{10,8},{9,1... | collective-permute-start | bytes 1179656 | tf_op jit(solution)/shard_map/ppermute | solution.py:1060
  518.5 17.2 %collective-permute-start.52 = (bf16[2,3,256,128]{3,2,1,0:T(8,128)(2,1)}, bf16[2,3,256,128]{3,2,1,0:T(8,128)(2,1)}, u32[]{:S(2)}, u32[]{:S(2)}) collective-permute-start(bf16[2,3,256,128]{3,2,1,0:T(8,128)(2,1)} %dynamic-slice_bitcast_fusion.14), channel_id=1, source_target_pairs={{0,4},{4,0},{1,5},{5,1},{2,6},{6,2},{3,7},{7,3},{8,12},{12,8},{9,1... | collective-permute-start | bytes 1179656 | tf_op jit(solution)/shard_map/ppermute | solution.py:1060
  520.7 10.6 %collective-permute-start.40 = (bf16[2,64,1024]{2,1,0:T(8,128)(2,1)S(1)}, bf16[2,64,1024]{2,1,0:T(8,128)(2,1)S(1)}, u32[]{:S(2)}, u32[]{:S(2)}) collective-permute-start(bf16[2,64,1024]{2,1,0:T(8,128)(2,1)S(1)} %dynamic-slice_bitcast_fusion.16), channel_id=1, source_target_pairs={{0,2},{2,0},{1,3},{3,1},{4,6},{6,4},{5,7},{7,5},{8,10},{10,8},{9,1... | collective-permute-start | bytes 786440 | tf_op jit(solution)/shard_map/ppermute | solution.py:1060
  523.9 50.1 %collective-permute-start.36 = (bf16[256,1024]{1,0:T(8,128)(2,1)S(1)}, bf16[256,1024]{1,0:T(8,128)(2,1)S(1)}, u32[]{:S(2)}, u32[]{:S(2)}) collective-permute-start(bf16[256,1024]{1,0:T(8,128)(2,1)S(1)} %add_convert_fusion.4), channel_id=1, source_target_pairs={{0,0},{1,8},{2,16},{3,24},{4,4},{5,12},{6,20},{7,28},{8,1},{9,9},{... | collective-permute-start | bytes 1572872 | tf_op jit(solution)/shard_map/ppermute | solution.py:1083
  543.0 28.3 %collective-permute-start.42 = (bf16[64,1024]{1,0:T(8,128)(2,1)S(1)}, bf16[64,1024]{1,0:T(8,128)(2,1)S(1)}, u32[]{:S(2)}, u32[]{:S(2)}) collective-permute-start(bf16[64,1024]{1,0:T(8,128)(2,1)S(1)} %fusion.73), channel_id=1, source_target_pairs={{0,0},{1,8},{2,16},{3,24},{4,4},{5,12},{6,20},{7,28},{8,1},{9,9},{... | collective-permute-start | bytes 393224 | tf_op jit(solution)/shard_map/ppermute | solution.py:1083
  548.6 25.4 %collective-permute-start.50 = (bf16[256,128]{1,0:T(8,128)(2,1)S(1)}, bf16[256,128]{1,0:T(8,128)(2,1)S(1)}, u32[]{:S(2)}, u32[]{:S(2)}) collective-permute-start(bf16[256,128]{1,0:T(8,128)(2,1)S(1)} %get-tuple-element.184), channel_id=1, source_target_pairs={{1,0},{9,1},{17,2},{25,3},{6,4},{14,5},{22,6},{30,7},{0,8},{8,9},{... | collective-permute-start | bytes 196616 | tf_op jit(solution)/shard_map/ppermute | solution.py:1477
  550.5 23.5 %collective-permute-start.49 = (bf16[256,128]{1,0:T(8,128)(2,1)S(1)}, bf16[256,128]{1,0:T(8,128)(2,1)S(1)}, u32[]{:S(2)}, u32[]{:S(2)}) collective-permute-start(bf16[256,128]{1,0:T(8,128)(2,1)S(1)} %get-tuple-element.185), channel_id=1, source_target_pairs={{4,0},{12,1},{20,2},{28,3},{2,4},{10,5},{18,6},{26,7},{7,8},{15,9}... | collective-permute-start | bytes 196616 | tf_op jit(solution)/shard_map/ppermute | solution.py:1477
  551.5 23.8 %collective-permute-start.48 = (bf16[256,128]{1,0:T(8,128)(2,1)S(1)}, bf16[256,128]{1,0:T(8,128)(2,1)S(1)}, u32[]{:S(2)}, u32[]{:S(2)}) collective-permute-start(bf16[256,128]{1,0:T(8,128)(2,1)S(1)} %get-tuple-element.183), channel_id=1, source_target_pairs={{0,0},{8,1},{16,2},{24,3},{5,4},{13,5},{21,6},{29,7},{3,8},{11,9},... | collective-permute-start | bytes 196616 | tf_op jit(solution)/shard_map/ppermute | solution.py:1477
  571.4 9.6 %collective-permute-start.55 = (bf16[2,256,128]{2,1,0:T(8,128)(2,1)S(1)}, bf16[2,256,128]{2,1,0:T(8,128)(2,1)S(1)}, u32[]{:S(2)}, u32[]{:S(2)}) collective-permute-start(bf16[2,256,128]{2,1,0:T(8,128)(2,1)S(1)} %slice_bitcast_fusion.1), channel_id=1, source_target_pairs={{0,0},{1,8},{2,16},{3,24},{4,4},{5,12},{6,20},{7,28},{8,1},{9,9},{... | collective-permute-start | bytes 393224 | tf_op jit(solution)/shard_map/ppermute | solution.py:1083
  (73 other events, 584.6 us)
Sparse Core Ops, SparseCore 0:
  64.9 26.0 all-gather.5
  92.9 45.4 all-gather.7
  148.7 36.6 all-gather.9
  279.5 44.4 reduce-scatter.4
  343.9 44.1 reduce-scatter.10
  455.4 32.6 reduce-scatter.6
  538.0 33.0 reduce-scatter.8

commit v4 on v3

--- a/solution.py
+++ b/solution.py
@@ -750,16 +750,21 @@
         lax.fori_loop(0, pos_blocks, move, 0)
 
 
-def cross_forward_kernel(q_ref, key_ref, value_ref, low_ref, high_ref, out_ref):
+def cross_forward_kernel(q_ref, key_ref, value_ref, low_ref, high_ref, out_ref, bar_ref):
     rows, width = q_ref.shape[0], key_ref.shape[1]
     queries, keys, values = q_ref[...], key_ref[0], value_ref[0]
-    k_pos = lax.broadcasted_iota(jnp.int32, (rows, width), 1)
-    allowed = (k_pos >= low_ref[...]) & (k_pos < high_ref[...])
+
+    @pl.when(pl.program_id(0) == 0)
+    def _():
+        k_pos = lax.broadcasted_iota(jnp.int32, (rows, width), 1)
+        allowed = (k_pos >= low_ref[...]) & (k_pos < high_ref[...])
+        bar_ref[...] = jnp.where(allowed, 0.0, NEG)
+
     parts = []
     for head in range(2):
         picked = jnp.where(lane_mask(rows, head), queries, jnp.zeros_like(queries))
         scores = lax.dot_general(picked, keys, CONTRACT_COLS, preferred_element_type=jnp.float32)
-        scores = jnp.where(allowed, scores, NEG)
+        scores = scores + bar_ref[...]
         terms = jnp.exp(scores - jnp.max(scores, axis=1, keepdims=True))
         inverse = 1.0 / jnp.sum(terms, axis=1, keepdims=True)
         parts.append(
@@ -768,11 +773,16 @@
     out_ref[...] = jnp.where(lane_mask(rows, 0), parts[0], parts[1]).astype(jnp.bfloat16)
 
 
-def cross_backward_kernel(q_ref, key_ref, value_ref, grad_ref, low_ref, high_ref, dq_ref, dkv_ref):
+def cross_backward_kernel(q_ref, key_ref, value_ref, grad_ref, low_ref, high_ref, dq_ref, dkv_ref, bar_ref):
     rows, width = q_ref.shape[0], key_ref.shape[1]
     queries, keys, values, grads = q_ref[...], key_ref[0], value_ref[0], grad_ref[...]
-    k_pos = lax.broadcasted_iota(jnp.int32, (width, rows), 0)
-    allowed = (k_pos >= low_ref[...]) & (k_pos < high_ref[...])
+
+    @pl.when(pl.program_id(0) == 0)
+    def _():
+        k_pos = lax.broadcasted_iota(jnp.int32, (width, rows), 0)
+        allowed = (k_pos >= low_ref[...]) & (k_pos < high_ref[...])
+        bar_ref[...] = jnp.where(allowed, 0.0, NEG)
+
     dq_parts = []
     dkey = jnp.zeros((width, PAIR), jnp.float32)
     dvalue = jnp.zeros((width, PAIR), jnp.float32)
@@ -781,7 +791,7 @@
         picked = jnp.where(inside, queries, jnp.zeros_like(queries))
         grad = jnp.where(inside, grads, jnp.zeros_like(grads))
         scores = lax.dot_general(keys, picked, CONTRACT_COLS, preferred_element_type=jnp.float32)
-        scores = jnp.where(allowed, scores, NEG)
+        scores = scores + bar_ref[...]
         terms = jnp.exp(scores - jnp.max(scores, axis=0, keepdims=True))
         probs = terms * (1.0 / jnp.sum(terms, axis=0, keepdims=True))
         dprobs = lax.dot_general(values, grad, CONTRACT_COLS, preferred_element_type=jnp.float32)
@@ -858,6 +868,7 @@
         ],
         out_specs=pl.BlockSpec((rows, PAIR), lambda p: (0, p)),
         out_shape=jax.ShapeDtypeStruct((rows, features), jnp.bfloat16),
+        scratch_shapes=[pltpu.VMEM((rows, src), jnp.float32)],
         compiler_params=kernel_params(),
         cost_estimate=kernel_cost(1),
     )(queries, kv_cross, kv_cross, span_low[:, None], span_high[:, None])
@@ -886,6 +897,7 @@
             jax.ShapeDtypeStruct((rows, features), jnp.bfloat16),
             jax.ShapeDtypeStruct((2, pairs, src, PAIR), jnp.bfloat16),
         ],
+        scratch_shapes=[pltpu.VMEM((src, rows), jnp.float32)],
         compiler_params=kernel_params(),
         cost_estimate=kernel_cost(1),
     )(queries, kv_cross, kv_cross, grads, span_low[None, :], span_high[None, :])

time: 597 us -> 599 us (level)
  no operation moved by 1% of the time
where the time goes in v4:
time: 599 us; the launch traced here: 594 us
  waiting for transfers between devices  167 us (28%)
  Pallas kernels  107 us (18%)
  local copies, waits for them, and re-layouts  92.8 us (15%)
  starting transfers between devices  87.8 us (15%)
  other arithmetic  63.8 us (11%)
  matrix products  54.5 us (9%)
  between operations  21.6 us (4%)
    ppermute x47, waiting for transfers between devices, over(): return lax.ppermute(value, axis, [(i, i ^ distance) for i in range(count)])  97.8 us
    ppermute x8, waiting for transfers between devices, trade_places(): return lax.ppermute(value, ALL, pairs)  61.2 us
    ppermute x47, starting transfers between devices, over(): return lax.ppermute(value, axis, [(i, i ^ distance) for i in range(count)])  34.6 us
    ppermute x8, starting transfers between devices, trade_places(): return lax.ppermute(value, ALL, pairs)  33.7 us
    unnamed x153, local copies, waits for them, and re-layouts  28.2 us
    dot_general x8, matrix products, plain_dot(): return jnp.dot(left, right, preferred_element_type=jnp.float32)  26.8 us
    pallas_call x2, Pallas kernels, mlp_forward_back(): pl.pallas_call(mlp_kernel, grid=(rows // ROW_BLOCK,), in_specs=[pl.BlockS...  25.7 us
    convert_element_type x15, other arithmetic, low(): return value.astype(jnp.bfloat16)  20.7 us
  transfers between devices with their start and end apart: 67, of which 24 were waited for; matrix products, arithmetic and copies ran while one was open for 30% of the time, Pallas kernels for 13%

profile of v4, /device:TPU:2, one launch (start us, length us, event | category | flops | bytes accessed | tf_op | source)
XLA Modules:
  0.0 594.0 jit_solution(17521573890251782517)
XLA Ops:
  16.1 5.9 %collective-permute-start = (bf16[320,1024]{1,0:T(8,128)(2,1)}, bf16[320,1024]{1,0:T(8,128)(2,1)S(1)}, u32[]{:S(2)}, u32[]{:S(2)}) collective-permute-start(bf16[320,1024]{1,0:T(8,128)(2,1)} %pad_maximum_fusion.6), channel_id=1, source_target_pairs={{0,0},{1,8},{2,16},{3,24},{4,4},{5,12},{6,20},{7,28},{8,1},{9,9},{... | collective-permute-start | bytes 1966088 | tf_op jit(solution)/shard_map/ppermute | solution.py:1095
  24.1 3.3 shard_map.297
  30.7 5.7 collective-permute-start.12
  37.1 26.2 %collective-permute-done = bf16[320,1024]{1,0:T(8,128)(2,1)S(1)} collective-permute-done((bf16[320,1024]{1,0:T(8,128)(2,1)}, bf16[320,1024]{1,0:T(8,128)(2,1)S(1)}, u32[]{:S(2)}, u32[]{:S(2)}) %collective-permute-start) | collective-permute-done | bytes 655392 | tf_op jit(solution)/shard_map/ppermute | solution.py:1095
  73.4 3.4 broadcast_in_dim.102
  76.7 2.6 constant_dynamic-update-slice_fusion.19
  79.7 3.2 constant_dynamic-slice_fusion.1.down_ref
  87.3 6.2 %collective-permute-done.2 = bf16[256,1024]{1,0:T(8,128)(2,1)S(1)} collective-permute-done((bf16[256,1024]{1,0:T(8,128)(2,1)S(1)}, bf16[256,1024]{1,0:T(8,128)(2,1)S(1)}, u32[]{:S(2)}, u32[]{:S(2)}) %collective-permute-start.2) | collective-permute-done | bytes 524320 | tf_op jit(solution)/shard_map/ppermute | solution.py:1072
  93.6 24.1 %collective-permute-done.3 = bf16[256,1024]{1,0:T(8,128)(2,1)S(1)} collective-permute-done((bf16[256,1024]{1,0:T(8,128)(2,1)S(1)}, bf16[256,1024]{1,0:T(8,128)(2,1)S(1)}, u32[]{:S(2)}, u32[]{:S(2)}) %collective-permute-start.3) | collective-permute-done | bytes 524320 | tf_op jit(solution)/shard_map/ppermute | solution.py:1072
  123.5 3.3 collective-permute-done.5
  128.8 3.0 pad_maximum_fusion
  143.0 2.5 fusion.48
  145.5 3.0 multiply_convert_fusion.1
  148.6 3.0 multiply_convert_fusion
  151.8 13.1 %shard_map.298 = bf16[2048,128]{1,0:T(8,128)(2,1)} custom-call(s32[8]{0:T(128)S(1)} %bitcast_subtract_fusion.2.starts_ref, s32[1]{0:T(128)} %bitcast.5.own_ref, bf16[2048,384]{1,0:T(8,128)(2,1)S(1)} %pad_maximum_fusion.4.qkv_ref), custom_call_target="tpu_custom_call" | custom-call | flops 1150000000 | bytes 1048576 | tf_op jit(solution)/shard_map/pallas_call | solution.py:819
  165.0 5.3 all-to-all-start
  170.7 2.7 slice_dynamic-update-slice_fusion.1
  173.4 2.6 slice_dynamic-update-slice_fusion
  176.0 6.9 %all-to-all-done = bf16[8,256,128]{2,1,0:T(8,128)(2,1)S(1)} async-done(((bf16[8,256,128]{2,1,0:T(8,128)(2,1)}), bf16[8,256,128]{2,1,0:T(8,128)(2,1)S(1)}, u32[]{:S(2)}, u32[]{:S(2)}) %all-to-all-start) | async-done | bytes 524320 | tf_op jit(solution)/shard_map/all_to_all | solution.py:1316
  182.9 2.6 fusion.93
  190.0 9.4 %shard_map.299.refs_4_ = bf16[256,1024]{1,0:T(8,128)(2,1)S(1)} custom-call(bf16[256,1024]{1,0:T(8,128)(2,1)S(1)} %fusion.34.q_ref, bf16[8,512,256]{2,1,0:T(8,128)(2,1)S(1)} %bitcast.238, bf16[8,512,256]{2,1,0:T(8,128)(2,1)S(1)} %bitcast.239, s32[256,1]{1,0:T(8,128)S(1)} %copy.71.low_ref, s32[256,1]{1,0:T(8,128)S(1)} %copy.72.high_ref), custom_call_target="tpu_custom_call" | custom-call | flops 1150000000 | bytes 1048576 | tf_op jit(solution)/shard_map/pallas_call | solution.py:859
  199.4 2.6 fusion.94
  205.8 10.9 %collective-permute-done.13 = bf16[256,1024]{1,0:T(8,128)(2,1)S(1)} collective-permute-done((bf16[256,1024]{1,0:T(8,128)(2,1)S(1)}, bf16[256,1024]{1,0:T(8,128)(2,1)S(1)}, u32[]{:S(2)}, u32[]{:S(2)}) %collective-permute-start.13) | collective-permute-done | bytes 524320 | tf_op jit(solution)/shard_map/ppermute | solution.py:1072
  220.1 4.3 collective-permute-done.15
  226.7 2.6 dynamic-slice_bitcast_fusion.12
  231.6 12.8 %shard_map.301 = (bf16[1024,1024]{1,0:T(8,128)(2,1)S(1)}, bf16[1024,1024]{1,0:T(8,128)(2,1)S(1)}, bf16[1024,1024]{1,0:T(8,128)(2,1)}, f32[1,1024]{1,0:T(1,128)S(1)}) custom-call(bf16[1024,1024]{1,0:T(8,128)(2,1)} %collective-permute-done.17.act_ref.left_two_ref, bf16[1024,1024]{1,0:T(8,128)(2,1)} %get-tuple-element.82.grad_ref.left_two_ref, ...), custom_call_target="tpu_custom_call" | custom-call | flops 1150000000 | bytes 1048576 | tf_op jit(solution)/shard_map/pallas_call | solution.py:938
  247.5 12.9 %shard_map.300 = (bf16[1024,1024]{1,0:T(8,128)(2,1)S(1)}, bf16[1024,1024]{1,0:T(8,128)(2,1)S(1)}, bf16[1024,1024]{1,0:T(8,128)(2,1)}, f32[1,1024]{1,0:T(1,128)S(1)}) custom-call(bf16[1024,1024]{1,0:T(8,128)(2,1)} %copy-done.6, bf16[1024,1024]{1,0:T(8,128)(2,1)} %get-tuple-element.80.grad_ref.left_ref, ...), custom_call_target="tpu_custom_call" | custom-call | flops 1150000000 | bytes 1048576 | tf_op jit(solution)/shard_map/pallas_call | solution.py:938
  263.1 8.0 %shard_map.302 = bf16[1024,1024]{1,0:T(8,128)(2,1)S(1)} custom-call(bf16[1024,1024]{1,0:T(8,128)(2,1)S(1)} %copy-done.7, bf16[1024,1024]{1,0:T(8,128)(2,1)} %copy-done.14, bf16[1024,1024]{1,0:T(8,128)(2,1)} %collective-permute-done.17.act_ref.left_two_ref, bf16[1024,1024]{1,0:T(8,128)(2,1)} %copy-done.13), custom_call_target="tpu_custom_call" | custom-call | flops 1150000000 | bytes 1048576 | tf_op jit(solution)/shard_map/pallas_call | solution.py:992
  272.4 2.5 add_convert_fusion.3
  280.2 9.1 %shard_map.303 = bf16[1024,1024]{1,0:T(8,128)(2,1)} custom-call(bf16[1024,1024]{1,0:T(8,128)(2,1)S(1)} %copy-done.2, bf16[1024,1024]{1,0:T(8,128)(2,1)} %copy-done.9, bf16[1024,1024]{1,0:T(8,128)(2,1)} %get-tuple-element.82.grad_ref.left_two_ref, bf16[1024,1024]{1,0:T(8,128)(2,1)} %copy-done.11), custom_call_target="tpu_custom_call" | custom-call | flops 1150000000 | bytes 1048576 | tf_op jit(solution)/shard_map/pallas_call | solution.py:992
  294.1 5.2 convolution_convert_fusion.1
  299.4 6.0 %collective-permute-done.21 = bf16[256,1024]{1,0:T(8,128)(2,1)S(1)} collective-permute-done((bf16[256,1024]{1,0:T(8,128)(2,1)S(1)}, bf16[256,1024]{1,0:T(8,128)(2,1)S(1)}, u32[]{:S(2)}, u32[]{:S(2)}) %collective-permute-start.21) | collective-permute-done | bytes 524320 | tf_op jit(solution)/shard_map/ppermute | solution.py:1072
  309.8 3.1 convert_reduce_fusion.4
  312.9 14.5 %shard_map.304 = (bf16[256,1024]{1,0:T(8,128)(2,1)S(1)}, bf16[2,8,512,128]{3,2,1,0:T(8,128)(2,1)S(1)}) custom-call(bf16[256,1024]{1,0:T(8,128)(2,1)S(1)} %fusion.34.q_ref, bf16[8,512,256]{2,1,0:T(8,128)(2,1)S(1)} %bitcast.240, bf16[8,512,256]{2,1,0:T(8,128)(2,1)S(1)} %bitcast.241, bf16[256,1024]{1,0:T(8,128)(2,1)S(1)} %get-tuple-element.217.grad_ref, ...), custom_call_target="tpu_custom_call" | custom-call | flops 1150000000 | bytes 1048576 | tf_op jit(solution)/shard_map/pallas_call | solution.py:881
  329.4 3.3 multiply_reduce_fusion.1
  334.6 3.8 convert_reduce_fusion.7
  338.5 4.8 shard_map.305
  346.1 4.3 all-to-all-start.1
  354.5 5.5 add_convert_fusion.2
  360.0 4.8 add_convert_fusion
  364.8 4.0 collective-permute-done.24
  368.9 18.8 %shard_map.306 = bf16[2048,384]{1,0:T(8,128)(2,1)S(1)} custom-call(s32[8]{0:T(128)S(1)} %bitcast_subtract_fusion.2.starts_ref, s32[1]{0:T(128)} %bitcast.5.own_ref, bf16[2048,384]{1,0:T(8,128)(2,1)S(1)} %copy-done.17, bf16[2048,128]{1,0:T(8,128)(2,1)S(1)} %bitcast.244), custom_call_target="tpu_custom_call" | custom-call | flops 1150000000 | bytes 1048576 | tf_op jit(solution)/shard_map/pallas_call | solution.py:837
  387.7 3.7 convolution_convert_fusion
  391.8 3.9 fusion.67
  399.7 3.0 fusion.63
  407.1 4.0 fusion.14
  418.1 4.7 collective-permute-start.56
  424.2 2.5 convolution_convert_fusion.2
  428.0 2.5 add_convert_fusion.1
  432.1 14.7 %collective-permute-done.56 = bf16[256,1024]{1,0:T(8,128)(2,1)S(1)} collective-permute-done((bf16[256,1024]{1,0:T(8,128)(2,1)S(1)}, bf16[256,1024]{1,0:T(8,128)(2,1)S(1)}, u32[]{:S(2)}, u32[]{:S(2)}) %collective-permute-start.56) | collective-permute-done | bytes 524320 | tf_op jit(solution)/shard_map/ppermute | solution.py:1095
  448.0 3.6 collective-permute-done.29
  458.9 7.0 %collective-permute-done.32 = bf16[256,1024]{1,0:T(8,128)(2,1)} collective-permute-done((bf16[256,1024]{1,0:T(8,128)(2,1)}, bf16[256,1024]{1,0:T(8,128)(2,1)}, u32[]{:S(2)}, u32[]{:S(2)}) %collective-permute-start.32) | collective-permute-done | bytes 524320 | tf_op jit(solution)/shard_map/ppermute | solution.py:1072
  478.6 4.3 collective-permute-start.37
  492.1 5.2 collective-permute-done.44
  499.0 3.0 collective-permute-done.45
  502.2 5.1 collective-permute-done.46
  510.4 5.4 collective-permute-done.47
  525.2 3.2 collective-permute-start.36
  528.4 3.9 collective-permute-done.40
  541.5 2.4 collective-permute-done.41
  544.0 6.0 %collective-permute-start.42 = (bf16[64,1024]{1,0:T(8,128)(2,1)S(1)}, bf16[64,1024]{1,0:T(8,128)(2,1)S(1)}, u32[]{:S(2)}, u32[]{:S(2)}) collective-permute-start(bf16[64,1024]{1,0:T(8,128)(2,1)S(1)} %fusion.73), channel_id=1, source_target_pairs={{0,0},{1,8},{2,16},{3,24},{4,4},{5,12},{6,20},{7,28},{8,1},{9,9},{... | collective-permute-start | bytes 393224 | tf_op jit(solution)/shard_map/ppermute | solution.py:1095
  553.5 5.7 collective-permute-start.48
  559.3 14.8 %collective-permute-done.42 = bf16[64,1024]{1,0:T(8,128)(2,1)S(1)} collective-permute-done((bf16[64,1024]{1,0:T(8,128)(2,1)S(1)}, bf16[64,1024]{1,0:T(8,128)(2,1)S(1)}, u32[]{:S(2)}, u32[]{:S(2)}) %collective-permute-start.42) | collective-permute-done | bytes 131104 | tf_op jit(solution)/shard_map/ppermute | solution.py:1095
  578.0 5.6 collective-permute-done.55
  (430 shorter events, 176.0 us)
Async XLA Ops:
  7.2 135.9 %all-gather.6.cloned.1.call-start = ((), (), s32[]{:S(2)}) async-start(), calls=%async_computation.6 | async-start | bytes 1179648 | tf_op jit(solution)/shard_map/all_gather | solution.py:1292
  14.2 72.1 %collective-permute-start.9 = (bf16[128,3072]{1,0:T(8,128)(2,1)}, bf16[128,3072]{1,0:T(8,128)(2,1)}, u32[]{:S(2)}, u32[]{:S(2)}) collective-permute-start(bf16[128,3072]{1,0:T(8,128)(2,1)} %constant_dynamic-slice_fusion), channel_id=1, source_target_pairs={{0,2},{2,0},{1,3},{3,1},{4,6},{6,4},{5,7},{7,5},{8,10},{10,8},{9,1... | collective-permute-start | bytes 2359304 | tf_op jit(solution)/shard_map/ppermute | solution.py:1072
  16.1 47.1 %collective-permute-start = (bf16[320,1024]{1,0:T(8,128)(2,1)}, bf16[320,1024]{1,0:T(8,128)(2,1)S(1)}, u32[]{:S(2)}, u32[]{:S(2)}) collective-permute-start(bf16[320,1024]{1,0:T(8,128)(2,1)} %pad_maximum_fusion.6), channel_id=1, source_target_pairs={{0,0},{1,8},{2,16},{3,24},{4,4},{5,12},{6,20},{7,28},{8,1},{9,9},{... | collective-permute-start | bytes 1966088 | tf_op jit(solution)/shard_map/ppermute | solution.py:1095
  22.1 42.7 %collective-permute-start.1 = (s32[2,8]{1,0:T(2,128)S(1)}, s32[2,8]{1,0:T(2,128)S(1)}, u32[]{:S(2)}, u32[]{:S(2)}) collective-permute-start(s32[2,8]{1,0:T(2,128)S(1)} %pad_add_fusion), channel_id=1, source_target_pairs={{0,0},{1,8},{2,16},{3,24},{4,4},{5,12},{6,20},{7,28},{8,1},{9,9},{... | collective-permute-start | bytes 200 | tf_op jit(solution)/shard_map/ppermute | solution.py:1095
  30.7 90.3 %collective-permute-start.6 = (bf16[512,1664]{1,0:T(8,128)(2,1)}, bf16[512,1664]{1,0:T(8,128)(2,1)}, u32[]{:S(2)}, u32[]{:S(2)}) collective-permute-start(bf16[512,1664]{1,0:T(8,128)(2,1)} %slice.434), channel_id=1, source_target_pairs={{0,2},{2,0},{1,3},{3,1},{4,6},{6,4},{5,7},{7,5},{8,10},{10,8},{9,1... | collective-permute-start | bytes 5111816 | tf_op jit(solution)/shard_map/ppermute | solution.py:1072
  30.7 48.7 %collective-permute-start.12 = (bf16[256,1024]{1,0:T(8,128)(2,1)}, bf16[256,1024]{1,0:T(8,128)(2,1)}, u32[]{:S(2)}, u32[]{:S(2)}) collective-permute-start(bf16[256,1024]{1,0:T(8,128)(2,1)} %bitcast.20), channel_id=1, source_target_pairs={{0,0},{1,8},{2,16},{3,24},{4,4},{5,12},{6,20},{7,28},{8,1},{9,9},{... | collective-permute-start | bytes 1572872 | tf_op jit(solution)/shard_map/ppermute | solution.py:1095
  64.8 83.8 %all-gather.8.cloned.1.call-start = ((), (), s32[]{:S(2)}) async-start(), calls=%async_computation.11 | async-start | bytes 4718592 | tf_op jit(solution)/shard_map/all_gather | solution.py:1295
  79.4 108.9 %all-gather.10.cloned.1.call-start = ((), (), s32[]{:S(2)}) async-start(), calls=%async_computation.12 | async-start | bytes 2359296 | tf_op jit(solution)/shard_map/all_gather | solution.py:1312
  84.3 9.2 %collective-permute-start.2 = (bf16[256,1024]{1,0:T(8,128)(2,1)S(1)}, bf16[256,1024]{1,0:T(8,128)(2,1)S(1)}, u32[]{:S(2)}, u32[]{:S(2)}) collective-permute-start(bf16[256,1024]{1,0:T(8,128)(2,1)S(1)} %get-tuple-element.138), channel_id=1, source_target_pairs={{0,4},{4,0},{1,5},{5,1},{2,6},{6,2},{3,7},{7,3},{8,12},{12,8},{9,1... | collective-permute-start | bytes 1572872 | tf_op jit(solution)/shard_map/ppermute | solution.py:1072
  85.9 31.9 %collective-permute-start.3 = (bf16[256,1024]{1,0:T(8,128)(2,1)S(1)}, bf16[256,1024]{1,0:T(8,128)(2,1)S(1)}, u32[]{:S(2)}, u32[]{:S(2)}) collective-permute-start(bf16[256,1024]{1,0:T(8,128)(2,1)S(1)} %get-tuple-element.138), channel_id=1, source_target_pairs={{0,2},{2,0},{1,3},{3,1},{4,6},{6,4},{5,7},{7,5},{8,10},{10,8},{9,1... | collective-permute-start | bytes 1572872 | tf_op jit(solution)/shard_map/ppermute | solution.py:1072
  86.3 41.2 %collective-permute-start.10 = (bf16[128,3072]{1,0:T(8,128)(2,1)}, bf16[128,3072]{1,0:T(8,128)(2,1)S(1)}, u32[]{:S(2)}, u32[]{:S(2)}) collective-permute-start(bf16[128,3072]{1,0:T(8,128)(2,1)} %collective-permute-done.9), channel_id=1, source_target_pairs={{0,4},{4,0},{1,5},{5,1},{2,6},{6,2},{3,7},{7,3},{8,12},{12,8},{9,1... | collective-permute-start | bytes 2359304 | tf_op jit(solution)/shard_map/ppermute | solution.py:1072
  93.5 29.2 %collective-permute-start.4 = (bf16[128,1024]{1,0:T(8,128)(2,1)S(1)}, bf16[128,1024]{1,0:T(8,128)(2,1)S(1)}, u32[]{:S(2)}, u32[]{:S(2)}) collective-permute-start(bf16[128,1024]{1,0:T(8,128)(2,1)S(1)} %slice.430), channel_id=1, source_target_pairs={{0,2},{2,0},{1,3},{3,1},{4,6},{6,4},{5,7},{7,5},{8,10},{10,8},{9,1... | collective-permute-start | bytes 786440 | tf_op jit(solution)/shard_map/ppermute | solution.py:1072
  117.7 9.0 %collective-permute-start.5 = (bf16[128,1024]{1,0:T(8,128)(2,1)S(1)}, bf16[128,1024]{1,0:T(8,128)(2,1)S(1)}, u32[]{:S(2)}, u32[]{:S(2)}) collective-permute-start(bf16[128,1024]{1,0:T(8,128)(2,1)S(1)} %slice.431), channel_id=1, source_target_pairs={{0,4},{4,0},{1,5},{5,1},{2,6},{6,2},{3,7},{7,3},{8,12},{12,8},{9,1... | collective-permute-start | bytes 786440 | tf_op jit(solution)/shard_map/ppermute | solution.py:1072
  122.6 10.9 %collective-permute-start.7 = (bf16[512,1664]{1,0:T(8,128)(2,1)S(1)}, bf16[512,1664]{1,0:T(8,128)(2,1)S(1)}, u32[]{:S(2)}, u32[]{:S(2)}) collective-permute-start(bf16[512,1664]{1,0:T(8,128)(2,1)S(1)} %pad_maximum_fusion.3), channel_id=1, source_target_pairs={{0,1},{1,0},{2,3},{3,2},{4,5},{5,4},{6,7},{7,6},{8,9},{9,8},{10,11... | collective-permute-start | bytes 5111816 | tf_op jit(solution)/shard_map/ppermute | solution.py:1072
  127.5 21.1 %collective-permute-start.8 = (bf16[1024,1024]{1,0:T(8,128)(2,1)}, bf16[1024,1024]{1,0:T(8,128)(2,1)}, u32[]{:S(2)}, u32[]{:S(2)}) collective-permute-start(bf16[1024,1024]{1,0:T(8,128)(2,1)} %constant_dynamic-update-slice_fusion), channel_id=1, source_target_pairs={{0,1},{1,0},{2,3},{3,2},{4,5},{5,4},{6,7},{7,6},{8,9},{9,8},{10,11... | collective-permute-start | bytes 6291464 | tf_op jit(solution)/shard_map/ppermute | solution.py:1072
  131.7 38.9 %collective-permute-start.11 = (bf16[512,3072]{1,0:T(8,128)(2,1)}, bf16[512,3072]{1,0:T(8,128)(2,1)}, u32[]{:S(2)}, u32[]{:S(2)}) collective-permute-start(bf16[512,3072]{1,0:T(8,128)(2,1)} %pad_maximum_fusion), channel_id=1, source_target_pairs={{0,1},{1,0},{2,3},{3,2},{4,5},{5,4},{6,7},{7,6},{8,9},{9,8},{10,11... | collective-permute-start | bytes 9437192 | tf_op jit(solution)/shard_map/ppermute | solution.py:1072
  165.0 17.9 %all-to-all-start = ((bf16[8,256,128]{2,1,0:T(8,128)(2,1)}), bf16[8,256,128]{2,1,0:T(8,128)(2,1)S(1)}, u32[]{:S(2)}, u32[]{:S(2)}) async-start(bf16[8,256,128]{2,1,0:T(8,128)(2,1)} %bitcast.13), calls=%async_computation | async-start | bytes 1048576 | tf_op jit(solution)/shard_map/all_to_all | solution.py:1316
  170.2 168.2 %reduce-scatter.5.cloned.1.call-start = ((), (), s32[]{:S(2)}) async-start(), calls=%async_computation.7 | async-start | bytes 2621440 | tf_op jit(solution)/shard_map/reduce_scatter | solution.py:1350
  202.5 14.1 %collective-permute-start.13 = (bf16[256,1024]{1,0:T(8,128)(2,1)S(1)}, bf16[256,1024]{1,0:T(8,128)(2,1)S(1)}, u32[]{:S(2)}, u32[]{:S(2)}) collective-permute-start(bf16[256,1024]{1,0:T(8,128)(2,1)S(1)} %get-tuple-element.136), channel_id=1, source_target_pairs={{0,4},{4,0},{1,5},{5,1},{2,6},{6,2},{3,7},{7,3},{8,12},{12,8},{9,1... | collective-permute-start | bytes 1572872 | tf_op jit(solution)/shard_map/ppermute | solution.py:1072
  204.3 14.1 %collective-permute-start.14 = (bf16[256,1024]{1,0:T(8,128)(2,1)S(1)}, bf16[256,1024]{1,0:T(8,128)(2,1)S(1)}, u32[]{:S(2)}, u32[]{:S(2)}) collective-permute-start(bf16[256,1024]{1,0:T(8,128)(2,1)S(1)} %get-tuple-element.136), channel_id=1, source_target_pairs={{0,2},{2,0},{1,3},{3,1},{4,6},{6,4},{5,7},{7,5},{8,10},{10,8},{9,1... | collective-permute-start | bytes 1572872 | tf_op jit(solution)/shard_map/ppermute | solution.py:1072
  216.7 7.7 %collective-permute-start.15 = (bf16[128,1024]{1,0:T(8,128)(2,1)S(1)}, bf16[128,1024]{1,0:T(8,128)(2,1)S(1)}, u32[]{:S(2)}, u32[]{:S(2)}) collective-permute-start(bf16[128,1024]{1,0:T(8,128)(2,1)S(1)} %slice.452), channel_id=1, source_target_pairs={{0,2},{2,0},{1,3},{3,1},{4,6},{6,4},{5,7},{7,5},{8,10},{10,8},{9,1... | collective-permute-start | bytes 786440 | tf_op jit(solution)/shard_map/ppermute | solution.py:1072
  218.5 7.3 %collective-permute-start.16 = (bf16[128,1024]{1,0:T(8,128)(2,1)S(1)}, bf16[128,1024]{1,0:T(8,128)(2,1)S(1)}, u32[]{:S(2)}, u32[]{:S(2)}) collective-permute-start(bf16[128,1024]{1,0:T(8,128)(2,1)S(1)} %slice.453), channel_id=1, source_target_pairs={{0,4},{4,0},{1,5},{5,1},{2,6},{6,2},{3,7},{7,3},{8,12},{12,8},{9,1... | collective-permute-start | bytes 786440 | tf_op jit(solution)/shard_map/ppermute | solution.py:1072
  225.8 5.8 collective-permute-start.17
  247.1 25.3 %collective-permute-start.18 = (bf16[1024,1024]{1,0:T(8,128)(2,1)}, bf16[1024,1024]{1,0:T(8,128)(2,1)S(1)}, u32[]{:S(2)}, u32[]{:S(2)}) collective-permute-start(bf16[1024,1024]{1,0:T(8,128)(2,1)} %get-tuple-element.74), channel_id=1, source_target_pairs={{0,1},{1,0},{2,3},{3,2},{4,5},{5,4},{6,7},{7,6},{8,9},{9,8},{10,11... | collective-permute-start | bytes 6291464 | tf_op jit(solution)/shard_map/ppermute | solution.py:1072
  277.2 12.1 %collective-permute-start.19 = (bf16[128,1024]{1,0:T(8,128)(2,1)}, bf16[128,1024]{1,0:T(8,128)(2,1)}, u32[]{:S(2)}, u32[]{:S(2)}) collective-permute-start(bf16[128,1024]{1,0:T(8,128)(2,1)} %get-tuple-element.164), channel_id=1, source_target_pairs={{0,2},{2,0},{1,3},{3,1},{4,6},{6,4},{5,7},{7,5},{8,10},{10,8},{9,1... | collective-permute-start | bytes 786440 | tf_op jit(solution)/shard_map/ppermute | solution.py:1072
  278.3 11.1 %collective-permute-start.20 = (bf16[128,1024]{1,0:T(8,128)(2,1)}, bf16[128,1024]{1,0:T(8,128)(2,1)}, u32[]{:S(2)}, u32[]{:S(2)}) collective-permute-start(bf16[128,1024]{1,0:T(8,128)(2,1)} %get-tuple-element.163), channel_id=1, source_target_pairs={{0,4},{4,0},{1,5},{5,1},{2,6},{6,2},{3,7},{7,3},{8,12},{12,8},{9,1... | collective-permute-start | bytes 786440 | tf_op jit(solution)/shard_map/ppermute | solution.py:1072
  280.2 202.7 %reduce-scatter.11.cloned.1.call-start = ((), (), s32[]{:S(2)}) async-start(), calls=%async_computation.10 | async-start | bytes 2621440 | tf_op jit(solution)/shard_map/reduce_scatter | solution.py:1351
  291.9 13.4 %collective-permute-start.21 = (bf16[256,1024]{1,0:T(8,128)(2,1)S(1)}, bf16[256,1024]{1,0:T(8,128)(2,1)S(1)}, u32[]{:S(2)}, u32[]{:S(2)}) collective-permute-start(bf16[256,1024]{1,0:T(8,128)(2,1)S(1)} %pad_maximum_fusion.7), channel_id=1, source_target_pairs={{0,4},{4,0},{1,5},{5,1},{2,6},{6,2},{3,7},{7,3},{8,12},{12,8},{9,1... | collective-permute-start | bytes 1572872 | tf_op jit(solution)/shard_map/ppermute | solution.py:1072
  293.1 13.2 %collective-permute-start.22 = (bf16[256,1024]{1,0:T(8,128)(2,1)S(1)}, bf16[256,1024]{1,0:T(8,128)(2,1)S(1)}, u32[]{:S(2)}, u32[]{:S(2)}) collective-permute-start(bf16[256,1024]{1,0:T(8,128)(2,1)S(1)} %pad_maximum_fusion.8), channel_id=1, source_target_pairs={{0,2},{2,0},{1,3},{3,1},{4,6},{6,4},{5,7},{7,5},{8,10},{10,8},{9,1... | collective-permute-start | bytes 1572872 | tf_op jit(solution)/shard_map/ppermute | solution.py:1072
  327.5 10.9 %collective-permute-start.23 = (bf16[2,2,2,512,128]{4,3,2,1,0:T(8,128)(2,1)S(1)}, bf16[2,2,2,512,128]{4,3,2,1,0:T(8,128)(2,1)}, u32[]{:S(2)}, u32[]{:S(2)}) collective-permute-start(bf16[2,2,2,512,128]{4,3,2,1,0:T(8,128)(2,1)S(1)} %dynamic-slice_bitcast_fusion), channel_id=1, source_target_pairs={{0,1},{1,0},{2,3},{3,2},{4,5},{5,4},{6,7},{7,6},{8,9},{9,8},{10,11... | collective-permute-start | bytes 3145736 | tf_op jit(solution)/shard_map/ppermute | solution.py:1072
  343.3 16.7 %collective-permute-start.25 = (bf16[2,2,4,3,256,128]{5,4,3,2,1,0:T(8,128)(2,1)}, bf16[2,2,4,3,256,128]{5,4,3,2,1,0:T(8,128)(2,1)}, u32[]{:S(2)}, u32[]{:S(2)}) collective-permute-start(bf16[2,2,4,3,256,128]{5,4,3,2,1,0:T(8,128)(2,1)} %get-tuple-element.95), channel_id=1, source_target_pairs={{0,1},{1,0},{2,3},{3,2},{4,5},{5,4},{6,7},{7,6},{8,9},{9,8},{10,11... | collective-permute-start | bytes 9437192 | tf_op jit(solution)/shard_map/ppermute | solution.py:1072
  343.3 11.2 %collective-permute-start.26 = (bf16[1024,1024]{1,0:T(8,128)(2,1)}, bf16[1024,1024]{1,0:T(8,128)(2,1)}, u32[]{:S(2)}, u32[]{:S(2)}) collective-permute-start(bf16[1024,1024]{1,0:T(8,128)(2,1)} %convolution_convert_fusion.1), channel_id=1, source_target_pairs={{0,1},{1,0},{2,3},{3,2},{4,5},{5,4},{6,7},{7,6},{8,9},{9,8},{10,11... | collective-permute-start | bytes 6291464 | tf_op jit(solution)/shard_map/ppermute | solution.py:1072
  346.1 18.7 %all-to-all-start.1 = ((bf16[256,8,128]{2,0,1:T(8,128)(2,1)}), bf16[256,8,128]{2,0,1:T(8,128)(2,1)S(1)}, u32[]{:S(2)}, u32[]{:S(2)}) async-start(bf16[256,8,128]{2,0,1:T(8,128)(2,1)} %copy_bitcast_fusion.1), calls=%async_computation.2 | async-start | bytes 1048576 | tf_op jit(solution)/shard_map/all_to_all | solution.py:1382
  350.5 181.9 %reduce-scatter.7.cloned.1.call-start = ((), (), s32[]{:S(2)}) async-start(), calls=%async_computation.8 | async-start | bytes 1638400 | tf_op jit(solution)/shard_map/reduce_scatter | solution.py:1457
  354.3 14.6 %collective-permute-start.24 = (bf16[2,2,512,128]{3,2,1,0:T(8,128)(2,1)}, bf16[2,2,512,128]{3,2,1,0:T(8,128)(2,1)S(1)}, u32[]{:S(2)}, u32[]{:S(2)}) collective-permute-start(bf16[2,2,512,128]{3,2,1,0:T(8,128)(2,1)} %dynamic-slice_bitcast_fusion.4), channel_id=1, source_target_pairs={{0,2},{2,0},{1,3},{3,1},{4,6},{6,4},{5,7},{7,5},{8,10},{10,8},{9,1... | collective-permute-start | bytes 1572872 | tf_op jit(solution)/shard_map/ppermute | solution.py:1072
  396.6 21.5 %collective-permute-start.27 = (bf16[128,1024]{1,0:T(8,128)(2,1)}, bf16[128,1024]{1,0:T(8,128)(2,1)}, u32[]{:S(2)}, u32[]{:S(2)}) collective-permute-start(bf16[128,1024]{1,0:T(8,128)(2,1)} %get-tuple-element.151), channel_id=1, source_target_pairs={{0,2},{2,0},{1,3},{3,1},{4,6},{6,4},{5,7},{7,5},{8,10},{10,8},{9,1... | collective-permute-start | bytes 786440 | tf_op jit(solution)/shard_map/ppermute | solution.py:1072
  398.2 24.6 %collective-permute-start.34 = (bf16[128,1024]{1,0:T(8,128)(2,1)}, bf16[128,1024]{1,0:T(8,128)(2,1)}, u32[]{:S(2)}, u32[]{:S(2)}) collective-permute-start(bf16[128,1024]{1,0:T(8,128)(2,1)} %get-tuple-element.152), channel_id=1, source_target_pairs={{0,4},{4,0},{1,5},{5,1},{2,6},{6,2},{3,7},{7,3},{8,12},{12,8},{9,1... | collective-permute-start | bytes 786440 | tf_op jit(solution)/shard_map/ppermute | solution.py:1072
  399.7 27.1 %collective-permute-start.28 = (bf16[1024,1024]{1,0:T(8,128)(2,1)}, bf16[1024,1024]{1,0:T(8,128)(2,1)S(1)}, u32[]{:S(2)}, u32[]{:S(2)}) collective-permute-start(bf16[1024,1024]{1,0:T(8,128)(2,1)} %convolution_convert_fusion), channel_id=1, source_target_pairs={{0,1},{1,0},{2,3},{3,2},{4,5},{5,4},{6,7},{7,6},{8,9},{9,8},{10,11... | collective-permute-start | bytes 6291464 | tf_op jit(solution)/shard_map/ppermute | solution.py:1072
  403.6 11.5 %collective-permute-start.38 = (bf16[2,512,128]{2,1,0:T(8,128)(2,1)}, bf16[2,512,128]{2,1,0:T(8,128)(2,1)}, u32[]{:S(2)}, u32[]{:S(2)}) collective-permute-start(bf16[2,512,128]{2,1,0:T(8,128)(2,1)} %dynamic-slice_bitcast_fusion.17), channel_id=1, source_target_pairs={{0,4},{4,0},{1,5},{5,1},{2,6},{6,2},{3,7},{7,3},{8,12},{12,8},{9,1... | collective-permute-start | bytes 786440 | tf_op jit(solution)/shard_map/ppermute | solution.py:1072
  405.6 80.5 %collective-permute-start.53 = (bf16[2,2,3,256,128]{4,3,2,1,0:T(8,128)(2,1)}, bf16[2,2,3,256,128]{4,3,2,1,0:T(8,128)(2,1)}, u32[]{:S(2)}, u32[]{:S(2)}) collective-permute-start(bf16[2,2,3,256,128]{4,3,2,1,0:T(8,128)(2,1)} %dynamic-slice_bitcast_fusion.1), channel_id=1, source_target_pairs={{0,4},{4,0},{1,5},{5,1},{2,6},{6,2},{3,7},{7,3},{8,12},{12,8},{9,1... | collective-permute-start | bytes 2359304 | tf_op jit(solution)/shard_map/ppermute | solution.py:1072
  415.1 72.5 %collective-permute-start.51 = (bf16[2,2,3,256,128]{4,3,2,1,0:T(8,128)(2,1)}, bf16[2,2,3,256,128]{4,3,2,1,0:T(8,128)(2,1)}, u32[]{:S(2)}, u32[]{:S(2)}) collective-permute-start(bf16[2,2,3,256,128]{4,3,2,1,0:T(8,128)(2,1)} %dynamic-slice_bitcast_fusion.2), channel_id=1, source_target_pairs={{0,2},{2,0},{1,3},{3,1},{4,6},{6,4},{5,7},{7,5},{8,10},{10,8},{9,1... | collective-permute-start | bytes 2359304 | tf_op jit(solution)/shard_map/ppermute | solution.py:1072
  418.1 28.7 %collective-permute-start.56 = (bf16[256,1024]{1,0:T(8,128)(2,1)S(1)}, bf16[256,1024]{1,0:T(8,128)(2,1)S(1)}, u32[]{:S(2)}, u32[]{:S(2)}) collective-permute-start(bf16[256,1024]{1,0:T(8,128)(2,1)S(1)} %broadcast_add_fusion), channel_id=1, source_target_pairs={{0,0},{1,8},{2,16},{3,24},{4,4},{5,12},{6,20},{7,28},{8,1},{9,9},{... | collective-permute-start | bytes 1572872 | tf_op jit(solution)/shard_map/ppermute | solution.py:1095
  430.7 20.9 %collective-permute-start.29 = (bf16[128,1024]{1,0:T(8,128)(2,1)S(1)}, bf16[128,1024]{1,0:T(8,128)(2,1)S(1)}, u32[]{:S(2)}, u32[]{:S(2)}) collective-permute-start(bf16[128,1024]{1,0:T(8,128)(2,1)S(1)} %get-tuple-element.157), channel_id=1, source_target_pairs={{0,2},{2,0},{1,3},{3,1},{4,6},{6,4},{5,7},{7,5},{8,10},{10,8},{9,1... | collective-permute-start | bytes 786440 | tf_op jit(solution)/shard_map/ppermute | solution.py:1072
  430.8 20.9 %collective-permute-start.31 = (bf16[128,1024]{1,0:T(8,128)(2,1)S(1)}, bf16[128,1024]{1,0:T(8,128)(2,1)S(1)}, u32[]{:S(2)}, u32[]{:S(2)}) collective-permute-start(bf16[128,1024]{1,0:T(8,128)(2,1)S(1)} %get-tuple-element.158), channel_id=1, source_target_pairs={{0,4},{4,0},{1,5},{5,1},{2,6},{6,2},{3,7},{7,3},{8,12},{12,8},{9,1... | collective-permute-start | bytes 786440 | tf_op jit(solution)/shard_map/ppermute | solution.py:1072
  452.7 13.2 %collective-permute-start.32 = (bf16[256,1024]{1,0:T(8,128)(2,1)}, bf16[256,1024]{1,0:T(8,128)(2,1)}, u32[]{:S(2)}, u32[]{:S(2)}) collective-permute-start(bf16[256,1024]{1,0:T(8,128)(2,1)} %pad_maximum_fusion.10), channel_id=1, source_target_pairs={{0,2},{2,0},{1,3},{3,1},{4,6},{6,4},{5,7},{7,5},{8,10},{10,8},{9,1... | collective-permute-start | bytes 1572872 | tf_op jit(solution)/shard_map/ppermute | solution.py:1072
  453.5 13.2 %collective-permute-start.30 = (bf16[256,1024]{1,0:T(8,128)(2,1)}, bf16[256,1024]{1,0:T(8,128)(2,1)}, u32[]{:S(2)}, u32[]{:S(2)}) collective-permute-start(bf16[256,1024]{1,0:T(8,128)(2,1)} %pad_maximum_fusion.9), channel_id=1, source_target_pairs={{0,4},{4,0},{1,5},{5,1},{2,6},{6,2},{3,7},{7,3},{8,12},{12,8},{9,1... | collective-permute-start | bytes 1572872 | tf_op jit(solution)/shard_map/ppermute | solution.py:1072
  456.5 127.9 %reduce-scatter.9.cloned.1.call-start = ((), (), s32[]{:S(2)}) async-start(), calls=%async_computation.9 | async-start | bytes 983040 | tf_op jit(solution)/shard_map/reduce_scatter | solution.py:1465
  473.9 48.6 %collective-permute-start.35 = (bf16[256,1024]{1,0:T(8,128)(2,1)}, bf16[256,1024]{1,0:T(8,128)(2,1)}, u32[]{:S(2)}, u32[]{:S(2)}) collective-permute-start(bf16[256,1024]{1,0:T(8,128)(2,1)} %maximum_add_fusion.1), channel_id=1, source_target_pairs={{0,2},{2,0},{1,3},{3,1},{4,6},{6,4},{5,7},{7,5},{8,10},{10,8},{9,1... | collective-permute-start | bytes 1572872 | tf_op jit(solution)/shard_map/ppermute | solution.py:1072
  476.5 47.0 %collective-permute-start.33 = (bf16[256,1024]{1,0:T(8,128)(2,1)}, bf16[256,1024]{1,0:T(8,128)(2,1)}, u32[]{:S(2)}, u32[]{:S(2)}) collective-permute-start(bf16[256,1024]{1,0:T(8,128)(2,1)} %maximum_add_fusion), channel_id=1, source_target_pairs={{0,4},{4,0},{1,5},{5,1},{2,6},{6,2},{3,7},{7,3},{8,12},{12,8},{9,1... | collective-permute-start | bytes 1572872 | tf_op jit(solution)/shard_map/ppermute | solution.py:1072
  478.6 60.8 %collective-permute-start.37 = (bf16[256,1024]{1,0:T(8,128)(2,1)}, bf16[256,1024]{1,0:T(8,128)(2,1)}, u32[]{:S(2)}, u32[]{:S(2)}) collective-permute-start(bf16[256,1024]{1,0:T(8,128)(2,1)} %fusion.55), channel_id=1, source_target_pairs={{0,0},{1,8},{2,16},{3,24},{4,4},{5,12},{6,20},{7,28},{8,1},{9,9},{... | collective-permute-start | bytes 1572872 | tf_op jit(solution)/shard_map/ppermute | solution.py:1095
  487.6 14.4 %collective-permute-start.57 = (bf16[128,1024]{1,0:T(8,128)(2,1)S(1)}, bf16[128,1024]{1,0:T(8,128)(2,1)S(1)}, u32[]{:S(2)}, u32[]{:S(2)}) collective-permute-start(bf16[128,1024]{1,0:T(8,128)(2,1)S(1)} %dynamic-slice_bitcast_fusion.15), channel_id=1, source_target_pairs={{0,4},{4,0},{1,5},{5,1},{2,6},{6,2},{3,7},{7,3},{8,12},{12,8},{9,1... | collective-permute-start | bytes 786440 | tf_op jit(solution)/shard_map/ppermute | solution.py:1072
  490.1 7.2 %collective-permute-start.44 = (f32[21,1024]{1,0:T(8,128)S(1)}, f32[21,1024]{1,0:T(8,128)S(1)}, u32[]{:S(2)}, u32[]{:S(2)}) collective-permute-start(f32[21,1024]{1,0:T(8,128)S(1)} %fusion.116), channel_id=1, source_target_pairs={{0,2},{2,0},{1,3},{3,1},{4,6},{6,4},{5,7},{7,5},{8,10},{10,8},{9,1... | collective-permute-start | bytes 258056 | tf_op jit(solution)/shard_map/ppermute | solution.py:1072
  502.0 18.0 %collective-permute-start.39 = (bf16[2,2,64,1024]{3,2,1,0:T(8,128)(2,1)}, bf16[2,2,64,1024]{3,2,1,0:T(8,128)(2,1)}, u32[]{:S(2)}, u32[]{:S(2)}) collective-permute-start(bf16[2,2,64,1024]{3,2,1,0:T(8,128)(2,1)} %dynamic-slice_bitcast_fusion.3), channel_id=1, source_target_pairs={{0,1},{1,0},{2,3},{3,2},{4,5},{5,4},{6,7},{7,6},{8,9},{9,8},{10,11... | collective-permute-start | bytes 1572872 | tf_op jit(solution)/shard_map/ppermute | solution.py:1072
  502.0 5.3 collective-permute-start.46
  508.0 7.9 %collective-permute-start.47 = (f32[21,1024]{1,0:T(8,128)}, f32[21,1024]{1,0:T(8,128)}, u32[]{:S(2)}, u32[]{:S(2)}) collective-permute-start(f32[21,1024]{1,0:T(8,128)} %add.607), channel_id=1, source_target_pairs={{0,16},{8,24},{16,0},{24,8},{1,17},{9,25},{17,1},{25,9},{2,18},{10... | collective-permute-start | bytes 258056 | tf_op jit(solution)/shard_map/ppermute | solution.py:1072
  515.8 19.8 %collective-permute-start.54 = (bf16[2,3,256,128]{3,2,1,0:T(8,128)(2,1)S(1)}, bf16[2,3,256,128]{3,2,1,0:T(8,128)(2,1)}, u32[]{:S(2)}, u32[]{:S(2)}) collective-permute-start(bf16[2,3,256,128]{3,2,1,0:T(8,128)(2,1)S(1)} %dynamic-slice_bitcast_fusion.13), channel_id=1, source_target_pairs={{0,2},{2,0},{1,3},{3,1},{4,6},{6,4},{5,7},{7,5},{8,10},{10,8},{9,1... | collective-permute-start | bytes 1179656 | tf_op jit(solution)/shard_map/ppermute | solution.py:1072
  520.0 16.7 %collective-permute-start.52 = (bf16[2,3,256,128]{3,2,1,0:T(8,128)(2,1)}, bf16[2,3,256,128]{3,2,1,0:T(8,128)(2,1)}, u32[]{:S(2)}, u32[]{:S(2)}) collective-permute-start(bf16[2,3,256,128]{3,2,1,0:T(8,128)(2,1)} %dynamic-slice_bitcast_fusion.14), channel_id=1, source_target_pairs={{0,4},{4,0},{1,5},{5,1},{2,6},{6,2},{3,7},{7,3},{8,12},{12,8},{9,1... | collective-permute-start | bytes 1179656 | tf_op jit(solution)/shard_map/ppermute | solution.py:1072
  522.5 9.8 %collective-permute-start.40 = (bf16[2,64,1024]{2,1,0:T(8,128)(2,1)S(1)}, bf16[2,64,1024]{2,1,0:T(8,128)(2,1)S(1)}, u32[]{:S(2)}, u32[]{:S(2)}) collective-permute-start(bf16[2,64,1024]{2,1,0:T(8,128)(2,1)S(1)} %dynamic-slice_bitcast_fusion.16), channel_id=1, source_target_pairs={{0,2},{2,0},{1,3},{3,1},{4,6},{6,4},{5,7},{7,5},{8,10},{10,8},{9,1... | collective-permute-start | bytes 786440 | tf_op jit(solution)/shard_map/ppermute | solution.py:1072
  525.2 51.5 %collective-permute-start.36 = (bf16[256,1024]{1,0:T(8,128)(2,1)S(1)}, bf16[256,1024]{1,0:T(8,128)(2,1)S(1)}, u32[]{:S(2)}, u32[]{:S(2)}) collective-permute-start(bf16[256,1024]{1,0:T(8,128)(2,1)S(1)} %add_convert_fusion.4), channel_id=1, source_target_pairs={{0,0},{1,8},{2,16},{3,24},{4,4},{5,12},{6,20},{7,28},{8,1},{9,9},{... | collective-permute-start | bytes 1572872 | tf_op jit(solution)/shard_map/ppermute | solution.py:1095
  544.0 30.1 %collective-permute-start.42 = (bf16[64,1024]{1,0:T(8,128)(2,1)S(1)}, bf16[64,1024]{1,0:T(8,128)(2,1)S(1)}, u32[]{:S(2)}, u32[]{:S(2)}) collective-permute-start(bf16[64,1024]{1,0:T(8,128)(2,1)S(1)} %fusion.73), channel_id=1, source_target_pairs={{0,0},{1,8},{2,16},{3,24},{4,4},{5,12},{6,20},{7,28},{8,1},{9,9},{... | collective-permute-start | bytes 393224 | tf_op jit(solution)/shard_map/ppermute | solution.py:1095
  550.1 26.6 %collective-permute-start.50 = (bf16[256,128]{1,0:T(8,128)(2,1)S(1)}, bf16[256,128]{1,0:T(8,128)(2,1)S(1)}, u32[]{:S(2)}, u32[]{:S(2)}) collective-permute-start(bf16[256,128]{1,0:T(8,128)(2,1)S(1)} %get-tuple-element.184), channel_id=1, source_target_pairs={{1,0},{9,1},{17,2},{25,3},{6,4},{14,5},{22,6},{30,7},{0,8},{8,9},{... | collective-permute-start | bytes 196616 | tf_op jit(solution)/shard_map/ppermute | solution.py:1489
  552.0 24.7 %collective-permute-start.49 = (bf16[256,128]{1,0:T(8,128)(2,1)S(1)}, bf16[256,128]{1,0:T(8,128)(2,1)S(1)}, u32[]{:S(2)}, u32[]{:S(2)}) collective-permute-start(bf16[256,128]{1,0:T(8,128)(2,1)S(1)} %get-tuple-element.185), channel_id=1, source_target_pairs={{4,0},{12,1},{20,2},{28,3},{2,4},{10,5},{18,6},{26,7},{7,8},{15,9}... | collective-permute-start | bytes 196616 | tf_op jit(solution)/shard_map/ppermute | solution.py:1489
  553.5 23.7 %collective-permute-start.48 = (bf16[256,128]{1,0:T(8,128)(2,1)S(1)}, bf16[256,128]{1,0:T(8,128)(2,1)S(1)}, u32[]{:S(2)}, u32[]{:S(2)}) collective-permute-start(bf16[256,128]{1,0:T(8,128)(2,1)S(1)} %get-tuple-element.183), channel_id=1, source_target_pairs={{0,0},{8,1},{16,2},{24,3},{5,4},{13,5},{21,6},{29,7},{3,8},{11,9},... | collective-permute-start | bytes 196616 | tf_op jit(solution)/shard_map/ppermute | solution.py:1489
  574.1 9.6 %collective-permute-start.55 = (bf16[2,256,128]{2,1,0:T(8,128)(2,1)S(1)}, bf16[2,256,128]{2,1,0:T(8,128)(2,1)S(1)}, u32[]{:S(2)}, u32[]{:S(2)}) collective-permute-start(bf16[2,256,128]{2,1,0:T(8,128)(2,1)S(1)} %slice_bitcast_fusion.1), channel_id=1, source_target_pairs={{0,0},{1,8},{2,16},{3,24},{4,4},{5,12},{6,20},{7,28},{8,1},{9,9},{... | collective-permute-start | bytes 393224 | tf_op jit(solution)/shard_map/ppermute | solution.py:1095
  (73 other events, 582.2 us)
Sparse Core Ops, SparseCore 0:
  64.9 26.0 all-gather.5
  92.9 45.4 all-gather.7
  148.7 36.8 all-gather.9
  280.3 44.0 reduce-scatter.4
  344.7 43.5 reduce-scatter.10
  456.6 33.2 reduce-scatter.6
  539.0 33.2 reduce-scatter.8
